TPU v7x, 32 devices: a whole 2x2x4 slice. The times are simulated.
32 devices in a mesh: rep: 8 (over y, x, core), shard: 4 (over z).
Axes of the slice: x: 2, y: 2, z: 4, core: 2. Of those that a mesh axis runs over, the one named last changes fastest.
Arguments:
- tokens: bfloat16 [16384, 1024], P(('rep', 'shard')), may hold values from -6 to 6
- doc_ids: int32 [16384], P(('rep', 'shard')), may hold values from 0 to 511, as said below
- routes: int32 [16384, 8], P(('rep', 'shard')), may hold values from 0 to 15, all different within a row; in each aligned block of 512 rows (0 to 511, 512 to 1023, ...) at most 288 rows name the same one
- norm_in_gain: bfloat16 [1024], P('shard'), may hold values from 0.5 to 1.5
- w_query: bfloat16 [1024, 1024], P('shard'), may hold values from -0.1875 to 0.1875
- w_key: bfloat16 [1024, 512], P('shard'), may hold values from -0.1875 to 0.1875
- w_value: bfloat16 [1024, 512], P('shard'), may hold values from -0.1875 to 0.1875
- w_out: bfloat16 [1024, 1024], P('shard'), may hold values from -0.75 to 0.75
- norm_mid_gain: bfloat16 [1024], P('shard'), may hold values from 0.5 to 1.5
- w_router: bfloat16 [1024, 16], P('shard'), may hold values from -0.09375 to 0.09375
- w_expert_in: bfloat16 [16, 1024, 1024], P('shard'), may hold values from -0.1875 to 0.1875
- w_expert_down: bfloat16 [16, 512, 1024], P('shard'), may hold values from -0.75 to 0.75
- cotangent: bfloat16 [16384, 1024], P(('rep', 'shard')), may hold values from -6 to 6
Outputs:
- mixed: bfloat16 [16384, 1024], P(('rep', 'shard'))
- grad_tokens: float32 [16384, 1024], P(('rep', 'shard'))
- grad_norm_in_gain: float32 [1024], P('shard')
- grad_w_query: float32 [1024, 1024], P('shard')
- grad_w_key: float32 [1024, 512], P('shard')
- grad_w_value: float32 [1024, 512], P('shard')
- grad_w_out: float32 [1024, 1024], P('shard')
- grad_norm_mid_gain: float32 [1024], P('shard')
- grad_w_router: float32 [1024, 16], P('shard')
- grad_w_expert_in: float32 [16, 1024, 1024], P('shard')
- grad_w_expert_down: float32 [16, 512, 1024], P('shard')
Inputs may be any that keep to these rules, and one draw needn't show every extreme that they name: `doc_ids`: in every aligned block of 512 tokens the numbers start at 0 and rise by 0 or 1 from token to token. Among the 512 tokens of one device, no expert is named by more than 288 routes.
All inputs are finite; a program needn't handle non-finite values.
Results may differ from a plain program's by a relative error of at most 0.019.
Values may be sent and summed in bfloat16 or wider, within the bound.
A program may use at most 320 MiB of HBM per device.

v0:
```python
import jax
import jax.numpy as jnp
from jax import lax
from jax.experimental import pallas as pl
from jax.experimental.pallas import tpu as pltpu
from jax.sharding import PartitionSpec as P

HEADS = 16
KV_HEADS = 8
HEAD_DIM = 64
EXPERTS = 16
PAD = 128
VMEM_BYTES = 54 * 2**20


epsilon = 1e-06
rope_base = 10000.0
masked_score = -1e30


def positions(doc_rows):
    row_count = doc_rows.shape[0]
    places = jnp.arange(row_count, dtype=jnp.int32)
    opening = jnp.concatenate([jnp.ones((1,), dtype=jnp.bool_), doc_rows[1:] != doc_rows[:-1]])
    begins = lax.cummax(jnp.where(opening, places, 0), axis=0)
    return places - begins


def rotary_tables(places, head_width):
    half_width = head_width // 2
    frequencies = jnp.power(
        rope_base, -2.0 * jnp.arange(half_width, dtype=jnp.float32) / head_width
    )
    angles = places.astype(jnp.float32)[:, None] * frequencies[None, :]
    return (jnp.cos(angles)[:, None, :], jnp.sin(angles)[:, None, :])


def rotate(values, cosine, sine_table):
    half_width = values.shape[-1] // 2
    former, latter = (values[..., :half_width], values[..., half_width:])
    return jnp.concatenate(
        [former * cosine - latter * sine_table, latter * cosine + former * sine_table], axis=-1
    )


def unrotate(values, cosine, sine_table):
    half_width = values.shape[-1] // 2
    former, latter = (values[..., :half_width], values[..., half_width:])
    return jnp.concatenate(
        [former * cosine + latter * sine_table, latter * cosine - former * sine_table], axis=-1
    )


def normalize(values):
    row_scale = lax.rsqrt(jnp.mean(values * values, axis=-1, keepdims=True) + epsilon)
    return (values * row_scale, row_scale)


def norm_back(grad_scaled, normed, row_scale, gain_full):
    grad_normed = grad_scaled * gain_full
    inner = jnp.mean(grad_normed * normed, axis=-1, keepdims=True)
    return (row_scale * (grad_normed - normed * inner), jnp.sum(grad_scaled * normed, axis=0))


def score_block(query_blk, key_part, doc_query, doc_key):
    scores = jnp.einsum(
        "qgrd,kgd->grqk", query_blk, key_part, preferred_element_type=jnp.float32
    ) * query_blk.shape[-1] ** (-0.5)
    query_place = jnp.arange(query_blk.shape[0], dtype=jnp.int32)
    key_place = jnp.arange(key_part.shape[0], dtype=jnp.int32)
    allowed = (doc_query[:, None] == doc_key[None, :]) & (
        query_place[:, None] >= key_place[None, :]
    )
    return jnp.where(allowed, scores, masked_score)


def attend(query_rows, key_rows, value_rows, doc_rows):
    scores = score_block(query_rows, key_rows, doc_rows, doc_rows)
    row_max = jnp.max(scores, axis=-1, keepdims=True)
    exponent = jnp.exp(scores - row_max)
    row_total = jnp.sum(exponent, axis=-1, keepdims=True)
    probs_low = (exponent / row_total).astype(jnp.bfloat16)
    outputs = jnp.einsum(
        "grqk,kgd->qgrd", probs_low, value_rows, preferred_element_type=jnp.float32
    ).astype(jnp.bfloat16)
    lse_parts = row_max + jnp.log(row_total)
    return (outputs, lse_parts)


def attend_back(query_rows, key_rows, value_rows, doc_rows, log_sums, grad_att):
    row_count = query_rows.shape[0]
    block_rows = min(512, row_count)
    scale_factor = query_rows.shape[-1] ** (-0.5)
    grad_key = jnp.zeros(key_rows.shape, jnp.float32)
    grad_value = jnp.zeros(value_rows.shape, jnp.float32)
    scores = score_block(query_rows, key_rows, doc_rows, doc_rows)
    probs = jnp.exp(scores - log_sums)
    grad_probs = jnp.einsum(
        "qgrd,kgd->grqk", grad_att, value_rows, preferred_element_type=jnp.float32
    )
    inner = jnp.sum(probs * grad_probs, axis=-1, keepdims=True)
    grad_scores = (probs * (grad_probs - inner)).astype(jnp.bfloat16)
    query_parts = (
        jnp.einsum("grqk,kgd->qgrd", grad_scores, key_rows, preferred_element_type=jnp.float32)
        * scale_factor
    )
    grad_key = grad_key.at[:block_rows].add(
        jnp.einsum("grqk,qgrd->kgd", grad_scores, query_rows, preferred_element_type=jnp.float32)
        * scale_factor
    )
    grad_value = grad_value.at[:block_rows].add(
        jnp.einsum(
            "grqk,qgrd->kgd",
            probs.astype(jnp.bfloat16),
            grad_att,
            preferred_element_type=jnp.float32,
        )
    )
    return (query_parts, grad_key, grad_value)


MESH = pl.DeviceIdType.MESH
HALVES = 2


def bit_orders(reps):
    bits = reps.bit_length() - 1
    first = list(range(bits))
    return (first, first[:1] + first[1:][::-1])


def rep_place(rep_at, order):
    place = 0
    for bit in order:
        place = place * 2 + rep_at // 2**bit % 2
    return place


def partner(rep_at, bit):
    return rep_at + 2**bit * (1 - 2 * (rep_at // 2**bit % 2))


def halves_of(columns):
    tiles = columns // 128
    left = (tiles + 1) // 2 * 128
    return (pl.ds(0, left), pl.ds(left, columns - left))


def meet(rep_at, shard_at, reps, shard_count):
    barrier = pltpu.get_barrier_semaphore()
    bits = reps.bit_length() - 1
    for bit in range(bits):
        pl.semaphore_signal(
            barrier, inc=1, device_id=(partner(rep_at, bit), shard_at), device_id_type=MESH
        )
    for step in range(1, shard_count):
        pl.semaphore_signal(
            barrier,
            inc=1,
            device_id=(rep_at, (shard_at + step) % shard_count),
            device_id_type=MESH,
        )
    pl.semaphore_wait(barrier, bits + shard_count - 1)


def spread(out, orders, columns, rep_at, shard_at, sends, recvs):
    bits = len(orders[0])
    flying = [None] * HALVES
    for at in reversed(range(bits)):
        window = 2 ** (bits - 1 - at)
        for half in range(HALVES):
            order = orders[half]
            place = rep_place(rep_at, order)
            begin = place // window * window
            if flying[half] is not None:
                flying[half].wait()
            block = out.at[:, pl.ds(begin, window), :, columns[half]]
            flying[half] = pltpu.make_async_remote_copy(
                src_ref=block,
                dst_ref=block,
                send_sem=sends.at[half, at],
                recv_sem=recvs.at[half, at],
                device_id=(partner(rep_at, order[at]), shard_at),
                device_id_type=MESH,
            )
            flying[half].start()
    for half in range(HALVES):
        flying[half].wait()


def gather_kernel(reps, shard_count, piece, out, z_send, z_recv, sends, recvs):
    rep_at, shard_at = (lax.axis_index("rep"), lax.axis_index("shard"))
    orders = bit_orders(reps)
    columns = halves_of(piece.shape[-1])
    meet(rep_at, shard_at, reps, shard_count)
    flying = []
    for half in range(HALVES):
        place = rep_place(rep_at, orders[half])
        for step in range(1, shard_count):
            copy = pltpu.make_async_remote_copy(
                src_ref=piece.at[place, :, columns[half]],
                dst_ref=out.at[shard_at, place, :, columns[half]],
                send_sem=z_send.at[half, step - 1],
                recv_sem=z_recv.at[half, step - 1],
                device_id=(rep_at, (shard_at + step) % shard_count),
                device_id_type=MESH,
            )
            copy.start()
            flying.append(copy)
        out[shard_at, place, :, columns[half]] = piece[place, :, columns[half]]
    for copy in flying:
        copy.wait()
    spread(out, orders, columns, rep_at, shard_at, sends, recvs)


def gather_all(piece, reps, shard_count, number):
    own, width = piece.shape
    rows = own // reps
    bits = reps.bit_length() - 1
    out = pl.pallas_call(
        lambda *refs: gather_kernel(reps, shard_count, *refs),
        out_shape=jax.ShapeDtypeStruct((shard_count, reps, rows, width), piece.dtype),
        in_specs=[pl.BlockSpec(memory_space=pltpu.VMEM)],
        out_specs=pl.BlockSpec(memory_space=pltpu.VMEM),
        scratch_shapes=[
            pltpu.SemaphoreType.DMA((HALVES, shard_count)),
            pltpu.SemaphoreType.DMA((HALVES, shard_count)),
            pltpu.SemaphoreType.DMA((HALVES, bits)),
            pltpu.SemaphoreType.DMA((HALVES, bits)),
        ],
        compiler_params=pltpu.CompilerParams(
            collective_id=number, has_side_effects=True, vmem_limit_bytes=VMEM_BYTES
        ),
        cost_estimate=pl.CostEstimate(
            flops=0, bytes_accessed=16 * shard_count * own * width, transcendentals=0
        ),
    )(piece.reshape(reps, rows, width))
    return out.reshape(shard_count * own, width)


def reduce_kernel(reps, shard_count, parts, out, *scratch):
    bits = reps.bit_length() - 1
    f32 = jnp.float32
    landed = [scratch[half * bits : (half + 1) * bits] for half in range(HALVES)]
    rest = scratch[HALVES * bits :]
    if shard_count > 1:
        z_land, (z_send, z_recv) = (rest[:HALVES], rest[HALVES : HALVES + 2])
        rest = rest[HALVES + 2 :]
    r_send, r_recv, sends, recvs = rest
    rep_at, shard_at = (lax.axis_index("rep"), lax.axis_index("shard"))
    orders = bit_orders(reps)
    columns = halves_of(parts.shape[-1])
    meet(rep_at, shard_at, reps, shard_count)
    flying = [None] * HALVES

    def source(half, at):
        return parts.at[:, :, :, columns[half]] if at == 0 else landed[half][at - 1]

    def begin(half, at):
        bit = orders[half][at]
        many = reps // 2 ** (at + 1)
        away = (1 - rep_at // 2**bit % 2) * many
        flying[half] = pltpu.make_async_remote_copy(
            src_ref=source(half, at).at[:, pl.ds(away, many)],
            dst_ref=landed[half][at],
            send_sem=r_send.at[half, at],
            recv_sem=r_recv.at[half, at],
            device_id=(partner(rep_at, bit), shard_at),
            device_id_type=MESH,
        )
        flying[half].start()

    for half in range(HALVES):
        begin(half, 0)
    for at in range(bits):
        many = reps // 2 ** (at + 1)
        for half in range(HALVES):
            flying[half].wait()
            keep = rep_at // 2 ** orders[half][at] % 2 * many
            mine, came = (source(half, at), landed[half][at])

            @pl.loop(0, parts.shape[0] * many)
            def _(index):
                outer, inner = (index // many, index % many)
                came[outer, inner] = (
                    came[outer, inner].astype(f32) + mine[outer, keep + inner].astype(f32)
                ).astype(came.dtype)

            if at + 1 < bits:
                begin(half, at + 1)
    copies = []
    if shard_count > 1:
        for half in range(HALVES):
            for step in range(1, shard_count):
                to = (shard_at + step) % shard_count
                copy = pltpu.make_async_remote_copy(
                    src_ref=landed[half][-1].at[to, 0],
                    dst_ref=z_land[half].at[step - 1],
                    send_sem=z_send.at[half, step - 1],
                    recv_sem=z_recv.at[half, step - 1],
                    device_id=(rep_at, to),
                    device_id_type=MESH,
                )
                copy.start()
                copies.append(copy)
    for copy in copies:
        copy.wait()
    for half in range(HALVES):
        place = rep_place(rep_at, orders[half])
        if shard_count > 1:
            total = landed[half][-1][shard_at, 0].astype(f32)
            for step in range(1, shard_count):
                total = total + z_land[half][step - 1].astype(f32)
            out[0, place, :, columns[half]] = total.astype(out.dtype)
        else:
            out[0, place, :, columns[half]] = landed[half][-1][0, 0]
    spread(out, orders, columns, rep_at, shard_at, sends, recvs)


def reduce_all(parts, reps, shard_count, number):
    total, width = parts.shape
    rows = total // (reps * shard_count)
    bits = reps.bit_length() - 1
    widths = (halves_of(width)[0].size, halves_of(width)[1].size)
    scratch = []
    for wide in widths:
        for at in range(bits):
            scratch.append(
                pltpu.VMEM((shard_count, reps // 2 ** (at + 1), rows, wide), parts.dtype)
            )
    if shard_count > 1:
        scratch += [pltpu.VMEM((shard_count - 1, rows, wide), parts.dtype) for wide in widths]
        scratch += [pltpu.SemaphoreType.DMA((HALVES, shard_count)) for _ in range(2)]
    scratch += [pltpu.SemaphoreType.DMA((HALVES, bits)) for _ in range(4)]
    out = pl.pallas_call(
        lambda *refs: reduce_kernel(reps, shard_count, *refs),
        out_shape=jax.ShapeDtypeStruct((1, reps, rows, width), parts.dtype),
        in_specs=[pl.BlockSpec(memory_space=pltpu.VMEM)],
        out_specs=pl.BlockSpec(memory_space=pltpu.VMEM),
        scratch_shapes=scratch,
        compiler_params=pltpu.CompilerParams(
            collective_id=number, has_side_effects=True, vmem_limit_bytes=VMEM_BYTES
        ),
        cost_estimate=pl.CostEstimate(
            flops=0, bytes_accessed=32 * total * width, transcendentals=0
        ),
    )(parts.reshape(shard_count, reps, rows, width))
    return out.reshape(reps * rows, width)


def gather_shard(piece):
    return lax.all_gather(piece, "shard", axis=0, tiled=True)


def shards(
    tokens,
    doc_ids,
    routes,
    norm_in_gain,
    w_query,
    w_key,
    w_value,
    w_out,
    norm_mid_gain,
    w_router,
    w_expert_in,
    w_expert_down,
    cotangent,
):
    bf16, f32 = jnp.bfloat16, jnp.float32
    row_count, model_width = tokens.shape
    groups = HEADS // KV_HEADS
    query_cols = w_query.shape[1]
    kv_cols = w_key.shape[1]
    own_rows = w_query.shape[0]
    own_experts, ff = w_expert_down.shape[:2]
    shard_at = lax.axis_index("shard")

    small = jnp.concatenate(
        [
            w_router,
            norm_in_gain[:, None],
            norm_mid_gain[:, None],
            jnp.zeros((own_rows, PAD - EXPERTS - 2), bf16),
        ],
        axis=1,
    )
    reps, shard_count = (lax.axis_size("rep"), lax.axis_size("shard"))
    all_w = gather_all(
        jnp.concatenate([w_query, w_key, w_value, w_out, small], axis=1), reps, shard_count, 1
    )
    qkv_cols = query_cols + 2 * kv_cols
    qkv_w = all_w[:, :qkv_cols]
    out_w = all_w[:, qkv_cols : qkv_cols + w_out.shape[1]]
    small_full = all_w[:, qkv_cols + w_out.shape[1] :]
    router_full = small_full[:, :EXPERTS]
    gain_in = small_full[:, EXPERTS].astype(f32)
    gain_mid = small_full[:, EXPERTS + 1].astype(f32)
    mask_own = jnp.any(
        routes[:, :, None] == jnp.arange(EXPERTS, dtype=jnp.int32)[None, None, :], axis=1
    )
    side = jnp.concatenate(
        [cotangent, mask_own.astype(bf16), jnp.zeros((row_count, PAD - EXPERTS), bf16)], axis=1
    )
    side_all = gather_shard(side)
    dy_all = side_all[:, :model_width]
    mask_all = side_all[:, model_width : model_width + EXPERTS] > 0

    inputs = tokens.astype(f32)
    grad_final = cotangent.astype(f32)
    cosine, sine_table = rotary_tables(positions(doc_ids), HEAD_DIM)
    normed_in, scale_in = normalize(inputs)
    first_low = (normed_in * gain_in).astype(bf16)
    qkv_pre = jnp.dot(first_low, qkv_w, preferred_element_type=f32)
    query_pre = qkv_pre[:, :query_cols]
    key_pre = qkv_pre[:, query_cols : query_cols + kv_cols]
    value_pre = qkv_pre[:, query_cols + kv_cols :]
    query_rows = (
        rotate(query_pre.reshape(row_count, HEADS, HEAD_DIM), cosine, sine_table)
        .astype(bf16)
        .reshape(row_count, KV_HEADS, groups, HEAD_DIM)
    )
    key_rows = rotate(key_pre.reshape(row_count, KV_HEADS, HEAD_DIM), cosine, sine_table).astype(
        bf16
    )
    value_rows = value_pre.astype(bf16).reshape(row_count, KV_HEADS, HEAD_DIM)
    att_rows, log_sums = attend(query_rows, key_rows, value_rows, doc_ids)
    att_low = att_rows.reshape(row_count, query_cols)
    middle = inputs + jnp.dot(att_low, out_w, preferred_element_type=f32)
    normed_mid, scale_mid = normalize(middle)
    second_low = (normed_mid * gain_mid).astype(bf16)

    second_all = gather_shard(second_low)
    logits = jnp.dot(second_all, router_full, preferred_element_type=f32)
    chosen = jnp.where(mask_all, logits, masked_score)
    gate_exp = jnp.where(mask_all, jnp.exp(chosen - jnp.max(chosen, axis=1, keepdims=True)), 0.0)
    gates_all = gate_exp / jnp.sum(gate_exp, axis=1, keepdims=True)
    gates_here = lax.dynamic_slice_in_dim(gates_all, shard_at * own_experts, own_experts, axis=1)
    gates_own = lax.dynamic_slice_in_dim(gates_all, shard_at * row_count, row_count, axis=0)

    gated, grad_both, grad_gates_here = experts(
        second_all, dy_all, gates_here, w_expert_in, w_expert_down
    )
    combined = jnp.einsum("etf,efd->td", gated, w_expert_down, preferred_element_type=f32)
    combined_own = lax.psum_scatter(
        combined.astype(bf16), "shard", scatter_dimension=0, tiled=True
    )
    grad_second_here = jnp.einsum("etf,edf->td", grad_both, w_expert_in, preferred_element_type=f32)
    gate_cols = lax.dynamic_update_slice_in_dim(
        jnp.zeros((grad_gates_here.shape[0], EXPERTS), f32),
        grad_gates_here,
        shard_at * own_experts,
        axis=1,
    )
    gate_high = gate_cols.astype(bf16)
    gate_low = (gate_cols - gate_high.astype(f32)).astype(bf16)
    back_rows = jnp.concatenate(
        [
            grad_second_here.astype(bf16),
            gate_high,
            gate_low,
            jnp.zeros((gate_cols.shape[0], PAD - 2 * EXPERTS), bf16),
        ],
        axis=1,
    )
    back_own = lax.psum_scatter(back_rows, "shard", scatter_dimension=0, tiled=True)
    grad_in_here = jnp.einsum("td,etf->edf", second_all, grad_both, preferred_element_type=f32)
    grad_down_here = jnp.einsum("etf,td->efd", gated, dy_all, preferred_element_type=f32)
    expert_grads = jnp.concatenate([grad_in_here.astype(bf16), grad_down_here.astype(bf16)], axis=1)
    expert_own = reduce_all(expert_grads.reshape(-1, model_width), reps, 1, 2)
    back_own, expert_own = lax.optimization_barrier((back_own, expert_own))
    expert_own = expert_own.reshape(expert_grads.shape)
    grad_in_own = expert_own[:, :model_width].astype(f32)
    grad_down_own = expert_own[:, model_width:].astype(f32)

    mixed = (middle + combined_own.astype(f32)).astype(bf16)
    gate_back = back_own[:, model_width : model_width + 2 * EXPERTS].astype(f32)
    grad_gates = gate_back[:, :EXPERTS] + gate_back[:, EXPERTS:]
    grad_logits = (
        gates_own * (grad_gates - jnp.sum(gates_own * grad_gates, axis=1, keepdims=True))
    ).astype(bf16)
    grad_router = jnp.einsum("td,te->de", second_low, grad_logits, preferred_element_type=f32)
    grad_second = back_own[:, :model_width].astype(f32) + jnp.einsum(
        "te,de->td", grad_logits, router_full, preferred_element_type=f32
    )
    grad_mid_norm, grad_gain_mid = norm_back(grad_second, normed_mid, scale_mid, gain_mid)
    grad_middle = grad_final + grad_mid_norm
    grad_branch = grad_middle.astype(bf16)
    grad_out_w = jnp.einsum("ta,td->ad", att_low, grad_branch, preferred_element_type=f32)
    grad_att = jnp.einsum("td,ad->ta", grad_branch, out_w, preferred_element_type=f32).astype(bf16)
    grad_query_rot, grad_key_rot, grad_value_rows = attend_back(
        query_rows,
        key_rows,
        value_rows,
        doc_ids,
        log_sums,
        grad_att.reshape(row_count, KV_HEADS, groups, HEAD_DIM),
    )
    grad_query_pre = (
        unrotate(grad_query_rot.reshape(row_count, HEADS, HEAD_DIM), cosine, sine_table)
        .astype(bf16)
        .reshape(row_count, query_cols)
    )
    grad_key_pre = unrotate(grad_key_rot, cosine, sine_table).astype(bf16)
    grad_pre = jnp.concatenate(
        [
            grad_query_pre,
            grad_key_pre.reshape(row_count, kv_cols),
            grad_value_rows.astype(bf16).reshape(row_count, kv_cols),
        ],
        axis=1,
    )
    grad_qkv = jnp.einsum("td,tc->dc", first_low, grad_pre, preferred_element_type=f32)
    columns = jnp.einsum("tc,dc->td", grad_pre, qkv_w, preferred_element_type=f32)
    grad_in_norm, grad_gain_in = norm_back(columns, normed_in, scale_in, gain_in)
    grad_tokens = grad_middle + grad_in_norm

    joint = jnp.concatenate(
        [
            grad_qkv.astype(bf16),
            grad_out_w.astype(bf16),
            grad_router.astype(bf16),
            grad_gain_in.astype(bf16)[:, None],
            grad_gain_mid.astype(bf16)[:, None],
            jnp.zeros((model_width, PAD - EXPERTS - 2), bf16),
        ],
        axis=1,
    )
    joint_own = reduce_all(joint, reps, shard_count, 3).astype(f32)
    edges = [0]
    for width in (query_cols, kv_cols, kv_cols, w_out.shape[1], EXPERTS, 1, 1):
        edges.append(edges[-1] + width)
    pieces = [joint_own[:, a:b] for a, b in zip(edges[:-1], edges[1:])]
    query_own, key_own, value_own, out_own, router_own, gain_in_own, gain_mid_own = pieces
    return (
        mixed,
        grad_tokens,
        gain_in_own[:, 0],
        query_own,
        key_own,
        value_own,
        out_own,
        gain_mid_own[:, 0],
        router_own,
        grad_in_own,
        grad_down_own,
    )


def experts(rows, dy_rows, gates, in_w, down_w):
    f32, bf16 = jnp.float32, jnp.bfloat16
    both = jnp.einsum("td,edf->etf", rows, in_w, preferred_element_type=f32)
    half_width = both.shape[-1] // 2
    gate_part, up_part = (both[..., :half_width], both[..., half_width:])
    sigmoid_gate = jax.nn.sigmoid(gate_part)
    silu_gate = gate_part * sigmoid_gate
    hidden = (silu_gate * up_part).astype(bf16).astype(f32)
    back = jnp.einsum("td,efd->etf", dy_rows, down_w, preferred_element_type=f32)
    gate_cols = gates.T[:, :, None]
    grad_gates = jnp.sum(hidden * back, axis=-1).T
    gated = (hidden * gate_cols).astype(bf16)
    grad_hidden = back * gate_cols
    grad_gate = grad_hidden * up_part * sigmoid_gate * (1.0 + gate_part * (1.0 - sigmoid_gate))
    grad_both = jnp.concatenate([grad_gate, grad_hidden * silu_gate], axis=-1).astype(bf16)
    return (gated, grad_both, grad_gates)


def solution(mesh):
    in_specs = (
        P(("rep", "shard"), None),
        P(("rep", "shard")),
        P(("rep", "shard"), None),
        P("shard"),
        P("shard", None),
        P("shard", None),
        P("shard", None),
        P("shard", None),
        P("shard"),
        P("shard", None),
        P("shard", None, None),
        P("shard", None, None),
        P(("rep", "shard"), None),
    )
    out_specs = (
        P(("rep", "shard"), None),
        P(("rep", "shard"), None),
        P("shard"),
        P("shard", None),
        P("shard", None),
        P("shard", None),
        P("shard", None),
        P("shard"),
        P("shard", None),
        P("shard", None, None),
        P("shard", None, None),
    )
    return jax.shard_map(shards, mesh=mesh, in_specs=in_specs, out_specs=out_specs, check_vma=False)
```

profile of v0, /device:TPU:0, one launch (start us, length us, event | category | flops | bytes accessed | tf_op | source)
XLA Modules:
  0.0 757.9 jit_solution(7413480688803308159)
XLA Ops:
  13.7 61.6 %shard_map.222 = bf16[4,8,32,3200]{3,2,1,0:T(8,128)(2,1)} custom-call(bf16[8,32,3200]{2,1,0:T(8,128)(2,1)} %concatenate.81.refs_0_), custom_call_target="tpu_custom_call" | custom-call | bytes 52428800 | tf_op jit(solution)/shard_map/pallas_call | solution.py:220
  78.4 4.8 fusion.24
  96.8 9.0 %fusion.79 = (f32[8,2,512]{2,1,0:T(2,128)S(1)}, f32[8,2,512,512]{2,3,1,0:T(8,128)}) fusion(bf16[512,8,2,32]{0,3,2,1:T(8,128)(2,1)} %bitcast.156, bf16[512,8,2,32]{0,3,2,1:T(8,128)(2,1)} %bitcast.154, bf16[512,8,32]{0,2,1:T(8,128)(2,1)S(1)} %get-tuple-element.95, bf16[512,8,32]{0,2,1:T(8,128)(2,1)S(1)} %get-tuple-element.94, pred[512,512]{0,1:T(8,128)(4,1)S(1)} %fusion.59), kind=kOutput, calls=%fused_computation.145 | convolution fusion | flops 552591360 | bytes 18644992 | tf_op jit(solution)/shard_map/qgrd,kgd->grqk/dot_general | solution.py:66
  105.8 8.2 %fusion.6 = f32[8,2,512]{2,1,0:T(2,128)S(1)} fusion(f32[8,2,512,512]{2,3,1,0:T(8,128)} %get-tuple-element.99, f32[8,2,512]{2,1,0:T(2,128)S(1)} %get-tuple-element.98), kind=kLoop, calls=%fused_computation.21 | loop fusion | flops 8380416 | bytes 16842752 | tf_op jit(solution)/shard_map/reduce_sum | solution.py:81
  114.0 8.0 %fusion.47 = bf16[8,64,2,512]{3,1,2,0:T(8,128)(2,1)S(1)} fusion(bf16[512,8,64,1]{0,2,3,1:T(8,128)(2,1)S(1)} %bitcast.152, f32[8,2,512,512]{2,3,1,0:T(8,128)} %get-tuple-element.99, f32[8,2,512]{2,1,0:T(2,128)S(1)} %fusion.6, f32[8,2,512]{2,1,0:T(2,128)S(1)} %get-tuple-element.98), kind=kOutput, calls=%fused_computation.77 | convolution fusion | flops 549978112 | bytes 18415616 | tf_op jit(solution)/shard_map/grqk,kgd->qgrd/dot_general | solution.py:83
  131.6 76.7 %all-gather.3.cloned.1.call-done = bf16[2048,1024]{0,1:T(8,128)(2,1)} async-done(((bf16[512,1024]{0,1:T(8,128)(2,1)}), bf16[2048,1024]{0,1:T(8,128)(2,1)}) %all-gather.3.cloned.1.call-update) | async-done | bytes 4194320 | tf_op jit(solution)/shard_map/all_gather | solution.py:352
  208.3 25.3 %convolution_bitcast_fusion = f32[4,2048,1024]{1,2,0:T(8,128)} fusion(bf16[4,1024,1024]{2,1,0:T(8,128)(2,1)} %param.31, bf16[2048,1024]{0,1:T(8,128)(2,1)} %all-gather.3.cloned.1.call-done), kind=kOutput, calls=%fused_computation.2 | convolution fusion | flops 17179869184 | bytes 46137344 | tf_op jit(solution)/shard_map/td,edf->etf/dot_general | solution.py:552
  233.5 64.9 %all-gather.5.cloned.1.call-done = bf16[2048,1152]{0,1:T(8,128)(2,1)} async-done(((bf16[512,1152]{0,1:T(8,128)(2,1)}), bf16[2048,1152]{0,1:T(8,128)(2,1)}) %all-gather.5.cloned.1.call-update) | async-done | bytes 4718608 | tf_op jit(solution)/shard_map/all_gather | solution.py:352
  303.9 28.4 %multiply_convert_fusion.1 = (bf16[4,2048,512]{1,2,0:T(8,128)(2,1)}, bf16[4,2048,512]{1,2,0:T(8,128)(2,1)}, f32[4,2048]{1,0:T(4,128)S(1)}, bf16[4,2048,512]{1,2,0:T(8,128)(2,1)}) fusion(f32[4,2048,1024]{1,2,0:T(8,128)} %convolution_bitcast_fusion, f32[4,2048]{1,0:T(4,128)S(1)} %dynamic-slice_bitcast_fusion, bf16[4,512,1024]{2,1,0:T(8,128)(2,1)} %param.32, ...), kind=kOutput, calls=%fused_computation.15 | convolution fusion | flops 8669618176 | bytes 67174400 | tf_op jit(solution)/shard_map/td,efd->etf/dot_general | solution.py:558
  332.3 22.9 %bitcast_convert_fusion = bf16[2048,1024]{0,1:T(8,128)(2,1)S(1)} fusion(bf16[4,1024,1024]{2,1,0:T(8,128)(2,1)} %param.31, bf16[4,2048,512]{1,2,0:T(8,128)(2,1)} %get-tuple-element.77, bf16[4,2048,512]{1,2,0:T(8,128)(2,1)} %get-tuple-element.76), kind=kOutput, calls=%fused_computation.28 | convolution fusion | flops 17215520768 | bytes 29360128 | tf_op jit(solution)/shard_map/etf,edf->td/dot_general | solution.py:448
  355.2 6.3 maximum_maximum_fusion
  361.6 14.0 %bitcast_convert_fusion.1 = bf16[2048,1024]{0,1:T(8,128)(2,1)} fusion(bf16[4,512,1024]{2,1,0:T(8,128)(2,1)} %param.32, bf16[4,2048,512]{1,2,0:T(8,128)(2,1)} %get-tuple-element.79, f32[4,2048]{1,0:T(4,128)S(1)} %dynamic-slice_bitcast_fusion), kind=kOutput, calls=%fused_computation.29 | convolution fusion | flops 8604614656 | bytes 16809984 | tf_op jit(solution)/shard_map/etf,efd->td/dot_general | solution.py:444
  376.3 13.9 %fusion.31 = bf16[4,512,1024]{2,1,0:T(8,128)(2,1)} fusion(bf16[2048,1152]{0,1:T(8,128)(2,1)} %all-gather.5.cloned.1.call-done, bf16[4,2048,512]{1,2,0:T(8,128)(2,1)} %get-tuple-element.79, f32[4,2048]{1,0:T(4,128)S(1)} %dynamic-slice_bitcast_fusion), kind=kOutput, calls=%fused_computation.53 | convolution fusion | flops 8604614656 | bytes 16809984 | tf_op jit(solution)/shard_map/etf,td->efd/dot_general | solution.py:468
  390.1 24.5 %convert_bitcast_fusion = bf16[4,1024,1024]{2,1,0:T(8,128)(2,1)} fusion(bf16[4,2048,512]{1,2,0:T(8,128)(2,1)} %get-tuple-element.77, bf16[4,2048,512]{1,2,0:T(8,128)(2,1)} %get-tuple-element.76, bf16[2048,1024]{0,1:T(8,128)(2,1)} %all-gather.3.cloned.1.call-done), kind=kOutput, calls=%fused_computation.31 | convolution fusion | flops 17217617920 | bytes 29360128 | tf_op jit(solution)/shard_map/td,etf->edf/dot_general | solution.py:467
  414.7 13.3 %pad_maximum_fusion.1 = bf16[4,1536,1024]{2,1,0:T(8,128)(2,1)} fusion(bf16[4,512,1024]{2,1,0:T(8,128)(2,1)} %fusion.31, bf16[4,1024,1024]{2,1,0:T(8,128)(2,1)} %convert_bitcast_fusion), kind=kLoop, calls=%fused_computation.23 | loop fusion | flops 25165824 | bytes 25165824 | tf_op jit(solution)/shard_map/concatenate | solution.py:469
  428.0 139.1 %shard_map.223 = bf16[1,8,768,1024]{3,2,1,0:T(8,128)(2,1)} custom-call(bf16[1,8,768,1024]{3,2,1,0:T(8,128)(2,1)} %bitcast.136), custom_call_target="tpu_custom_call" | custom-call | bytes 201326592 | tf_op jit(solution)/shard_map/pallas_call | solution.py:335
  579.8 15.1 %fusion.2 = (f32[8,2,512]{2,1,0:T(2,128)S(1)}, f32[8,512,512,2]{2,1,3,0:T(8,128)}) fusion(f32[8,2,512,512]{2,3,1,0:T(8,128)} %get-tuple-element.99, f32[8,2,512]{2,1,0:T(2,128)} %bitcast.168, bf16[512,8,64,1]{0,2,3,1:T(8,128)(2,1)S(1)} %bitcast.153, bf16[512,8,2,64]{0,3,2,1:T(8,128)(2,1)S(1)} %bitcast.137), kind=kOutput, calls=%fused_computation.8 | convolution fusion | flops 549445632 | bytes 35192832 | tf_op jit(solution)/shard_map/qgrd,kgd->grqk/dot_general | solution.py:98
  596.2 8.3 %fusion.4 = bf16[8,2,512,512]{2,3,1,0:T(8,128)(2,1)S(1)} fusion(f32[8,512,512,2]{2,1,3,0:T(8,128)} %get-tuple-element.106, f32[8,2,512,512]{2,3,1,0:T(8,128)S(1)} %bitcast.133, f32[8,2,512]{2,1,0:T(2,128)S(1)} %get-tuple-element.105, f32[8,2,512]{2,1,0:T(2,128)S(1)} %bitcast.170), kind=kLoop, calls=%fused_computation.10 | loop fusion | flops 16777216 | bytes 42008576 | tf_op jit(solution)/shard_map/convert_element_type | solution.py:102
  610.8 6.0 fusion.55
  631.0 5.0 fusion.39
  639.6 10.5 %concatenate.98.refs_0_ = bf16[4,8,32,3200]{3,2,1,0:T(8,128)(2,1)} concatenate(bf16[4,8,32,2048]{3,2,1,0:T(8,128)(2,1)} %bitcast.150, bf16[4,8,32,1024]{3,2,1,0:T(8,128)(2,1)S(1)} %bitcast.158, bf16[4,8,32,16]{3,2,1,0:T(8,128)(2,1)} %bitcast.159, bf16[4,8,32,1]{3,2,1,0:T(8,128)(2,1)S(1)} %convert_element_type.237, bf16[4,8,32,1]{3,2,1,0:T(8,128)(2,1)} %convert_element_type.238, ...), dimensions={3} | concatenate | bytes 13107200 | tf_op jit(solution)/shard_map/concatenate | solution.py:518
  650.1 71.0 %shard_map.224 = bf16[1,8,32,3200]{3,2,1,0:T(8,128)(2,1)} custom-call(bf16[4,8,32,3200]{3,2,1,0:T(8,128)(2,1)} %concatenate.98.refs_0_), custom_call_target="tpu_custom_call" | custom-call | bytes 104857600 | tf_op jit(solution)/shard_map/pallas_call | solution.py:335
  726.3 11.7 %slice_convert_fusion = f32[4,1024,1024]{2,1,0:T(8,128)} fusion(bf16[4,1536,1024]{2,1,0:T(8,128)(2,1)} %bitcast.134), kind=kLoop, calls=%fused_computation.27 | loop fusion | flops 4194304 | bytes 25165824 | tf_op jit(solution)/shard_map/convert_element_type | solution.py:473
  738.0 6.6 slice_convert_fusion.1
  (193 shorter events, 88.1 us)
Async XLA Ops:
  7.2 201.1 %all-gather.3.cloned.1.call-start = ((), (), s32[]{:S(2)}) async-start(), calls=%async_computation.2 | async-start | bytes 5242880 | tf_op jit(solution)/shard_map/all_gather | solution.py:352
  13.7 63.9 %copy-start.20 = (bf16[512,1024]{1,0:T(8,128)(2,1)S(1)}, bf16[512,1024]{1,0:T(8,128)(2,1)}, u32[]{:S(2)}) copy-start(bf16[512,1024]{1,0:T(8,128)(2,1)} %param.21) | copy-start | bytes 3145732
  78.1 44.0 %copy-start.4 = (bf16[512,1024]{0,1:T(8,128)(2,1)}, bf16[512,1024]{0,1:T(8,128)(2,1)S(1)}, u32[]{:S(2)}) copy-start(bf16[512,1024]{0,1:T(8,128)(2,1)S(1)} %copy.134) | copy-start | bytes 3145732
  95.3 10.5 %copy-start.21 = (bf16[512,8,32]{0,2,1:T(8,128)(2,1)}, bf16[512,8,32]{0,2,1:T(8,128)(2,1)S(1)}, u32[]{:S(2)}) copy-start(bf16[512,8,32]{0,2,1:T(8,128)(2,1)S(1)} %get-tuple-element.94) | copy-start | bytes 786436
  95.3 10.5 %copy-start.23 = (bf16[512,8,32]{0,2,1:T(8,128)(2,1)}, bf16[512,8,32]{0,2,1:T(8,128)(2,1)S(1)}, u32[]{:S(2)}) copy-start(bf16[512,8,32]{0,2,1:T(8,128)(2,1)S(1)} %get-tuple-element.95) | copy-start | bytes 786436
  96.7 17.3 %copy-start.11 = (bf16[512,512]{0,1:T(8,128)(2,1)}, bf16[512,512]{0,1:T(8,128)(2,1)S(1)}, u32[]{:S(2)}) copy-start(bf16[512,512]{0,1:T(8,128)(2,1)S(1)} %copy.139) | copy-start | bytes 1572868
  128.4 170.0 %all-gather.5.cloned.1.call-start = ((), (), s32[]{:S(2)}) async-start(), calls=%async_computation.3 | async-start | bytes 5898240 | tf_op jit(solution)/shard_map/all_gather | solution.py:352
  129.9 103.6 %copy-start.6 = (bf16[512,1024]{0,1:T(8,128)(2,1)}, bf16[512,1024]{0,1:T(8,128)(2,1)S(1)}, u32[]{:S(2)}) copy-start(bf16[512,1024]{0,1:T(8,128)(2,1)S(1)} %copy.147) | copy-start | bytes 3145732
  131.4 435.7 %reduce-scatter.5.cloned.1.call-start = ((), (), s32[]{:S(2)}) async-start(), calls=%async_computation.5 | async-start | bytes 5898240 | tf_op jit(solution)/shard_map/reduce_scatter | solution.py:466
  361.5 209.8 %reduce-scatter.3.cloned.1.call-start = ((), (), s32[]{:S(2)}) async-start(), calls=%async_computation.4 | async-start | bytes 5242880 | tf_op jit(solution)/shard_map/reduce_scatter | solution.py:445
  361.6 14.1 %copy-start.30 = (f32[8,2,512]{2,1,0:T(2,128)S(1)}, f32[8,2,512]{2,1,0:T(2,128)}, u32[]{:S(2)}) copy-start(f32[8,2,512]{2,1,0:T(2,128)} %copy-done.29) | copy-start | bytes 98308
  361.6 14.1 %copy-start.32 = (f32[8,2,512]{2,1,0:T(2,128)S(1)}, f32[8,2,512]{2,1,0:T(2,128)}, u32[]{:S(2)}) copy-start(f32[8,2,512]{2,1,0:T(2,128)} %copy-done.31) | copy-start | bytes 98308
  428.0 140.0 %copy-start.28 = (f32[2048,16]{0,1:T(8,128)S(1)}, f32[2048,16]{0,1:T(8,128)}, u32[]{:S(2)}) copy-start(f32[2048,16]{0,1:T(8,128)} %copy-done.27) | copy-start | bytes 393220
  428.0 140.0 %copy-start.2 = (f32[512,1024]{0,1:T(8,128)S(1)}, f32[512,1024]{0,1:T(8,128)}, u32[]{:S(2)}) copy-start(f32[512,1024]{0,1:T(8,128)} %copy-done.1) | copy-start | bytes 6291460
  428.0 140.0 %copy-start.34 = (f32[1024,1]{0,1:T(1,128)S(1)}, f32[1024,1]{0,1:T(1,128)}, u32[]{:S(2)}) copy-start(f32[1024,1]{0,1:T(1,128)} %copy-done.33) | copy-start | bytes 12292
  428.0 140.0 %copy-start.37 = (f32[512]{0:T(512)S(1)}, f32[512]{0:T(512)}, u32[]{:S(2)}) copy-start(f32[512]{0:T(512)} %copy-done.36) | copy-start | bytes 6148
  579.7 15.1 %slice-start = ((s8[16777216]{0:T(1024)(128)(4,1)}), s8[4194304]{0:T(1024)(128)(4,1)S(1)}, s32[]{:S(2)}) async-start(s8[16777216]{0:T(1024)(128)(4,1)} %bitcast.132), calls=%async_computation.6 | async-start | bytes 8388608
  579.8 15.1 %slice-start.1 = ((s8[16777216]{0:T(1024)(128)(4,1)}), s8[4194304]{0:T(1024)(128)(4,1)S(1)}, s32[]{:S(2)}) async-start(s8[16777216]{0:T(1024)(128)(4,1)} %bitcast.132), calls=%async_computation.7 | async-start | bytes 8388608
  579.8 15.1 %slice-start.2 = ((s8[16777216]{0:T(1024)(128)(4,1)}), s8[4194304]{0:T(1024)(128)(4,1)S(1)}, s32[]{:S(2)}) async-start(s8[16777216]{0:T(1024)(128)(4,1)} %bitcast.132), calls=%async_computation.8 | async-start | bytes 8388608
  579.8 16.4 %slice-start.3 = ((s8[16777216]{0:T(1024)(128)(4,1)}), s8[4194304]{0:T(1024)(128)(4,1)S(1)}, s32[]{:S(2)}) async-start(s8[16777216]{0:T(1024)(128)(4,1)} %bitcast.132), calls=%async_computation.9 | async-start | bytes 8388608
  579.8 16.4 %copy-start.26 = (f32[2,8,512]{2,1,0:T(8,128)S(1)}, f32[2,8,512]{2,1,0:T(8,128)}, u32[]{:S(2)}) copy-start(f32[2,8,512]{2,1,0:T(8,128)} %log_add_fusion) | copy-start | bytes 98308
  596.2 11.7 %copy-start.22 = (bf16[512,8,32]{0,2,1:T(8,128)(2,1)S(1)}, bf16[512,8,32]{0,2,1:T(8,128)(2,1)}, u32[]{:S(2)}) copy-start(bf16[512,8,32]{0,2,1:T(8,128)(2,1)} %copy-done.21) | copy-start | bytes 786436
  596.2 11.7 %copy-start.24 = (bf16[512,8,32]{0,2,1:T(8,128)(2,1)S(1)}, bf16[512,8,32]{0,2,1:T(8,128)(2,1)}, u32[]{:S(2)}) copy-start(bf16[512,8,32]{0,2,1:T(8,128)(2,1)} %copy-done.23) | copy-start | bytes 786436
  631.0 8.6 %copy-start.15 = (bf16[1024,1024]{1,0:T(8,128)(2,1)S(1)}, bf16[1024,1024]{1,0:T(8,128)(2,1)}, u32[]{:S(2)}) copy-start(bf16[1024,1024]{1,0:T(8,128)(2,1)} %convolution_convert_fusion.1) | copy-start | bytes 6291460
  (31 other events, 117.0 us)
Sparse Core Ops, SparseCore 0:
  128.5 79.7 all-gather.2
  210.4 87.9 all-gather.4
  361.6 83.6 reduce-scatter.4
  447.5 77.2 reduce-scatter.2
where the time goes:
time: 768 us; the launch traced here: 758 us
  Pallas kernels  272 us (35%)
  matrix products  206 us (27%)
  waiting for transfers between devices  142 us (18%)
  other arithmetic  75 us (10%)
  local copies, waits for them, and re-layouts  49 us (6%)
  between operations  14.8 us (2%)
    pallas_call x2, Pallas kernels, reduce_all(): pl.pallas_call(lambda *refs: reduce_kernel(reps, shard_count, *refs), out...  210 us
    all_gather x2, waiting for transfers between devices, gather_shard(): return lax.all_gather(piece, 'shard', axis=0, tiled=True)  142 us
    pallas_call x1, Pallas kernels, gather_all(): pl.pallas_call(lambda *refs: gather_kernel(reps, shard_count, *refs), out...  61.6 us
    dot_general x1, matrix products, experts(): jnp.einsum('td,efd->etf', dy_rows, down_w, preferred_element_type=f32)  28.4 us
    dot_general x1, matrix products, experts(): both = jnp.einsum('td,edf->etf', rows, in_w, preferred_element_type=f32)  25.3 us
    dot_general x1, matrix products, shards(): jnp.einsum('td,etf->edf', second_all, grad_both, preferred_element_type=f32)  24.5 us
    dot_general x1, matrix products, shards(): jnp.einsum('etf,edf->td', grad_both, w_expert_in, preferred_element_type=...  22.9 us
    unnamed x110, local copies, waits for them, and re-layouts  15.9 us
  transfers between devices with their start and end apart: 4, of which 2 were waited for; matrix products, arithmetic and copies ran while one was open for 13% of the time, Pallas kernels for 18%

commit v1 on v0

--- a/solution.py
+++ b/solution.py
@@ -21,8 +21,7 @@
 def positions(doc_rows):
     row_count = doc_rows.shape[0]
     places = jnp.arange(row_count, dtype=jnp.int32)
-    opening = jnp.concatenate([jnp.ones((1,), dtype=jnp.bool_), doc_rows[1:] != doc_rows[:-1]])
-    begins = lax.cummax(jnp.where(opening, places, 0), axis=0)
+    begins = jnp.sum((doc_rows[None, :] < doc_rows[:, None]).astype(jnp.int32), axis=1)
     return places - begins
 
 
@@ -403,8 +402,6 @@
         [cotangent, mask_own.astype(bf16), jnp.zeros((row_count, PAD - EXPERTS), bf16)], axis=1
     )
     side_all = gather_shard(side)
-    dy_all = side_all[:, :model_width]
-    mask_all = side_all[:, model_width : model_width + EXPERTS] > 0
 
     inputs = tokens.astype(f32)
     grad_final = cotangent.astype(f32)
@@ -430,6 +427,9 @@
     normed_mid, scale_mid = normalize(middle)
     second_low = (normed_mid * gain_mid).astype(bf16)
 
+    second_low, side_all = lax.optimization_barrier((second_low, side_all))
+    dy_all = side_all[:, :model_width]
+    mask_all = side_all[:, model_width : model_width + EXPERTS] > 0
     second_all = gather_shard(second_low)
     logits = jnp.dot(second_all, router_full, preferred_element_type=f32)
     chosen = jnp.where(mask_all, logits, masked_score)
@@ -466,12 +466,11 @@
     back_own = lax.psum_scatter(back_rows, "shard", scatter_dimension=0, tiled=True)
     grad_in_here = jnp.einsum("td,etf->edf", second_all, grad_both, preferred_element_type=f32)
     grad_down_here = jnp.einsum("etf,td->efd", gated, dy_all, preferred_element_type=f32)
-    expert_grads = jnp.concatenate([grad_in_here.astype(bf16), grad_down_here.astype(bf16)], axis=1)
-    expert_own = reduce_all(expert_grads.reshape(-1, model_width), reps, 1, 2)
-    back_own, expert_own = lax.optimization_barrier((back_own, expert_own))
-    expert_own = expert_own.reshape(expert_grads.shape)
-    grad_in_own = expert_own[:, :model_width].astype(f32)
-    grad_down_own = expert_own[:, model_width:].astype(f32)
+    grad_in_own, grad_down_own = lax.optimization_barrier(
+        lax.psum((grad_in_here.astype(bf16), grad_down_here.astype(bf16)), "rep")
+    )
+    grad_in_own = grad_in_own.astype(f32)
+    grad_down_own = grad_down_own.astype(f32)
 
     mixed = (middle + combined_own.astype(f32)).astype(bf16)
     gate_back = back_own[:, model_width : model_width + 2 * EXPERTS].astype(f32)

time: 768 us -> 841 us (1.095)
  waiting for transfers between devices: 142 us -> 353 us
  Pallas kernels: 272 us -> 147 us
  other arithmetic: 75 us -> 49.7 us
  local copies, waits for them, and re-layouts: 49 us -> 59.9 us
    pallas_call x2 -> x1, Pallas kernels: 210 us -> 71.1 us  [reduce_all(): pl.pallas_call(lambda *refs: reduce_kernel(reps, shard_count, *refs), out...]
    psum x0 -> x1, waiting for transfers between devices: none -> 124 us  [shards(): lax.psum((grad_in_here.astype(bf16), grad_down_here.astype(bf16)), 'rep')]
    reduce_scatter x1, waiting for transfers between devices: 0.01 us -> 75.4 us  [shards(): lax.psum_scatter(combined.astype(bf16), 'shard', scatter_dimension=0, til...]
    reduce_scatter x1, waiting for transfers between devices: 0.02 us -> 67.9 us  [shards(): lax.psum_scatter(back_rows, 'shard', scatter_dimension=0, tiled=True)]
    all_gather x2, waiting for transfers between devices: 142 us -> 85.1 us  [gather_shard(): return lax.all_gather(piece, 'shard', axis=0, tiled=True)]
    pallas_call x1, Pallas kernels: 61.6 us -> 75.8 us  [gather_all(): pl.pallas_call(lambda *refs: gather_kernel(reps, shard_count, *refs), out...]
    unnamed x110 -> x129, local copies, waits for them, and re-layouts: 15.9 us -> 29.6 us
    concatenate x1 -> x0, other arithmetic: 13.3 us -> none  [shards(): jnp.concatenate([grad_in_here.astype(bf16), grad_down_here.astype(bf16)],...]
  transfers between devices with their start and end apart: 4 -> 5, of which waited for: 2 -> 4; matrix products, arithmetic and copies ran while one was open for 13% -> 15% of each run, Pallas kernels for 18% -> 9%
where the time goes in v1:
time: 841 us; the launch traced here: 830 us
  waiting for transfers between devices  353 us (42%)
  matrix products  205 us (24%)
  Pallas kernels  147 us (17%)
  local copies, waits for them, and re-layouts  59.9 us (7%)
  other arithmetic  49.7 us (6%)
  between operations  14.9 us (2%)
    psum x1, waiting for transfers between devices, shards(): lax.psum((grad_in_here.astype(bf16), grad_down_here.astype(bf16)), 'rep')  124 us
    all_gather x2, waiting for transfers between devices, gather_shard(): return lax.all_gather(piece, 'shard', axis=0, tiled=True)  85.1 us
    pallas_call x1, Pallas kernels, gather_all(): pl.pallas_call(lambda *refs: gather_kernel(reps, shard_count, *refs), out...  75.8 us
    reduce_scatter x1, waiting for transfers between devices, shards(): lax.psum_scatter(combined.astype(bf16), 'shard', scatter_dimension=0, til...  75.4 us
    pallas_call x1, Pallas kernels, reduce_all(): pl.pallas_call(lambda *refs: reduce_kernel(reps, shard_count, *refs), out...  71.1 us
    reduce_scatter x1, waiting for transfers between devices, shards(): lax.psum_scatter(back_rows, 'shard', scatter_dimension=0, tiled=True)  67.9 us
    unnamed x129, local copies, waits for them, and re-layouts  29.6 us
    dot_general x1, matrix products, experts(): jnp.einsum('td,efd->etf', dy_rows, down_w, preferred_element_type=f32)  28.4 us
  transfers between devices with their start and end apart: 5, of which 4 were waited for; matrix products, arithmetic and copies ran while one was open for 15% of the time, Pallas kernels for 9%

profile of v1, /device:TPU:0, one launch (start us, length us, event | category | flops | bytes accessed | tf_op | source)
XLA Modules:
  0.0 829.6 jit_solution(11272817480892342077)
XLA Ops:
  13.8 75.8 %shard_map.222 = bf16[4,8,32,3200]{3,2,1,0:T(8,128)(2,1)} custom-call(bf16[8,32,3200]{2,1,0:T(8,128)(2,1)} %concatenate.73.refs_0_), custom_call_target="tpu_custom_call" | custom-call | bytes 52428800 | tf_op jit(solution)/shard_map/pallas_call | solution.py:219
  92.7 4.8 fusion.27
  111.3 7.3 fusion.84
  118.7 8.3 %fusion.6 = f32[8,2,512]{2,1,0:T(2,128)S(1)} fusion(f32[8,2,512,512]{2,3,1,0:T(8,128)} %get-tuple-element.149, f32[8,2,512]{2,1,0:T(2,128)S(1)} %get-tuple-element.148), kind=kLoop, calls=%fused_computation.21 | loop fusion | flops 8380416 | bytes 16842752 | tf_op jit(solution)/shard_map/reduce_sum | solution.py:80
  127.0 7.9 fusion.53
  140.9 85.1 %all-gather.5.cloned.1.call-done = bf16[2048,1024]{0,1:T(8,128)(2,1)} async-done(((bf16[512,1024]{0,1:T(8,128)(2,1)}), bf16[2048,1024]{0,1:T(8,128)(2,1)}) %all-gather.5.cloned.1.call-update) | async-done | bytes 4194320 | tf_op jit(solution)/shard_map/all_gather | solution.py:351
  231.6 23.2 %convolution_bitcast_fusion = f32[4,2048,1024]{1,2,0:T(8,128)} fusion(bf16[4,1024,1024]{2,1,0:T(8,128)(2,1)} %param.31, bf16[2048,1024]{0,1:T(8,128)(2,1)S(1)} %copy-done.10), kind=kOutput, calls=%fused_computation.2 | convolution fusion | flops 17179869184 | bytes 46137344 | tf_op jit(solution)/shard_map/td,edf->etf/dot_general | solution.py:551
  254.8 28.4 %multiply_convert_fusion.1 = (bf16[4,2048,512]{1,2,0:T(8,128)(2,1)}, bf16[4,2048,512]{1,2,0:T(8,128)(2,1)}, f32[4,2048]{1,0:T(4,128)S(1)}, bf16[4,2048,512]{1,2,0:T(8,128)(2,1)}) fusion(f32[4,2048,1024]{1,2,0:T(8,128)} %convolution_bitcast_fusion, f32[4,2048]{1,0:T(4,128)S(1)} %dynamic-slice_bitcast_fusion, bf16[4,512,1024]{2,1,0:T(8,128)(2,1)} %param.32, ...), kind=kOutput, calls=%fused_computation.15 | convolution fusion | flops 8669618176 | bytes 67174400 | tf_op jit(solution)/shard_map/td,efd->etf/dot_general | solution.py:557
  283.2 14.1 %fusion.35 = bf16[4,512,1024]{2,1,0:T(8,128)(2,1)} fusion(bf16[2048,1152]{0,1:T(8,128)(2,1)} %all-gather.3.cloned.1.call-done, bf16[4,2048,512]{1,2,0:T(8,128)(2,1)} %get-tuple-element.129, f32[4,2048]{1,0:T(4,128)S(1)} %dynamic-slice_bitcast_fusion), kind=kOutput, calls=%fused_computation.53 | convolution fusion | flops 8604614656 | bytes 16809984 | tf_op jit(solution)/shard_map/etf,td->efd/dot_general | solution.py:468
  297.3 24.6 %convert_bitcast_fusion = bf16[4,1024,1024]{1,2,0:T(8,128)(2,1)} fusion(bf16[4,2048,512]{1,2,0:T(8,128)(2,1)} %get-tuple-element.127, bf16[4,2048,512]{1,2,0:T(8,128)(2,1)} %get-tuple-element.126, bf16[2048,1024]{0,1:T(8,128)(2,1)} %all-gather.5.cloned.1.call-done), kind=kOutput, calls=%fused_computation.28 | convolution fusion | flops 17217617920 | bytes 29360128 | tf_op jit(solution)/shard_map/td,etf->edf/dot_general | solution.py:467
  322.1 24.3 %bitcast_convert_fusion = bf16[2048,1024]{0,1:T(8,128)(2,1)S(1)} fusion(bf16[4,1024,1024]{2,1,0:T(8,128)(2,1)} %param.31, bf16[4,2048,512]{1,2,0:T(8,128)(2,1)} %get-tuple-element.127, bf16[4,2048,512]{1,2,0:T(8,128)(2,1)} %get-tuple-element.126), kind=kOutput, calls=%fused_computation.26 | convolution fusion | flops 17215520768 | bytes 29360128 | tf_op jit(solution)/shard_map/etf,edf->td/dot_general | solution.py:448
  346.4 6.3 maximum_maximum_fusion
  352.8 14.7 %bitcast_convert_fusion.1 = bf16[2048,1024]{0,1:T(8,128)(2,1)} fusion(bf16[4,512,1024]{2,1,0:T(8,128)(2,1)} %param.32, bf16[4,2048,512]{1,2,0:T(8,128)(2,1)} %get-tuple-element.129, f32[4,2048]{1,0:T(4,128)S(1)} %dynamic-slice_bitcast_fusion), kind=kOutput, calls=%fused_computation.27 | convolution fusion | flops 8604614656 | bytes 16809984 | tf_op jit(solution)/shard_map/etf,efd->td/dot_general | solution.py:444
  368.9 124.4 %all-reduce.3.cloned.1.call-done = (bf16[4,1024,1024]{1,2,0:T(8,128)(2,1)}, bf16[4,512,1024]{2,1,0:T(8,128)(2,1)}) async-done(((bf16[4,1024,1024]{1,2,0:T(8,128)(2,1)}, bf16[4,512,1024]{2,1,0:T(8,128)(2,1)}), (bf16[4,1024,1024]{1,2,0:T(8,128)(2,1)}, bf16[4,512,1024]{2,1,0:T(8,128)(2,1)})) %all-reduce.3.cloned.1.call-update) | async-done | bytes 12582928 | tf_op jit(solution)/shard_map/psum | solution.py:470
  493.3 13.0 %copy.164 = f32[4,1024,1024]{2,1,0:T(8,128)} copy(bf16[4,1024,1024]{1,2,0:T(8,128)(2,1)} %get-tuple-element.57) | data formatting | bytes 25165824
  506.2 6.8 convert_element_type.237
  513.0 67.9 %reduce-scatter.5.cloned.1.call-done = bf16[512,1152]{0,1:T(8,128)(2,1)} async-done(((bf16[2048,1152]{0,1:T(8,128)(2,1)}), bf16[512,1152]{0,1:T(8,128)(2,1)}) %reduce-scatter.5.cloned.1.call-update) | async-done | bytes 1179664 | tf_op jit(solution)/shard_map/reduce_scatter | solution.py:466
  585.1 75.4 %reduce-scatter.3.cloned.1.call-done = bf16[512,1024]{0,1:T(8,128)(2,1)} async-done(((bf16[2048,1024]{0,1:T(8,128)(2,1)}), bf16[512,1024]{0,1:T(8,128)(2,1)}) %reduce-scatter.3.cloned.1.call-update) | async-done | bytes 1048592 | tf_op jit(solution)/shard_map/reduce_scatter | solution.py:445
  668.9 15.2 %fusion.2 = (f32[8,2,512]{2,1,0:T(2,128)S(1)}, f32[8,512,512,2]{2,1,3,0:T(8,128)}) fusion(f32[8,2,512,512]{2,3,1,0:T(8,128)} %get-tuple-element.149, f32[8,2,512]{2,1,0:T(2,128)} %bitcast.155, bf16[512,8,64,1]{0,2,3,1:T(8,128)(2,1)S(1)} %bitcast.140, bf16[512,8,2,64]{0,3,2,1:T(8,128)(2,1)S(1)} %bitcast.124), kind=kOutput, calls=%fused_computation.8 | convolution fusion | flops 549445632 | bytes 35192832 | tf_op jit(solution)/shard_map/qgrd,kgd->grqk/dot_general | solution.py:97
  685.4 8.5 %fusion.4 = bf16[8,2,512,512]{2,3,1,0:T(8,128)(2,1)S(1)} fusion(f32[8,512,512,2]{2,1,3,0:T(8,128)} %get-tuple-element.156, f32[8,2,512,512]{2,3,1,0:T(8,128)S(1)} %bitcast.123, f32[8,2,512]{2,1,0:T(2,128)S(1)} %get-tuple-element.155, f32[8,2,512]{2,1,0:T(2,128)S(1)} %bitcast.157), kind=kLoop, calls=%fused_computation.10 | loop fusion | flops 16777216 | bytes 42008576 | tf_op jit(solution)/shard_map/convert_element_type | solution.py:101
  700.1 6.0 fusion.61
  721.2 5.1 fusion.45
  729.6 10.4 %concatenate.87.refs_0_ = bf16[4,8,32,3200]{3,2,1,0:T(8,128)(2,1)} concatenate(bf16[4,8,32,2048]{3,2,1,0:T(8,128)(2,1)} %bitcast.137, bf16[4,8,32,1024]{3,2,1,0:T(8,128)(2,1)S(1)} %bitcast.145, bf16[4,8,32,16]{3,2,1,0:T(8,128)(2,1)S(1)} %bitcast.146, bf16[4,8,32,1]{3,2,1,0:T(8,128)(2,1)} %convert_element_type.241, bf16[4,8,32,1]{3,2,1,0:T(8,128)(2,1)} %convert_element_type.242, ...), dimensions={3} | concatenate | bytes 13107200 | tf_op jit(solution)/shard_map/concatenate | solution.py:517
  740.0 71.1 %shard_map.223 = bf16[1,8,32,3200]{3,2,1,0:T(8,128)(2,1)} custom-call(bf16[4,8,32,3200]{3,2,1,0:T(8,128)(2,1)} %concatenate.87.refs_0_), custom_call_target="tpu_custom_call" | custom-call | bytes 104857600 | tf_op jit(solution)/shard_map/pallas_call | solution.py:334
  (207 shorter events, 86.2 us)
Async XLA Ops:
  7.2 133.6 %all-gather.3.cloned.1.call-start = ((), (), s32[]{:S(2)}) async-start(), calls=%async_computation.2 | async-start | bytes 5898240 | tf_op jit(solution)/shard_map/all_gather | solution.py:351
  8.9 80.7 %copy-start.6 = (bf16[512,1024]{0,1:T(8,128)(2,1)}, bf16[512,1024]{0,1:T(8,128)(2,1)S(1)}, u32[]{:S(2)}) copy-start(bf16[512,1024]{0,1:T(8,128)(2,1)S(1)} %copy.141) | copy-start | bytes 3145732
  11.1 214.9 %all-gather.5.cloned.1.call-start = ((), (), s32[]{:S(2)}) async-start(), calls=%async_computation.3 | async-start | bytes 5242880 | tf_op jit(solution)/shard_map/all_gather | solution.py:351
  13.8 78.0 %copy-start.23 = (bf16[512,1024]{1,0:T(8,128)(2,1)S(1)}, bf16[512,1024]{1,0:T(8,128)(2,1)}, u32[]{:S(2)}) copy-start(bf16[512,1024]{1,0:T(8,128)(2,1)} %param.21) | copy-start | bytes 3145732
  92.4 42.6 %copy-start.4 = (bf16[512,1024]{0,1:T(8,128)(2,1)}, bf16[512,1024]{0,1:T(8,128)(2,1)S(1)}, u32[]{:S(2)}) copy-start(bf16[512,1024]{0,1:T(8,128)(2,1)S(1)} %copy.130) | copy-start | bytes 3145732
  108.8 29.5 %copy-start.41 = (f32[1024,1]{0,1:T(1,128)}, f32[1024,1]{0,1:T(1,128)S(1)}, u32[]{:S(2)}) copy-start(f32[1024,1]{0,1:T(1,128)S(1)} %copy.193) | copy-start | bytes 12292
  118.6 8.4 %copy-start.36 = (f32[8,2,512]{2,1,0:T(2,128)}, f32[8,2,512]{2,1,0:T(2,128)S(1)}, u32[]{:S(2)}) copy-start(f32[8,2,512]{2,1,0:T(2,128)S(1)} %get-tuple-element.148) | copy-start | bytes 98308
  118.7 8.4 %copy-start.12 = (bf16[512,512]{0,1:T(8,128)(2,1)S(1)}, bf16[512,512]{0,1:T(8,128)(2,1)}, u32[]{:S(2)}) copy-start(bf16[512,512]{0,1:T(8,128)(2,1)} %copy.135) | copy-start | bytes 1572868
  140.9 352.4 %all-reduce.3.cloned.1.call-start = ((), (), s32[]{:S(2)}) async-start(), calls=%async_computation.6 | async-start | bytes 25165824 | tf_op jit(solution)/shard_map/psum | solution.py:470
  321.9 259.0 %reduce-scatter.5.cloned.1.call-start = ((), (), s32[]{:S(2)}) async-start(), calls=%async_computation.5 | async-start | bytes 5898240 | tf_op jit(solution)/shard_map/reduce_scatter | solution.py:466
  352.7 307.8 %reduce-scatter.3.cloned.1.call-start = ((), (), s32[]{:S(2)}) async-start(), calls=%async_computation.4 | async-start | bytes 5242880 | tf_op jit(solution)/shard_map/reduce_scatter | solution.py:445
  506.2 75.5 %copy-start.33 = (f32[2048,16]{0,1:T(8,128)S(1)}, f32[2048,16]{0,1:T(8,128)}, u32[]{:S(2)}) copy-start(f32[2048,16]{0,1:T(8,128)} %copy-done.32) | copy-start | bytes 393220
  506.2 75.5 %copy-start.2 = (f32[512,1024]{0,1:T(8,128)S(1)}, f32[512,1024]{0,1:T(8,128)}, u32[]{:S(2)}) copy-start(f32[512,1024]{0,1:T(8,128)} %copy-done.1) | copy-start | bytes 6291460
  506.2 75.5 %copy-start.42 = (f32[1024,1]{0,1:T(1,128)S(1)}, f32[1024,1]{0,1:T(1,128)}, u32[]{:S(2)}) copy-start(f32[1024,1]{0,1:T(1,128)} %copy-done.41) | copy-start | bytes 12292
  506.2 75.5 %copy-start.45 = (f32[512]{0:T(512)S(1)}, f32[512]{0:T(512)}, u32[]{:S(2)}) copy-start(f32[512]{0:T(512)} %copy-done.44) | copy-start | bytes 6148
  513.0 147.5 %copy-start.7 = (bf16[512,1024]{0,1:T(8,128)(2,1)S(1)}, bf16[512,1024]{0,1:T(8,128)(2,1)}, u32[]{:S(2)}) copy-start(bf16[512,1024]{0,1:T(8,128)(2,1)} %copy-done.6) | copy-start | bytes 3145732
  668.9 15.3 %slice-start = ((s8[16777216]{0:T(1024)(128)(4,1)}), s8[4194304]{0:T(1024)(128)(4,1)S(1)}, s32[]{:S(2)}) async-start(s8[16777216]{0:T(1024)(128)(4,1)} %bitcast.122), calls=%async_computation.7 | async-start | bytes 8388608
  668.9 15.3 %slice-start.1 = ((s8[16777216]{0:T(1024)(128)(4,1)}), s8[4194304]{0:T(1024)(128)(4,1)S(1)}, s32[]{:S(2)}) async-start(s8[16777216]{0:T(1024)(128)(4,1)} %bitcast.122), calls=%async_computation.8 | async-start | bytes 8388608
  668.9 15.3 %slice-start.2 = ((s8[16777216]{0:T(1024)(128)(4,1)}), s8[4194304]{0:T(1024)(128)(4,1)S(1)}, s32[]{:S(2)}) async-start(s8[16777216]{0:T(1024)(128)(4,1)} %bitcast.122), calls=%async_computation.9 | async-start | bytes 8388608
  668.9 16.4 %slice-start.3 = ((s8[16777216]{0:T(1024)(128)(4,1)}), s8[4194304]{0:T(1024)(128)(4,1)S(1)}, s32[]{:S(2)}) async-start(s8[16777216]{0:T(1024)(128)(4,1)} %bitcast.122), calls=%async_computation.10 | async-start | bytes 8388608
  668.9 16.4 %copy-start.31 = (f32[2,8,512]{2,1,0:T(8,128)S(1)}, f32[2,8,512]{2,1,0:T(8,128)}, u32[]{:S(2)}) copy-start(f32[2,8,512]{2,1,0:T(8,128)} %log_add_fusion) | copy-start | bytes 98308
  685.3 11.8 %copy-start.25 = (bf16[512,8,32]{0,2,1:T(8,128)(2,1)S(1)}, bf16[512,8,32]{0,2,1:T(8,128)(2,1)}, u32[]{:S(2)}) copy-start(bf16[512,8,32]{0,2,1:T(8,128)(2,1)} %copy-done.24) | copy-start | bytes 786436
  685.3 11.8 %copy-start.27 = (bf16[512,8,32]{0,2,1:T(8,128)(2,1)S(1)}, bf16[512,8,32]{0,2,1:T(8,128)(2,1)}, u32[]{:S(2)}) copy-start(bf16[512,8,32]{0,2,1:T(8,128)(2,1)} %copy-done.26) | copy-start | bytes 786436
  721.2 8.3 %copy-start.18 = (bf16[1024,1024]{1,0:T(8,128)(2,1)S(1)}, bf16[1024,1024]{1,0:T(8,128)(2,1)}, u32[]{:S(2)}) copy-start(bf16[1024,1024]{1,0:T(8,128)(2,1)} %convolution_convert_fusion.1) | copy-start | bytes 6291460
  (41 other events, 168.6 us)
Sparse Core Ops, SparseCore 0:
  11.3 104.1 all-gather.2
  141.0 84.9 all-gather.4
  322.0 171.1 all-reduce.2
  495.5 85.3 reduce-scatter.4
  583.2 77.2 reduce-scatter.2

commit v2 on v1

v2 whole, which is shorter than its diff:
```python
import jax
import jax.numpy as jnp
from jax import lax
from jax.experimental import pallas as pl
from jax.experimental.pallas import tpu as pltpu
from jax.sharding import PartitionSpec as P

HEADS = 16
KV_HEADS = 8
HEAD_DIM = 64
EXPERTS = 16
PAD = 128
VMEM_BYTES = 54 * 2**20


epsilon = 1e-06
rope_base = 10000.0
masked_score = -1e30


def positions(doc_rows):
    row_count = doc_rows.shape[0]
    places = jnp.arange(row_count, dtype=jnp.int32)
    begins = jnp.sum((doc_rows[None, :] < doc_rows[:, None]).astype(jnp.int32), axis=1)
    return places - begins


def rotary_tables(places, head_width):
    half_width = head_width // 2
    frequencies = jnp.power(
        rope_base, -2.0 * jnp.arange(half_width, dtype=jnp.float32) / head_width
    )
    angles = places.astype(jnp.float32)[:, None] * frequencies[None, :]
    return (jnp.cos(angles)[:, None, :], jnp.sin(angles)[:, None, :])


MESH = pl.DeviceIdType.MESH
HALVES = 2


def bit_orders(reps):
    bits = reps.bit_length() - 1
    first = list(range(bits))
    return (first, first[:1] + first[1:][::-1])


def rep_place(rep_at, order):
    place = 0
    for bit in order:
        place = place * 2 + rep_at // 2**bit % 2
    return place


def partner(rep_at, bit):
    return rep_at + 2**bit * (1 - 2 * (rep_at // 2**bit % 2))


def halves_of(columns):
    tiles = columns // 128
    left = (tiles + 1) // 2 * 128
    return (pl.ds(0, left), pl.ds(left, columns - left))


def meet(rep_at, shard_at, reps, shard_count):
    barrier = pltpu.get_barrier_semaphore()
    bits = reps.bit_length() - 1
    for bit in range(bits):
        pl.semaphore_signal(
            barrier, inc=1, device_id=(partner(rep_at, bit), shard_at), device_id_type=MESH
        )
    for step in range(1, shard_count):
        pl.semaphore_signal(
            barrier,
            inc=1,
            device_id=(rep_at, (shard_at + step) % shard_count),
            device_id_type=MESH,
        )
    pl.semaphore_wait(barrier, bits + shard_count - 1)


def spread(out, orders, columns, rep_at, shard_at, sends, recvs):
    bits = len(orders[0])
    flying = [None] * HALVES
    for at in reversed(range(bits)):
        window = 2 ** (bits - 1 - at)
        for half in range(HALVES):
            order = orders[half]
            place = rep_place(rep_at, order)
            begin = place // window * window
            if flying[half] is not None:
                flying[half].wait()
            block = out.at[:, pl.ds(begin, window), :, columns[half]]
            flying[half] = pltpu.make_async_remote_copy(
                src_ref=block,
                dst_ref=block,
                send_sem=sends.at[half, at],
                recv_sem=recvs.at[half, at],
                device_id=(partner(rep_at, order[at]), shard_at),
                device_id_type=MESH,
            )
            flying[half].start()
    for half in range(HALVES):
        flying[half].wait()


def gather_kernel(reps, shard_count, piece, out, z_send, z_recv, sends, recvs):
    rep_at, shard_at = (lax.axis_index("rep"), lax.axis_index("shard"))
    orders = bit_orders(reps)
    columns = halves_of(piece.shape[-1])
    meet(rep_at, shard_at, reps, shard_count)
    flying = []
    for half in range(HALVES):
        place = rep_place(rep_at, orders[half])
        for step in range(1, shard_count):
            copy = pltpu.make_async_remote_copy(
                src_ref=piece.at[place, :, columns[half]],
                dst_ref=out.at[shard_at, place, :, columns[half]],
                send_sem=z_send.at[half, step - 1],
                recv_sem=z_recv.at[half, step - 1],
                device_id=(rep_at, (shard_at + step) % shard_count),
                device_id_type=MESH,
            )
            copy.start()
            flying.append(copy)
        out[shard_at, place, :, columns[half]] = piece[place, :, columns[half]]
    for copy in flying:
        copy.wait()
    spread(out, orders, columns, rep_at, shard_at, sends, recvs)


def gather_all(piece, reps, shard_count, number):
    own, width = piece.shape
    rows = own // reps
    bits = reps.bit_length() - 1
    out = pl.pallas_call(
        lambda *refs: gather_kernel(reps, shard_count, *refs),
        out_shape=jax.ShapeDtypeStruct((shard_count, reps, rows, width), piece.dtype),
        in_specs=[pl.BlockSpec(memory_space=pltpu.VMEM)],
        out_specs=pl.BlockSpec(memory_space=pltpu.VMEM),
        scratch_shapes=[
            pltpu.SemaphoreType.DMA((HALVES, shard_count)),
            pltpu.SemaphoreType.DMA((HALVES, shard_count)),
            pltpu.SemaphoreType.DMA((HALVES, bits)),
            pltpu.SemaphoreType.DMA((HALVES, bits)),
        ],
        compiler_params=pltpu.CompilerParams(
            collective_id=number, has_side_effects=True, vmem_limit_bytes=VMEM_BYTES
        ),
        cost_estimate=pl.CostEstimate(
            flops=0, bytes_accessed=shard_count * own * width, transcendentals=0
        ),
    )(piece.reshape(reps, rows, width))
    return out.reshape(shard_count * own, width)


def reduce_kernel(reps, shard_count, parts, out, *scratch):
    bits = reps.bit_length() - 1
    f32 = jnp.float32
    landed = [scratch[half * bits : (half + 1) * bits] for half in range(HALVES)]
    rest = scratch[HALVES * bits :]
    if shard_count > 1:
        z_land, (z_send, z_recv) = (rest[:HALVES], rest[HALVES : HALVES + 2])
        rest = rest[HALVES + 2 :]
    r_send, r_recv, sends, recvs = rest
    rep_at, shard_at = (lax.axis_index("rep"), lax.axis_index("shard"))
    orders = bit_orders(reps)
    columns = halves_of(parts.shape[-1])
    meet(rep_at, shard_at, reps, shard_count)
    flying = [None] * HALVES

    def source(half, at):
        return parts.at[:, :, :, columns[half]] if at == 0 else landed[half][at - 1]

    def begin(half, at):
        bit = orders[half][at]
        many = reps // 2 ** (at + 1)
        away = (1 - rep_at // 2**bit % 2) * many
        flying[half] = pltpu.make_async_remote_copy(
            src_ref=source(half, at).at[:, pl.ds(away, many)],
            dst_ref=landed[half][at],
            send_sem=r_send.at[half, at],
            recv_sem=r_recv.at[half, at],
            device_id=(partner(rep_at, bit), shard_at),
            device_id_type=MESH,
        )
        flying[half].start()

    for half in range(HALVES):
        begin(half, 0)
    for at in range(bits):
        many = reps // 2 ** (at + 1)
        for half in range(HALVES):
            flying[half].wait()
            keep = rep_at // 2 ** orders[half][at] % 2 * many
            mine, came = (source(half, at), landed[half][at])

            @pl.loop(0, parts.shape[0] * many)
            def _(index):
                outer, inner = (index // many, index % many)
                came[outer, inner] = (
                    came[outer, inner].astype(f32) + mine[outer, keep + inner].astype(f32)
                ).astype(came.dtype)

            if at + 1 < bits:
                begin(half, at + 1)
    copies = []
    if shard_count > 1:
        for half in range(HALVES):
            for step in range(1, shard_count):
                to = (shard_at + step) % shard_count
                copy = pltpu.make_async_remote_copy(
                    src_ref=landed[half][-1].at[to, 0],
                    dst_ref=z_land[half].at[step - 1],
                    send_sem=z_send.at[half, step - 1],
                    recv_sem=z_recv.at[half, step - 1],
                    device_id=(rep_at, to),
                    device_id_type=MESH,
                )
                copy.start()
                copies.append(copy)
    for copy in copies:
        copy.wait()
    for half in range(HALVES):
        place = rep_place(rep_at, orders[half])
        if shard_count > 1:
            total = landed[half][-1][shard_at, 0].astype(f32)
            for step in range(1, shard_count):
                total = total + z_land[half][step - 1].astype(f32)
            out[0, place, :, columns[half]] = total.astype(out.dtype)
        else:
            out[0, place, :, columns[half]] = landed[half][-1][0, 0]
    spread(out, orders, columns, rep_at, shard_at, sends, recvs)


def reduce_all(parts, reps, shard_count, number):
    total, width = parts.shape
    rows = total // (reps * shard_count)
    bits = reps.bit_length() - 1
    widths = (halves_of(width)[0].size, halves_of(width)[1].size)
    scratch = []
    for wide in widths:
        for at in range(bits):
            scratch.append(
                pltpu.VMEM((shard_count, reps // 2 ** (at + 1), rows, wide), parts.dtype)
            )
    if shard_count > 1:
        scratch += [pltpu.VMEM((shard_count - 1, rows, wide), parts.dtype) for wide in widths]
        scratch += [pltpu.SemaphoreType.DMA((HALVES, shard_count)) for _ in range(2)]
    scratch += [pltpu.SemaphoreType.DMA((HALVES, bits)) for _ in range(4)]
    out = pl.pallas_call(
        lambda *refs: reduce_kernel(reps, shard_count, *refs),
        out_shape=jax.ShapeDtypeStruct((1, reps, rows, width), parts.dtype),
        in_specs=[pl.BlockSpec(memory_space=pltpu.VMEM)],
        out_specs=pl.BlockSpec(memory_space=pltpu.VMEM),
        scratch_shapes=scratch,
        compiler_params=pltpu.CompilerParams(
            collective_id=number, has_side_effects=True, vmem_limit_bytes=VMEM_BYTES
        ),
        cost_estimate=pl.CostEstimate(
            flops=0, bytes_accessed=total * width, transcendentals=0
        ),
    )(parts.reshape(shard_count, reps, rows, width))
    return out.reshape(reps * rows, width)


F32, BF16 = jnp.float32, jnp.bfloat16
LANES = 128
TILE = 256
LIGHT = pl.CostEstimate(flops=10**6, bytes_accessed=10**5, transcendentals=0)
GROUP = HEADS // KV_HEADS


def dot(a, b):
    return lax.dot_general(a, b, (((1,), (0,)), ((), ())), preferred_element_type=F32)


def dot_nt(a, b):
    return lax.dot_general(a, b, (((1,), (1,)), ((), ())), preferred_element_type=F32)


def lane_of(shape):
    return lax.broadcasted_iota(jnp.int32, shape, len(shape) - 1)


def swap_halves(values):
    near = lane_of(values.shape) % HEAD_DIM < HEAD_DIM // 2
    up = pltpu.roll(values, LANES - HEAD_DIM // 2, 1)
    down = pltpu.roll(values, HEAD_DIM // 2, 1)
    return jnp.where(near, up, down)


def rope_block(values, ct, st):
    return values * ct + swap_halves(values) * st


def unrope_block(values, ct, st):
    return values * ct - swap_halves(values) * st


def low_high(block, side):
    lane = lane_of(block.shape)
    wide = block.astype(F32)
    kept = jnp.where((lane < HEAD_DIM) if side == 0 else (lane >= HEAD_DIM), wide, 0.0)
    moved = pltpu.roll(kept, HEAD_DIM, 1)
    pair = (kept, moved) if side == 0 else (moved, kept)
    return [item.astype(BF16) for item in pair]


def fill_bias(bias, doc_col, doc_row):
    rows = bias.shape[0]
    keys = lax.broadcasted_iota(jnp.int32, (TILE, rows), 0)
    queries = lax.broadcasted_iota(jnp.int32, (TILE, rows), 1)
    for start in range(0, rows, TILE):
        allowed = (doc_col[start : start + TILE, :] == doc_row[...]) & (keys + start <= queries)
        bias[start : start + TILE, :] = jnp.where(allowed, 0.0, masked_score)


def tile_at(index, width=TILE):
    return pl.ds(pl.multiple_of(index * width, width), width)


def gate_softmax(second, small, mask):
    logits = dot(second, small)
    chosen = jnp.where(mask, logits, masked_score)
    gate_exp = jnp.where(mask, jnp.exp(chosen - jnp.max(chosen, axis=1, keepdims=True)), 0.0)
    return gate_exp / jnp.sum(gate_exp, axis=1, keepdims=True)


def forward_kernel(
    tokens, w, ct, st, doc_col, doc_row,
    second, middle, first_t, q8, keys, values, att_t, lse,
    first, att, bias,
):
    rows, width = tokens.shape
    q_cols, kv_cols = q8.shape[1], keys.shape[1]
    small_at = w.shape[1] - PAD
    gains = w[:, small_at:].astype(F32).T
    gain_in, gain_mid = gains[EXPERTS : EXPERTS + 1], gains[EXPERTS + 1 : EXPERTS + 2]
    for at in range(0, rows, LANES):
        x = tokens[at : at + LANES, :].astype(F32)
        scale = lax.rsqrt(jnp.mean(x * x, axis=-1, keepdims=True) + epsilon)
        low = (x * scale * gain_in).astype(BF16)
        first[at : at + LANES, :] = low
        first_t[:, at : at + LANES] = low.T

    def project(index):
        return dot(first[...], w[:, tile_at(index)])

    def roped(index):
        part = project(index)
        return jnp.concatenate(
            [
                rope_block(part[:, at : at + LANES], ct[...], st[...])
                for at in range(0, TILE, LANES)
            ],
            axis=1,
        )

    @pl.loop(0, q_cols // TILE)
    def _(j):
        q8[:, tile_at(j)] = (roped(j) * HEAD_DIM**-0.5).astype(BF16)

    @pl.loop(0, kv_cols // TILE)
    def _(j):
        keys[:, tile_at(j)] = roped(q_cols // TILE + j).astype(BF16)

    @pl.loop(0, kv_cols // TILE)
    def _(j):
        values[:, tile_at(j)] = project((q_cols + kv_cols) // TILE + j).astype(BF16)

    fill_bias(bias, doc_col, doc_row)

    @pl.loop(0, kv_cols // LANES)
    def _(pair):
        k128, v128 = keys[:, tile_at(pair, LANES)], values[:, tile_at(pair, LANES)]
        v_t = v128.astype(F32).T.astype(BF16)
        for side in range(2):
            low_k = low_high(k128, side)
            q = q8[:, tile_at(pair * 2 + side, LANES)]
            v_s = v_t[side * HEAD_DIM : (side + 1) * HEAD_DIM]
            for h in range(GROUP):
                head = pair * 2 * GROUP + side * GROUP + h
                for begin in range(0, rows, TILE):
                    kr = begin + TILE
                    s = dot_nt(low_k[h][:kr], q[begin:kr]) + bias[:kr, begin:kr]
                    top = jnp.max(s, axis=0, keepdims=True)
                    p = jnp.exp(s - top)
                    total = jnp.sum(p, axis=0, keepdims=True)
                    probs = (p * (1.0 / total)).astype(BF16)
                    lse[head, :, begin:kr] = top + jnp.log(total)
                    att_t[tile_at(head, HEAD_DIM), begin:kr] = dot(v_s[:, :kr], probs).astype(BF16)

    @pl.loop(0, width // TILE)
    def _(j):
        att[:, tile_at(j)] = att_t[tile_at(j), :].astype(F32).T.astype(BF16)

    @pl.loop(0, width // TILE)
    def _(j):
        out_w = w[:, pl.ds(pl.multiple_of(q_cols + 2 * kv_cols + j * TILE, TILE), TILE)]
        middle[:, tile_at(j)] = tokens[:, tile_at(j)].astype(F32) + dot(att[...], out_w)

    for at in range(0, rows, LANES):
        x = middle[at : at + LANES, :]
        scale = lax.rsqrt(jnp.mean(x * x, axis=-1, keepdims=True) + epsilon)
        second[at : at + LANES, :] = (x * scale * gain_mid).astype(BF16)


def split_kernel(joint, *outs):
    begin = 0
    for out in outs:
        out[...] = joint[:, begin : begin + out.shape[1]].astype(F32)
        begin += out.shape[1]


def shape_of(shape, kind):
    return jax.ShapeDtypeStruct(shape, kind)


def local_call(kernel, outs, scratch, *args):
    return pl.pallas_call(
        kernel,
        out_shape=outs,
        in_specs=[pl.BlockSpec(memory_space=pltpu.VMEM)] * len(args),
        out_specs=[pl.BlockSpec(memory_space=pltpu.VMEM)] * len(outs),
        scratch_shapes=scratch,
        compiler_params=pltpu.CompilerParams(vmem_limit_bytes=VMEM_BYTES),
        cost_estimate=LIGHT,
    )(*args)


def forward_block(tokens, w, ct, st, doc_ids, q_cols, kv_cols):
    rows, width = tokens.shape
    outs = [
        shape_of((rows, width), BF16),
        shape_of((rows, width), F32),
        shape_of((width, rows), BF16),
        shape_of((rows, q_cols), BF16),
        shape_of((rows, kv_cols), BF16),
        shape_of((rows, kv_cols), BF16),
        shape_of((q_cols, rows), BF16),
        shape_of((HEADS, 1, rows), F32),
    ]
    scratch = [
        pltpu.VMEM((rows, width), BF16),
        pltpu.VMEM((rows, q_cols), BF16),
        pltpu.VMEM((rows, rows), F32),
    ]
    return local_call(
        forward_kernel, outs, scratch, tokens, w, ct, st, doc_ids[:, None], doc_ids[None, :]
    )


def backward_kernel(
    tokens, side, middle, second, back_own, back_left, back_right, w, ct, st, doc_col, doc_row,
    first_t, q8, keys, values, att_t, lse,
    joint, grad_tokens,
    bias, grad_middle, grad_branch, grad_att, grad_pre, grad_first, dq_t, dk, dv, rows_t,
):
    rows, width = tokens.shape
    q_cols, kv_cols = q8.shape[1], keys.shape[1]
    qkv_cols = q_cols + 2 * kv_cols
    small_at = w.shape[1] - PAD
    small = w[:, small_at:]
    gains = small.astype(F32).T
    gain_in, gain_mid = gains[EXPERTS : EXPERTS + 1], gains[EXPERTS + 1 : EXPERTS + 2]
    tall = back_own.shape[1]
    gain_sum = jnp.zeros((1, width), F32)
    router_t = jnp.zeros((PAD, width), F32)
    for at in range(0, rows, LANES):
        here = slice(at, at + LANES)
        mask = side[here, width:] > 0
        gates = gate_softmax(second[here, :], small, mask)
        came = (
            back_own[here, width:].astype(F32)
            + back_left[here, width:].astype(F32)
            + back_right[here, width:].astype(F32)
        )
        gate_back = jnp.where(
            lane_of(came.shape) < EXPERTS, came + pltpu.roll(came, tall - width - EXPERTS, 1), 0.0
        )
        grad_logits = gates * (gate_back - jnp.sum(gates * gate_back, axis=1, keepdims=True))
        low_logits = grad_logits.astype(BF16)
        router_t += dot(grad_logits.T.astype(BF16), second[here, :])
        grad_second = (
            back_own[here, :width].astype(F32)
            + back_left[here, :width].astype(F32)
            + back_right[here, :width].astype(F32)
            + dot_nt(low_logits, small)
        )
        x = middle[here, :]
        scale = lax.rsqrt(jnp.mean(x * x, axis=-1, keepdims=True) + epsilon)
        normed = x * scale
        gain_sum += jnp.sum(grad_second * normed, axis=0, keepdims=True)
        u = grad_second * gain_mid
        inner = jnp.mean(u * normed, axis=-1, keepdims=True)
        total = side[here, :width].astype(F32) + scale * (u - normed * inner)
        grad_middle[here, :] = total
        grad_branch[here, :] = total.astype(BF16)
    rows_t[...] = router_t
    rows_t[EXPERTS + 1 : EXPERTS + 2, :] = gain_sum

    @pl.loop(0, width // TILE)
    def _(j):
        joint[:, pl.ds(pl.multiple_of(qkv_cols + j * TILE, TILE), TILE)] = dot(
            att_t[...], grad_branch[:, tile_at(j)]
        ).astype(BF16)
        out_rows = w[tile_at(j), pl.ds(qkv_cols, width)]
        grad_att[:, tile_at(j)] = dot_nt(grad_branch[...], out_rows).astype(BF16)

    fill_bias(bias, doc_col, doc_row)

    @pl.loop(0, kv_cols // LANES)
    def _(pair):
        k128, v128 = keys[:, tile_at(pair, LANES)], values[:, tile_at(pair, LANES)]
        k_t = k128.astype(F32).T.astype(BF16)
        sums = []
        for side_at in range(2):
            low_k, low_v = low_high(k128, side_at), low_high(v128, side_at)
            q = q8[:, tile_at(pair * 2 + side_at, LANES)]
            grad_o = grad_att[:, tile_at(pair * 2 + side_at, LANES)]
            k_s = k_t[side_at * HEAD_DIM : (side_at + 1) * HEAD_DIM]
            for h in range(GROUP):
                head = pair * 2 * GROUP + side_at * GROUP + h
                for begin in reversed(range(0, rows, TILE)):
                    kr = begin + TILE
                    s = dot_nt(low_k[h][:kr], q[begin:kr]) + bias[:kr, begin:kr]
                    p = jnp.exp(s - lse[head, :, begin:kr])
                    dp = dot_nt(low_v[h][:kr], grad_o[begin:kr])
                    inner = jnp.sum(p * dp, axis=0, keepdims=True)
                    ds = (p * (dp - inner)).astype(BF16)
                    dq_t[h * HEAD_DIM : (h + 1) * HEAD_DIM, begin:kr] = dot(k_s[:, :kr], ds)
                    more_k, more_v = dot(ds, q[begin:kr]), dot(p.astype(BF16), grad_o[begin:kr])
                    if kr == rows:
                        dk[h, :, :], dv[h, :, :] = more_k, more_v
                    else:
                        dk[h, :kr, :] += more_k
                        dv[h, :kr, :] += more_v
            grad_q = unrope_block(dq_t[...].T * HEAD_DIM**-0.5, ct[...], st[...])
            grad_pre[:, tile_at(pair * 2 + side_at, LANES)] = grad_q.astype(BF16)
            left = lane_of((rows, LANES)) < HEAD_DIM
            mixed_k = jnp.where(left, dk[0], dk[1])
            mixed_v = jnp.where(left, dv[0], dv[1])
            sums.append(
                (mixed_k + pltpu.roll(mixed_k, HEAD_DIM, 1), mixed_v + pltpu.roll(mixed_v, HEAD_DIM, 1))
            )
        left = lane_of((rows, LANES)) < HEAD_DIM
        grad_k = unrope_block(jnp.where(left, sums[0][0], sums[1][0]), ct[...], st[...])
        grad_v = jnp.where(left, sums[0][1], sums[1][1])
        k_at = pl.multiple_of(q_cols + pair * LANES, LANES)
        v_at = pl.multiple_of(q_cols + kv_cols + pair * LANES, LANES)
        grad_pre[:, pl.ds(k_at, LANES)] = grad_k.astype(BF16)
        grad_pre[:, pl.ds(v_at, LANES)] = grad_v.astype(BF16)

    @pl.loop(0, qkv_cols // TILE)
    def _(j):
        joint[:, tile_at(j)] = dot(first_t[...], grad_pre[:, tile_at(j)]).astype(BF16)

    @pl.loop(0, width // TILE)
    def _(j):
        grad_first[:, tile_at(j)] = dot_nt(grad_pre[...], w[tile_at(j), pl.ds(0, qkv_cols)])

    gain_sum = jnp.zeros((1, width), F32)
    for at in range(0, rows, LANES):
        here = slice(at, at + LANES)
        x = tokens[here, :].astype(F32)
        scale = lax.rsqrt(jnp.mean(x * x, axis=-1, keepdims=True) + epsilon)
        normed = x * scale
        columns = grad_first[here, :]
        gain_sum += jnp.sum(columns * normed, axis=0, keepdims=True)
        u = columns * gain_in
        inner = jnp.mean(u * normed, axis=-1, keepdims=True)
        grad_tokens[here, :] = grad_middle[here, :] + scale * (u - normed * inner)
    rows_t[EXPERTS : EXPERTS + 1, :] = gain_sum
    joint[:, pl.ds(small_at, PAD)] = rows_t[...].T.astype(BF16)


def backward_block(tokens, side, middle, second, backs, w, ct, st, doc_ids, kept):
    rows, width = tokens.shape
    q_cols, kv_cols = kept[1].shape[1], kept[2].shape[1]
    outs = [shape_of((width, w.shape[1]), BF16), shape_of((rows, width), F32)]
    scratch = [
        pltpu.VMEM((rows, rows), F32),
        pltpu.VMEM((rows, width), F32),
        pltpu.VMEM((rows, width), BF16),
        pltpu.VMEM((rows, q_cols), BF16),
        pltpu.VMEM((rows, q_cols + 2 * kv_cols), BF16),
        pltpu.VMEM((rows, width), F32),
        pltpu.VMEM((LANES, rows), F32),
        pltpu.VMEM((GROUP, rows, LANES), F32),
        pltpu.VMEM((GROUP, rows, LANES), F32),
        pltpu.VMEM((PAD, width), F32),
    ]
    return local_call(
        backward_kernel, outs, scratch,
        tokens, side, middle, second, *backs, w, ct, st, doc_ids[:, None], doc_ids[None, :], *kept,
    )


def expert_kernel(
    aliased, first_expert, second, side, small, in_w, down_w, *refs
):
    gated, grad_both, comb, back, gates, grad_gates, comb_sum, back_sum = refs[2 * aliased :]
    rows, width = second.shape
    ff = down_w.shape[1]
    at = pl.program_id(0)
    lane = lane_of((rows, PAD))

    @pl.when(at == 0)
    def _():
        gates[...] = gate_softmax(second[...], small[...], side[:, width:] > 0)
        grad_gates[...] = jnp.zeros_like(grad_gates)
        comb_sum[...] = jnp.zeros_like(comb_sum)
        back_sum[...] = jnp.zeros_like(back_sum)

    mine = lane == first_expert[0] + at
    gate = jnp.sum(jnp.where(mine, gates[...], 0.0), axis=1, keepdims=True)
    grad_col = jnp.zeros((rows, 1), F32)
    for start in range(0, ff, TILE):
        tile = slice(start, start + TILE)
        up_tile = slice(ff + start, ff + start + TILE)
        gate_part = dot(second[...], in_w[0, :, tile])
        up_part = dot(second[...], in_w[0, :, up_tile])
        came = dot_nt(side[:, :width], down_w[0, tile, :])
        sigmoid_gate = 0.5 * jnp.tanh(0.5 * gate_part) + 0.5
        silu_gate = gate_part * sigmoid_gate
        hidden = (silu_gate * up_part).astype(BF16).astype(F32)
        grad_col += jnp.sum(hidden * came, axis=1, keepdims=True)
        gated[0, 0, :, tile] = (hidden * gate).astype(BF16)
        grad_hidden = came * gate
        slope = sigmoid_gate + silu_gate * (1.0 - sigmoid_gate)
        grad_both[0, 0, :, tile] = (grad_hidden * up_part * slope).astype(BF16)
        grad_both[0, 0, :, up_tile] = (grad_hidden * silu_gate).astype(BF16)
    grad_gates[...] += jnp.where(mine, grad_col, 0.0)
    for start in range(0, width, TILE):
        tile = slice(start, start + TILE)
        comb_sum[:, tile] += dot(gated[0, 0], down_w[0, :, tile])
        back_sum[:, tile] += dot_nt(grad_both[0, 0], in_w[0, tile, :])

    @pl.when(at == pl.num_programs(0) - 1)
    def _():
        comb[...] = comb_sum[...].astype(BF16)
        back[:, :width] = back_sum[...].astype(BF16)
        high = grad_gates[...].astype(BF16).astype(F32)
        back[:, width:] = (high + pltpu.roll(grad_gates[...] - high, EXPERTS, 1)).astype(BF16)


def expert_block(first_expert, second, side, small, in_w, down_w, place, count, before):
    rows, width = second.shape
    experts, ff = down_w.shape[:2]
    whole = lambda *shape: pl.BlockSpec(shape, lambda e: (0,) * len(shape))
    in_specs = [
        pl.BlockSpec(memory_space=pltpu.SMEM),
        whole(rows, width),
        whole(*side.shape),
        whole(*small.shape),
        pl.BlockSpec((1, width, 2 * ff), lambda e: (e, 0, 0)),
        pl.BlockSpec((1, ff, width), lambda e: (e, 0, 0)),
    ] + [pl.BlockSpec(memory_space=pl.ANY)] * len(before)
    out_specs = [
        pl.BlockSpec((1, 1, rows, ff), lambda e: (e, place, 0, 0)),
        pl.BlockSpec((1, 1, rows, 2 * ff), lambda e: (e, place, 0, 0)),
        whole(rows, width),
        whole(*side.shape),
    ]
    outs = [
        shape_of((experts, count, rows, ff), BF16),
        shape_of((experts, count, rows, 2 * ff), BF16),
        shape_of((rows, width), BF16),
        shape_of(side.shape, BF16),
    ]
    return pl.pallas_call(
        lambda *refs: expert_kernel(bool(before), *refs),
        grid=(experts,),
        out_shape=outs,
        in_specs=in_specs,
        out_specs=out_specs,
        scratch_shapes=[
            pltpu.VMEM((rows, PAD), F32),
            pltpu.VMEM((rows, PAD), F32),
            pltpu.VMEM((rows, width), F32),
            pltpu.VMEM((rows, width), F32),
        ],
        input_output_aliases={6: 0, 7: 1} if before else {},
        compiler_params=pltpu.CompilerParams(
            vmem_limit_bytes=VMEM_BYTES, dimension_semantics=("arbitrary",)
        ),
        cost_estimate=LIGHT,
    )(first_expert, second, side, small, in_w, down_w, *before)


def shift(block, count, step):
    return lax.ppermute(block, "shard", [(at, (at + step) % count) for at in range(count)])


def tie(*values):
    return lax.optimization_barrier(values)


def gather_near(piece, count):
    got = {0: piece}
    right = left = piece
    for step in range(1, (count - 1) // 2 + 1):
        right, left = shift(right, count, 1), shift(left, count, -1)
        got[step], got[count - step] = right, left
    return got, right, left


def gather_far(right, left, count):
    half = right.shape[0] // 2
    return shift(right[:half], count, 1), shift(left[half:], count, -1)


def far_first(parts, count):
    half = parts[0].shape[0] // 2
    far = parts[count // 2]
    return shift(far[:half], count, -1), shift(far[half:], count, 1)


def near_rest(parts, left, right, count):
    half = parts[0].shape[0] // 2
    if count == 2:
        return jnp.concatenate([left, right], axis=0), jnp.zeros_like(parts[0])
    for step in reversed(range(1, count // 2)):
        near, far = parts[step], parts[count - step]
        if step == count // 2 - 1:
            left = jnp.concatenate([add_low(near[:half], left), near[half:]], axis=0)
            right = jnp.concatenate([far[:half], add_low(far[half:], right)], axis=0)
        else:
            left, right = add_low(near, left), add_low(far, right)
        left, right = shift(left, count, -1), shift(right, count, 1)
    return left, right


def add_low(a, b):
    return (a.astype(F32) + b.astype(F32)).astype(BF16)


def across(block, reps, bit):
    return lax.ppermute(block, "rep", [(at, at ^ 2**bit) for at in range(reps)])


def part_of(block, index):
    half = block.shape[0] // 2
    return lax.dynamic_slice_in_dim(block, index * half, half, axis=0)


def both_halves(mine, other, index):
    first = jnp.where(index == 0, mine, other)
    last = jnp.where(index == 0, other, mine)
    return jnp.concatenate([first, last])


def orders_of(bits):
    return list(range(1, bits)), list(range(1, bits))[::-1]


def sent(block, reps, bit, bit_of):
    return across(part_of(block, 1 - bit_of[bit]), reps, bit)


def kept_sum(block, came, bit, bit_of):
    return add_low(part_of(block, bit_of[bit]), came)


def place_kernel(begin, cut, half, upper, lower, *refs):
    at = begin + pl.program_id(0)

    @pl.when(at < cut)
    def _():
        refs[-1][...] = upper[...].astype(F32)

    @pl.when(at >= cut)
    def _():
        refs[-1][...] = lower[...].astype(F32)


def place_half(upper, lower, begin, rows, target, index):
    cut, width = upper.shape[0] // TILE, upper.shape[1]
    first, blocks = begin // TILE, rows // TILE
    grid_spec = pltpu.PrefetchScalarGridSpec(
        num_scalar_prefetch=1,
        grid=(blocks,),
        in_specs=[
            pl.BlockSpec((TILE, width), lambda at, half: (jnp.minimum(first + at, cut - 1), 0)),
            pl.BlockSpec((TILE, width), lambda at, half: (jnp.maximum(first + at - cut, 0), 0)),
        ]
        + [pl.BlockSpec(memory_space=pl.ANY)] * (target is not None),
        out_specs=pl.BlockSpec((TILE, width), lambda at, half: (half[0] * blocks + at, 0)),
    )
    return pl.pallas_call(
        lambda *refs: place_kernel(first, cut, *refs),
        grid_spec=grid_spec,
        out_shape=shape_of((2 * rows, width), F32),
        input_output_aliases={} if target is None else {3: 0},
        compiler_params=pltpu.CompilerParams(
            vmem_limit_bytes=VMEM_BYTES, dimension_semantics=("arbitrary",)
        ),
        cost_estimate=LIGHT,
    )(index[None].astype(jnp.int32), upper, lower, *([] if target is None else [target]))


def shards(
    tokens,
    doc_ids,
    routes,
    norm_in_gain,
    w_query,
    w_key,
    w_value,
    w_out,
    norm_mid_gain,
    w_router,
    w_expert_in,
    w_expert_down,
    cotangent,
):
    bf16, f32 = BF16, F32
    row_count, model_width = tokens.shape
    query_cols = w_query.shape[1]
    kv_cols = w_key.shape[1]
    own_rows = w_query.shape[0]
    own_experts, ff = w_expert_down.shape[:2]
    shard_at = lax.axis_index("shard")
    reps, shard_count = (lax.axis_size("rep"), lax.axis_size("shard"))

    mask_own = jnp.any(
        routes[:, :, None] == jnp.arange(PAD, dtype=jnp.int32)[None, None, :], axis=1
    )
    side = jnp.concatenate([cotangent, mask_own.astype(bf16)], axis=1)
    side_parts, side_right, side_left = gather_near(side, shard_count)

    small = jnp.concatenate(
        [
            w_router,
            norm_in_gain[:, None],
            norm_mid_gain[:, None],
            jnp.zeros((own_rows, PAD - EXPERTS - 2), bf16),
        ],
        axis=1,
    )
    all_w = gather_all(
        jnp.concatenate([w_query, w_key, w_value, w_out, small], axis=1), reps, shard_count, 1
    )
    small_at = query_cols + 2 * kv_cols + w_out.shape[1]

    cosine, sine_table = rotary_tables(positions(doc_ids), HEAD_DIM)
    cosine, sine_table = cosine[:, 0, :], sine_table[:, 0, :]
    ct = jnp.concatenate([cosine] * 4, axis=1)
    st = jnp.concatenate([-sine_table, sine_table] * 2, axis=1)
    all_w, side_parts, side_right, side_left = tie(all_w, side_parts, side_right, side_left)
    side_far = gather_far(side_right, side_left, shard_count)
    second_low, middle, *kept = forward_block(
        tokens, all_w, ct, st, doc_ids, query_cols, kv_cols
    )
    second_low, side_far = tie(second_low, side_far)
    far_at = shard_count // 2
    side_parts[far_at] = jnp.concatenate(side_far)
    second_parts, *ends = gather_near(second_low, shard_count)
    first_expert = (shard_at * own_experts)[None].astype(jnp.int32)
    order = sorted(range(shard_count), key=lambda k: min(k, shard_count - k))
    order = order[:-2] + order[:-3:-1]
    small_full = all_w[:, small_at:]
    combs, backs, kept_parts = {}, {}, ()
    back_far = None
    for place, k in enumerate(order):
        gated, grad_both, combs[k], backs[k] = expert_block(
            first_expert,
            second_parts[k],
            side_parts[k],
            small_full,
            w_expert_in,
            w_expert_down,
            place,
            shard_count,
            kept_parts,
        )
        if k == 0:
            gated, grad_both, second_parts, ends = tie(gated, grad_both, second_parts, ends)
            second_parts[far_at] = jnp.concatenate(gather_far(*ends, shard_count))
        kept_parts = (gated, grad_both)
        if k == far_at:
            back_far = far_first(backs, shard_count)
        elif back_far is not None:
            gated, grad_both, back_far, backs = tie(gated, grad_both, back_far, backs)
            kept_parts = (gated, grad_both)
    back_near = near_rest(backs, *back_far, shard_count)
    group_rows = shard_count * row_count
    second_all = jnp.concatenate([second_parts[k] for k in order])
    dy_all = jnp.concatenate([side_parts[k][:, :model_width] for k in order])
    grad_in_here = jnp.einsum(
        "td,etf->edf",
        second_all,
        grad_both.reshape(own_experts, group_rows, 2 * ff),
        preferred_element_type=f32,
    ).astype(bf16)
    grad_down_here = jnp.einsum(
        "etf,td->efd",
        gated.reshape(own_experts, group_rows, ff),
        dy_all,
        preferred_element_type=f32,
    ).astype(bf16)

    rep_at = lax.axis_index("rep")
    bits = reps.bit_length() - 1
    bit_of = [rep_at // 2**bit % 2 for bit in range(bits)]
    grads = [g.reshape(-1, model_width) for g in (grad_in_here, grad_down_here)]
    away = jnp.concatenate([part_of(g, 1 - bit_of[0]) for g in grads])
    mine = jnp.concatenate([part_of(g, bit_of[0]) for g in grads])
    held = add_low(mine, across(away, reps, 0))
    back_near, held, combs = tie(back_near, held, combs)
    comb_far = far_first(combs, shard_count)
    cut = held.shape[0] // 2
    blocks, block_orders = [held[:cut], held[cut:]], orders_of(bits)
    steps = bits - 1
    came = [sent(b, reps, o[0], bit_of) for b, o in zip(blocks, block_orders)]
    joint, grad_tokens = backward_block(
        tokens, side, middle, second_low, (backs[0], *back_near), all_w, ct, st, doc_ids, kept
    )
    joint, came, comb_far, blocks, combs = tie(joint, came, comb_far, blocks, combs)
    comb_near = near_rest(combs, *comb_far, shard_count)
    blocks = [kept_sum(b, c, o[0], bit_of) for b, c, o in zip(blocks, came, block_orders)]
    joint, blocks = tie(joint, blocks)
    came = [sent(b, reps, o[1], bit_of) for b, o in zip(blocks, block_orders)]
    joint_own = reduce_all(joint, reps, shard_count, 3)
    joint_own, blocks, comb_near, came = tie(joint_own, blocks, comb_near, came)
    mixed = middle + combs[0].astype(f32) + sum(part.astype(f32) for part in comb_near)
    mixed = mixed.astype(bf16)
    blocks = [kept_sum(b, c, o[1], bit_of) for b, c, o in zip(blocks, came, block_orders)]
    for at in range(2, steps):
        blocks = [
            kept_sum(b, sent(b, reps, o[at], bit_of), o[at], bit_of)
            for b, o in zip(blocks, block_orders)
        ]
    for at in reversed(range(steps)):
        blocks = [
            both_halves(b, across(b, reps, o[at]), bit_of[o[at]])
            for b, o in zip(blocks, block_orders)
        ]
    others = [across(b, reps, 0) for b in blocks]
    in_rows, down_rows = [g.shape[0] // 2 for g in grads]
    grad_in_own = place_half(*blocks, 0, in_rows, None, bit_of[0])
    grad_down_own = place_half(*blocks, in_rows, down_rows, None, bit_of[0])
    grad_in_own = place_half(*others, 0, in_rows, grad_in_own, 1 - bit_of[0])
    grad_down_own = place_half(*others, in_rows, down_rows, grad_down_own, 1 - bit_of[0])
    widths = (query_cols, kv_cols, kv_cols, w_out.shape[1], PAD)
    query_own, key_own, value_own, out_own, small_own = local_call(
        split_kernel, [shape_of((own_rows, wide), f32) for wide in widths], [], joint_own
    )
    return (
        mixed,
        grad_tokens,
        small_own[:, EXPERTS],
        query_own,
        key_own,
        value_own,
        out_own,
        small_own[:, EXPERTS + 1],
        small_own[:, :EXPERTS],
        grad_in_own.reshape(own_experts, model_width, 2 * ff),
        grad_down_own.reshape(own_experts, ff, model_width),
    )


def solution(mesh):
    in_specs = (
        P(("rep", "shard"), None),
        P(("rep", "shard")),
        P(("rep", "shard"), None),
        P("shard"),
        P("shard", None),
        P("shard", None),
        P("shard", None),
        P("shard", None),
        P("shard"),
        P("shard", None),
        P("shard", None, None),
        P("shard", None, None),
        P(("rep", "shard"), None),
    )
    out_specs = (
        P(("rep", "shard"), None),
        P(("rep", "shard"), None),
        P("shard"),
        P("shard", None),
        P("shard", None),
        P("shard", None),
        P("shard", None),
        P("shard"),
        P("shard", None),
        P("shard", None, None),
        P("shard", None, None),
    )
    return jax.shard_map(shards, mesh=mesh, in_specs=in_specs, out_specs=out_specs, check_vma=False)
```

time: 841 us -> 633 us (0.75)
  waiting for transfers between devices: 353 us -> 113 us
  Pallas kernels: 147 us -> 345 us
  matrix products: 205 us -> 31.8 us
  starting transfers between devices: 0.2 us -> 38.4 us
  local copies, waits for them, and re-layouts: 59.9 us -> 43.5 us
  between operations: 14.9 us -> 1.86 us
    pallas_call x0 -> x11, Pallas kernels: none -> 174 us  [the longest x4 81.4 us: expert_block(): pl.pallas_call(lambda *refs: expert_kernel(bool(before), *refs), grid=(ex...]
    dot_general x21 -> x2, matrix products: 205 us -> 31.8 us  [the longest x1 22.5 us: shards(): jnp.einsum('td,etf->edf', second_all, grad_both.reshape(own_experts, grou...]
    reduce_scatter x2 -> x0, waiting for transfers between devices: 143 us -> none  [the longest x1 75.4 us: shards(): lax.psum_scatter(combined.astype(bf16), 'shard', scatter_dimension=0, til...]
    psum x1 -> x0, waiting for transfers between devices: 124 us -> none  [shards(): lax.psum((grad_in_here.astype(bf16), grad_down_here.astype(bf16)), 'rep')]
    ppermute x0 -> x27, waiting for transfers between devices: none -> 113 us  [the longest x16 59.3 us: shift(): lax.ppermute(block, 'shard', [(at, (at + step) % count) for at in range(c...]
    all_gather x2 -> x0, waiting for transfers between devices: 85.1 us -> none  [gather_shard(): return lax.all_gather(piece, 'shard', axis=0, tiled=True)]
    ppermute x0 -> x27, starting transfers between devices: none -> 38.4 us  [the longest x16 30.8 us: shift(): lax.ppermute(block, 'shard', [(at, (at + step) % count) for at in range(c...]
    pallas_call x1, Pallas kernels: 75.8 us -> 99.7 us  [gather_all(): pl.pallas_call(lambda *refs: gather_kernel(reps, shard_count, *refs), out...]
  transfers between devices with their start and end apart: 5 -> 27, of which waited for: 4 -> 7; matrix products, arithmetic and copies ran while one was open for 15% -> 9% of each run, Pallas kernels for 9% -> 50%
where the time goes in v2:
time: 633 us; the launch traced here: 624 us
  Pallas kernels  345 us (55%)
  waiting for transfers between devices  113 us (18%)
  other arithmetic  50.8 us (8%)
  local copies, waits for them, and re-layouts  43.5 us (7%)
  starting transfers between devices  38.4 us (6%)
  matrix products  31.8 us (5%)
    pallas_call x1, Pallas kernels, gather_all(): pl.pallas_call(lambda *refs: gather_kernel(reps, shard_count, *refs), out...  99.7 us
    pallas_call x4, Pallas kernels, expert_block(): pl.pallas_call(lambda *refs: expert_kernel(bool(before), *refs), grid=(ex...  81.4 us
    pallas_call x1, Pallas kernels, reduce_all(): pl.pallas_call(lambda *refs: reduce_kernel(reps, shard_count, *refs), out...  70.5 us
    pallas_call x3, Pallas kernels, local_call(): pl.pallas_call(kernel, out_shape=outs, in_specs=[pl.BlockSpec(memory_spac...  69.1 us
    ppermute x16, waiting for transfers between devices, shift(): lax.ppermute(block, 'shard', [(at, (at + step) % count) for at in range(c...  59.3 us
    ppermute x11, waiting for transfers between devices, across(): lax.ppermute(block, 'rep', [(at, at ^ 2 ** bit) for at in range(reps)])  53.7 us
    ppermute x16, starting transfers between devices, shift(): lax.ppermute(block, 'shard', [(at, (at + step) % count) for at in range(c...  30.8 us
    pallas_call x4, Pallas kernels, place_half(): pl.pallas_call(lambda *refs: place_kernel(first, cut, *refs), grid_spec=g...  23.9 us
  transfers between devices with their start and end apart: 27, of which 7 were waited for; matrix products, arithmetic and copies ran while one was open for 9% of the time, Pallas kernels for 50%

profile of v2, /device:TPU:0, one launch (start us, length us, event | category | flops | bytes accessed | tf_op | source)
XLA Modules:
  0.0 624.0 jit_solution(12128081596467276137)
XLA Ops:
  17.9 99.7 %shard_map.212 = bf16[4,8,32,3200]{3,2,1,0:T(8,128)(2,1)} custom-call(bf16[8,32,3200]{2,1,0:T(8,128)(2,1)} %concatenate.77.refs_0_), custom_call_target="tpu_custom_call" | custom-call | bytes 3276800 | tf_op jit(solution)/shard_map/pallas_call | solution.py:135
  125.1 25.2 %shard_map.213 = (bf16[512,1024]{1,0:T(8,128)(2,1)}, f32[512,1024]{1,0:T(8,128)}, bf16[1024,512]{1,0:T(8,128)(2,1)}, bf16[512,1024]{1,0:T(8,128)(2,1)}, bf16[512...) custom-call(bf16[512,1024]{1,0:T(8,128)(2,1)} %tokens.3, ...), custom_call_target="tpu_custom_call" | custom-call | flops 1000000 | bytes 100000 | tf_op jit(solution)/shard_map/pallas_call | solution.py:420
  156.1 20.3 %shard_map.214 = (bf16[4,4,512,512]{3,2,1,0:T(8,128)(2,1)}, bf16[4,4,512,1024]{3,2,1,0:T(8,128)(2,1)}, bf16[512,1024]{1,0:T(8,128)(2,1)}, bf16[512,1152]{1,0:T(8,128)(2,1)}) custom-call(s32[1]{0:T(128)} %bitcast.8.refs_0_, bf16[512,1024]{1,0:T(8,128)(2,1)} %get-tuple-element.127.refs_1_.second, bf16[512,1152]{1,0:T(8,128)(2,1)} %copy-done.1, ...), custom_call_target="tpu_custom_call" | custom-call | flops 1000000 | bytes 100000 | tf_op jit(solution)/shard_map/pallas_call | solution.py:671
  178.5 20.4 %collective-permute-done.5.refs_1_ = bf16[512,1024]{1,0:T(8,128)(2,1)} collective-permute-done((bf16[512,1024]{1,0:T(8,128)(2,1)}, bf16[512,1024]{1,0:T(8,128)(2,1)}, u32[]{:S(2)}, u32[]{:S(2)}) %collective-permute-start.5) | collective-permute-done | bytes 1048608 | tf_op jit(solution)/shard_map/ppermute | solution.py:692
  207.3 20.5 %shard_map.215 = (bf16[4,4,512,512]{3,2,1,0:T(8,128)(2,1)}, bf16[4,4,512,1024]{3,2,1,0:T(8,128)(2,1)}, bf16[512,1024]{1,0:T(8,128)(2,1)}, bf16[512,1152]{1,0:T(8,128)(2,1)}) custom-call(s32[1]{0:T(128)} %bitcast.8.refs_0_, bf16[512,1024]{1,0:T(8,128)(2,1)} %collective-permute-done.4.refs_1_, ...), custom_call_target="tpu_custom_call", output_to_operand_aliasing={{0}: (6, {}), {1}: (7, {})} | custom-call | flops 1000000 | bytes 100000 | tf_op jit(solution)/shard_map/pallas_call | solution.py:671
  230.1 20.3 %shard_map.216 = (bf16[4,4,512,512]{3,2,1,0:T(8,128)(2,1)}, bf16[4,4,512,1024]{3,2,1,0:T(8,128)(2,1)}, bf16[512,1024]{1,0:T(8,128)(2,1)}, bf16[512,1152]{1,0:T(8,128)(2,1)}) custom-call(s32[1]{0:T(128)} %bitcast.8.refs_0_, bf16[512,1024]{1,0:T(8,128)(2,1)} %pad_maximum_fusion.8.refs_1_, ...), custom_call_target="tpu_custom_call", output_to_operand_aliasing={{0}: (6, {}), {1}: (7, {})} | custom-call | flops 1000000 | bytes 100000 | tf_op jit(solution)/shard_map/pallas_call | solution.py:671
  257.3 20.2 %shard_map.217 = (bf16[4,4,512,512]{3,2,1,0:T(8,128)(2,1)}, bf16[4,4,512,1024]{3,2,1,0:T(8,128)(2,1)}, bf16[512,1024]{1,0:T(8,128)(2,1)}, bf16[512,1152]{1,0:T(8,128)(2,1)}) custom-call(s32[1]{0:T(128)} %bitcast.8.refs_0_, bf16[512,1024]{1,0:T(8,128)(2,1)} %collective-permute-done.5.refs_1_, ...), custom_call_target="tpu_custom_call", output_to_operand_aliasing={{0}: (6, {}), {1}: (7, {})} | custom-call | flops 1000000 | bytes 100000 | tf_op jit(solution)/shard_map/pallas_call | solution.py:671
  281.2 22.5 %convolution_convert_fusion = bf16[4,1024,1024]{1,2,0:T(8,128)(2,1)} fusion(bf16[4,2048,1024]{2,1,0:T(8,128)(2,1)} %bitcast.32, bf16[2048,1024]{1,0:T(8,128)(2,1)S(1)} %constant_dynamic-update-slice_fusion.2), kind=kOutput, calls=%fused_computation.1 | convolution fusion | flops 17184063488 | bytes 29360128 | tf_op jit(solution)/shard_map/td,etf->edf/dot_general | solution.py:890
  303.7 9.3 %fusion.8 = bf16[4,512,1024]{2,1,0:T(8,128)(2,1)S(1)} fusion(bf16[4,2048,512]{2,1,0:T(8,128)(2,1)S(1)} %bitcast.35, bf16[512,1024]{1,0:T(8,128)(2,1)S(1)} %slice-done.2, bf16[512,1024]{1,0:T(8,128)(2,1)S(1)} %slice.104, bf16[512,1024]{1,0:T(8,128)(2,1)S(1)} %slice-done.3, bf16[512,1024]{1,0:T(8,128)(2,1)S(1)} %slice.89), kind=kOutput, calls=%fused_computation.16 | convolution fusion | flops 8608808960 | bytes 16777216 | tf_op jit(solution)/shard_map/etf,td->efd/dot_general | solution.py:896
  313.5 6.5 %constant_dynamic-slice_fusion.7 = (bf16[2048,1024]{1,0:T(8,128)(2,1)}, bf16[2048,1024]{1,0:T(8,128)(2,1)S(1)}) fusion(bf16[4096,1024]{1,0:T(8,128)(2,1)} %bitcast.41, s32[]{:T(128)S(6)} %select_n.104, s32[]{:T(128)S(6)} %select_n.106), kind=kLoop, calls=%fused_computation.64 | loop fusion | bytes 16777224 | tf_op jit(solution)/shard_map/dynamic_slice | solution.py:744
  324.9 3.9 collective-permute-start.10
  333.9 10.0 %add_convert_fusion = bf16[3072,1024]{1,0:T(8,128)(2,1)} fusion(bf16[3072,1024]{1,0:T(8,128)(2,1)} %collective-permute-done.12, bf16[1024,1024]{1,0:T(8,128)(2,1)S(1)} %get-tuple-element.223, bf16[2048,1024]{1,0:T(8,128)(2,1)} %get-tuple-element.219), kind=kLoop, calls=%fused_computation | loop fusion | flops 22020096 | bytes 18874368 | tf_op jit(solution)/shard_map/convert_element_type | solution.py:735
  343.9 11.2 %collective-permute-done.10.back_left = bf16[512,1152]{1,0:T(8,128)(2,1)} collective-permute-done((bf16[512,1152]{1,0:T(8,128)(2,1)S(1)}, bf16[512,1152]{1,0:T(8,128)(2,1)}, u32[]{:S(2)}, u32[]{:S(2)}) %collective-permute-start.10) | collective-permute-done | bytes 1179680 | tf_op jit(solution)/shard_map/ppermute | solution.py:692
  355.1 25.5 %collective-permute-done.11.back_right = bf16[512,1152]{1,0:T(8,128)(2,1)} collective-permute-done((bf16[512,1152]{1,0:T(8,128)(2,1)}, bf16[512,1152]{1,0:T(8,128)(2,1)}, u32[]{:S(2)}, u32[]{:S(2)}) %collective-permute-start.11) | collective-permute-done | bytes 1179680 | tf_op jit(solution)/shard_map/ppermute | solution.py:692
  392.5 40.7 %shard_map.218 = (bf16[1024,3200]{1,0:T(8,128)(2,1)}, f32[512,1024]{1,0:T(8,128)}) custom-call(bf16[512,1024]{1,0:T(8,128)(2,1)} %tokens.3, bf16[512,1152]{1,0:T(8,128)(2,1)} %copy-done.1, f32[512,1024]{1,0:T(8,128)} %get-tuple-element.93.middle, bf16[512,1024]{1,0:T(8,128)(2,1)} %get-tuple-element.127.refs_1_.second, ...), custom_call_target="tpu_custom_call" | custom-call | flops 1000000 | bytes 100000 | tf_op jit(solution)/shard_map/pallas_call | solution.py:420
  440.0 3.9 collective-permute-start.17
  451.3 70.5 %shard_map.219 = bf16[1,8,32,3200]{3,2,1,0:T(8,128)(2,1)} custom-call(bf16[4,8,32,3200]{3,2,1,0:T(8,128)(2,1)} %bitcast.42), custom_call_target="tpu_custom_call" | custom-call | bytes 3276800 | tf_op jit(solution)/shard_map/pallas_call | solution.py:250
  526.8 16.7 %collective-permute-done.21 = bf16[384,1024]{1,0:T(8,128)(2,1)} collective-permute-done((bf16[384,1024]{1,0:T(8,128)(2,1)S(1)}, bf16[384,1024]{1,0:T(8,128)(2,1)}, u32[]{:S(2)}, u32[]{:S(2)}) %collective-permute-start.21) | collective-permute-done | bytes 786464 | tf_op jit(solution)/shard_map/ppermute | solution.py:739
  549.2 33.1 %collective-permute-done.22 = bf16[768,1024]{1,0:T(8,128)(2,1)} collective-permute-done((bf16[768,1024]{1,0:T(8,128)(2,1)}, bf16[768,1024]{1,0:T(8,128)(2,1)}, u32[]{:S(2)}, u32[]{:S(2)}) %collective-permute-start.22) | collective-permute-done | bytes 1572896 | tf_op jit(solution)/shard_map/ppermute | solution.py:739
  595.4 4.2 add_convert_fusion.3
  599.6 7.6 %shard_map.221.refs_3_ = f32[4096,1024]{1,0:T(8,128)} custom-call(s32[1]{0:T(128)} %bitcast.20.refs_0_, bf16[1536,1024]{1,0:T(8,128)(2,1)} %copy-done, bf16[1536,1024]{1,0:T(8,128)(2,1)} %pad_maximum_fusion.2.refs_2_), custom_call_target="tpu_custom_call" | custom-call | flops 1000000 | bytes 100000 | tf_op jit(solution)/shard_map/pallas_call | solution.py:790
  607.2 4.4 shard_map.223.refs_3_
  611.6 7.6 %shard_map.222 = f32[4096,1024]{1,0:T(8,128)} custom-call(s32[1]{0:T(128)} %bitcast.19.refs_0_, bf16[1536,1024]{1,0:T(8,128)(2,1)} %collective-permute-done.23.refs_1_, bf16[1536,1024]{1,0:T(8,128)(2,1)} %collective-permute-done.26.refs_2_, f32[4096,1024]{1,0:T(8,128)} %shard_map.221.refs_3_), custom_call_target="tpu_custom_call", output_to_operand_aliasing={{}: (3, {})} | custom-call | flops 1000000 | bytes 100000 | tf_op jit(solution)/shard_map/pallas_call | solution.py:790
  619.2 4.4 shard_map.224
  (174 shorter events, 113.5 us)
Async XLA Ops:
  5.8 112.9 %collective-permute-start = (bf16[512,1152]{1,0:T(8,128)(2,1)S(1)}, bf16[512,1152]{1,0:T(8,128)(2,1)S(1)}, u32[]{:S(2)}, u32[]{:S(2)}) collective-permute-start(bf16[512,1152]{1,0:T(8,128)(2,1)S(1)} %pad_maximum_fusion.5.refs_2_.side), channel_id=1, source_target_pairs={{0,1},{1,2},{2,3},{3,0},{4,5},{5,6},{6,7},{7,4},{8,9},{9,10},{10,1... | collective-permute-start | bytes 3538952 | tf_op jit(solution)/shard_map/ppermute | solution.py:692
  8.9 109.9 %collective-permute-start.1 = (bf16[512,1152]{1,0:T(8,128)(2,1)S(1)}, bf16[512,1152]{1,0:T(8,128)(2,1)S(1)}, u32[]{:S(2)}, u32[]{:S(2)}) collective-permute-start(bf16[512,1152]{1,0:T(8,128)(2,1)S(1)} %pad_maximum_fusion.5.refs_2_.side), channel_id=1, source_target_pairs={{0,3},{1,0},{2,1},{3,2},{4,7},{5,4},{6,5},{7,6},{8,11},{9,8},{10,9... | collective-permute-start | bytes 3538952 | tf_op jit(solution)/shard_map/ppermute | solution.py:692
  118.8 31.5 %collective-permute-start.2 = (bf16[256,1152]{1,0:T(8,128)(2,1)S(1)}, bf16[256,1152]{1,0:T(8,128)(2,1)}, u32[]{:S(2)}, u32[]{:S(2)}) collective-permute-start(bf16[256,1152]{1,0:T(8,128)(2,1)S(1)} %slice.78), channel_id=1, source_target_pairs={{0,1},{1,2},{2,3},{3,0},{4,5},{5,6},{6,7},{7,4},{8,9},{9,10},{10,1... | collective-permute-start | bytes 1769480 | tf_op jit(solution)/shard_map/ppermute | solution.py:692
  121.7 28.6 %collective-permute-start.3 = (bf16[256,1152]{1,0:T(8,128)(2,1)S(1)}, bf16[256,1152]{1,0:T(8,128)(2,1)}, u32[]{:S(2)}, u32[]{:S(2)}) collective-permute-start(bf16[256,1152]{1,0:T(8,128)(2,1)S(1)} %slice.79), channel_id=1, source_target_pairs={{0,3},{1,0},{2,1},{3,2},{4,7},{5,4},{6,5},{7,6},{8,11},{9,8},{10,9... | collective-permute-start | bytes 1769480 | tf_op jit(solution)/shard_map/ppermute | solution.py:692
  150.3 28.2 %collective-permute-start.4 = (bf16[512,1024]{1,0:T(8,128)(2,1)}, bf16[512,1024]{1,0:T(8,128)(2,1)}, u32[]{:S(2)}, u32[]{:S(2)}) collective-permute-start(bf16[512,1024]{1,0:T(8,128)(2,1)} %get-tuple-element.127.refs_1_.second), channel_id=1, source_target_pairs={{0,1},{1,2},{2,3},{3,0},{4,5},{5,6},{6,7},{7,4},{8,9},{9,10},{10,1... | collective-permute-start | bytes 3145736 | tf_op jit(solution)/shard_map/ppermute | solution.py:692
  151.3 47.6 %collective-permute-start.5 = (bf16[512,1024]{1,0:T(8,128)(2,1)}, bf16[512,1024]{1,0:T(8,128)(2,1)}, u32[]{:S(2)}, u32[]{:S(2)}) collective-permute-start(bf16[512,1024]{1,0:T(8,128)(2,1)} %get-tuple-element.127.refs_1_.second), channel_id=1, source_target_pairs={{0,3},{1,0},{2,1},{3,2},{4,7},{5,4},{6,5},{7,6},{8,11},{9,8},{10,9... | collective-permute-start | bytes 3145736 | tf_op jit(solution)/shard_map/ppermute | solution.py:692
  200.8 27.0 %collective-permute-start.7 = (bf16[256,1024]{1,0:T(8,128)(2,1)}, bf16[256,1024]{1,0:T(8,128)(2,1)}, u32[]{:S(2)}, u32[]{:S(2)}) collective-permute-start(bf16[256,1024]{1,0:T(8,128)(2,1)} %slice.82), channel_id=1, source_target_pairs={{0,3},{1,0},{2,1},{3,2},{4,7},{5,4},{6,5},{7,6},{8,11},{9,8},{10,9... | collective-permute-start | bytes 1572872 | tf_op jit(solution)/shard_map/ppermute | solution.py:692
  204.6 23.3 %collective-permute-start.6 = (bf16[256,1024]{1,0:T(8,128)(2,1)}, bf16[256,1024]{1,0:T(8,128)(2,1)}, u32[]{:S(2)}, u32[]{:S(2)}) collective-permute-start(bf16[256,1024]{1,0:T(8,128)(2,1)} %slice.81), channel_id=1, source_target_pairs={{0,1},{1,2},{2,3},{3,0},{4,5},{5,6},{6,7},{7,4},{8,9},{9,10},{10,1... | collective-permute-start | bytes 1572872 | tf_op jit(solution)/shard_map/ppermute | solution.py:692
  251.8 29.4 %collective-permute-start.8 = (bf16[256,1152]{1,0:T(8,128)(2,1)S(1)}, bf16[256,1152]{1,0:T(8,128)(2,1)S(1)}, u32[]{:S(2)}, u32[]{:S(2)}) collective-permute-start(bf16[256,1152]{1,0:T(8,128)(2,1)S(1)} %get-tuple-element.234), channel_id=1, source_target_pairs={{0,3},{1,0},{2,1},{3,2},{4,7},{5,4},{6,5},{7,6},{8,11},{9,8},{10,9... | collective-permute-start | bytes 1769480 | tf_op jit(solution)/shard_map/ppermute | solution.py:692
  255.5 25.7 %collective-permute-start.9 = (bf16[256,1152]{1,0:T(8,128)(2,1)S(1)}, bf16[256,1152]{1,0:T(8,128)(2,1)S(1)}, u32[]{:S(2)}, u32[]{:S(2)}) collective-permute-start(bf16[256,1152]{1,0:T(8,128)(2,1)S(1)} %get-tuple-element.233), channel_id=1, source_target_pairs={{0,1},{1,2},{2,3},{3,0},{4,5},{5,6},{6,7},{7,4},{8,9},{9,10},{10,1... | collective-permute-start | bytes 1769480 | tf_op jit(solution)/shard_map/ppermute | solution.py:692
  324.9 30.2 %collective-permute-start.10 = (bf16[512,1152]{1,0:T(8,128)(2,1)S(1)}, bf16[512,1152]{1,0:T(8,128)(2,1)}, u32[]{:S(2)}, u32[]{:S(2)}) collective-permute-start(bf16[512,1152]{1,0:T(8,128)(2,1)S(1)} %pad_maximum_fusion.6), channel_id=1, source_target_pairs={{0,3},{1,0},{2,1},{3,2},{4,7},{5,4},{6,5},{7,6},{8,11},{9,8},{10,9... | collective-permute-start | bytes 3538952 | tf_op jit(solution)/shard_map/ppermute | solution.py:692
  330.1 50.6 %collective-permute-start.11 = (bf16[512,1152]{1,0:T(8,128)(2,1)}, bf16[512,1152]{1,0:T(8,128)(2,1)}, u32[]{:S(2)}, u32[]{:S(2)}) collective-permute-start(bf16[512,1152]{1,0:T(8,128)(2,1)} %pad_maximum_fusion.7), channel_id=1, source_target_pairs={{0,1},{1,2},{2,3},{3,0},{4,5},{5,6},{6,7},{7,4},{8,9},{9,10},{10,1... | collective-permute-start | bytes 3538952 | tf_op jit(solution)/shard_map/ppermute | solution.py:692
  385.5 47.7 %collective-permute-start.13 = (bf16[768,1024]{1,0:T(8,128)(2,1)}, bf16[768,1024]{1,0:T(8,128)(2,1)}, u32[]{:S(2)}, u32[]{:S(2)}) collective-permute-start(bf16[768,1024]{1,0:T(8,128)(2,1)} %constant_dynamic-slice_fusion.3), channel_id=1, source_target_pairs={{0,8},{4,12},{8,0},{12,4},{16,24},{20,28},{24,16},{28,20},{1,9},{5... | collective-permute-start | bytes 4718600 | tf_op jit(solution)/shard_map/ppermute | solution.py:739
  387.4 45.9 %collective-permute-start.14 = (bf16[768,1024]{1,0:T(8,128)(2,1)}, bf16[768,1024]{1,0:T(8,128)(2,1)}, u32[]{:S(2)}, u32[]{:S(2)}) collective-permute-start(bf16[768,1024]{1,0:T(8,128)(2,1)} %constant_dynamic-slice_fusion.2), channel_id=1, source_target_pairs={{0,16},{4,20},{8,24},{12,28},{16,0},{20,4},{24,8},{28,12},{1,17},{... | collective-permute-start | bytes 4718600 | tf_op jit(solution)/shard_map/ppermute | solution.py:739
  389.0 44.2 %collective-permute-start.15 = (bf16[256,1024]{1,0:T(8,128)(2,1)}, bf16[256,1024]{1,0:T(8,128)(2,1)}, u32[]{:S(2)}, u32[]{:S(2)}) collective-permute-start(bf16[256,1024]{1,0:T(8,128)(2,1)} %get-tuple-element.236), channel_id=1, source_target_pairs={{0,3},{1,0},{2,1},{3,2},{4,7},{5,4},{6,5},{7,6},{8,11},{9,8},{10,9... | collective-permute-start | bytes 1572872 | tf_op jit(solution)/shard_map/ppermute | solution.py:692
  392.5 40.7 %collective-permute-start.16 = (bf16[256,1024]{1,0:T(8,128)(2,1)}, bf16[256,1024]{1,0:T(8,128)(2,1)}, u32[]{:S(2)}, u32[]{:S(2)}) collective-permute-start(bf16[256,1024]{1,0:T(8,128)(2,1)} %get-tuple-element.235), channel_id=1, source_target_pairs={{0,1},{1,2},{2,3},{3,0},{4,5},{5,6},{6,7},{7,4},{8,9},{9,10},{10,1... | collective-permute-start | bytes 1572872 | tf_op jit(solution)/shard_map/ppermute | solution.py:692
  440.0 81.8 %collective-permute-start.17 = (bf16[512,1024]{1,0:T(8,128)(2,1)S(1)}, bf16[512,1024]{1,0:T(8,128)(2,1)}, u32[]{:S(2)}, u32[]{:S(2)}) collective-permute-start(bf16[512,1024]{1,0:T(8,128)(2,1)S(1)} %pad_maximum_fusion.9), channel_id=1, source_target_pairs={{0,3},{1,0},{2,1},{3,2},{4,7},{5,4},{6,5},{7,6},{8,11},{9,8},{10,9... | collective-permute-start | bytes 3145736 | tf_op jit(solution)/shard_map/ppermute | solution.py:692
  446.2 75.6 %collective-permute-start.18 = (bf16[512,1024]{1,0:T(8,128)(2,1)}, bf16[512,1024]{1,0:T(8,128)(2,1)}, u32[]{:S(2)}, u32[]{:S(2)}) collective-permute-start(bf16[512,1024]{1,0:T(8,128)(2,1)} %pad_maximum_fusion.10), channel_id=1, source_target_pairs={{0,1},{1,2},{2,3},{3,0},{4,5},{5,6},{6,7},{7,4},{8,9},{9,10},{10,1... | collective-permute-start | bytes 3145736 | tf_op jit(solution)/shard_map/ppermute | solution.py:692
  447.4 74.4 %collective-permute-start.19 = (bf16[384,1024]{1,0:T(8,128)(2,1)}, bf16[384,1024]{1,0:T(8,128)(2,1)}, u32[]{:S(2)}, u32[]{:S(2)}) collective-permute-start(bf16[384,1024]{1,0:T(8,128)(2,1)} %constant_dynamic-slice_fusion.1), channel_id=1, source_target_pairs={{0,16},{4,20},{8,24},{12,28},{16,0},{20,4},{24,8},{28,12},{1,17},{... | collective-permute-start | bytes 2359304 | tf_op jit(solution)/shard_map/ppermute | solution.py:739
  449.8 72.0 %collective-permute-start.20 = (bf16[384,1024]{1,0:T(8,128)(2,1)}, bf16[384,1024]{1,0:T(8,128)(2,1)S(1)}, u32[]{:S(2)}, u32[]{:S(2)}) collective-permute-start(bf16[384,1024]{1,0:T(8,128)(2,1)} %constant_dynamic-slice_fusion), channel_id=1, source_target_pairs={{0,8},{4,12},{8,0},{12,4},{16,24},{20,28},{24,16},{28,20},{1,9},{5... | collective-permute-start | bytes 2359304 | tf_op jit(solution)/shard_map/ppermute | solution.py:739
  546.1 36.2 %collective-permute-start.22 = (bf16[768,1024]{1,0:T(8,128)(2,1)}, bf16[768,1024]{1,0:T(8,128)(2,1)}, u32[]{:S(2)}, u32[]{:S(2)}) collective-permute-start(bf16[768,1024]{1,0:T(8,128)(2,1)} %pad_maximum_fusion.3), channel_id=1, source_target_pairs={{0,8},{4,12},{8,0},{12,4},{16,24},{20,28},{24,16},{28,20},{1,9},{5... | collective-permute-start | bytes 4718600 | tf_op jit(solution)/shard_map/ppermute | solution.py:739
  548.3 36.6 %collective-permute-start.25 = (bf16[768,1024]{1,0:T(8,128)(2,1)S(1)}, bf16[768,1024]{1,0:T(8,128)(2,1)S(1)}, u32[]{:S(2)}, u32[]{:S(2)}) collective-permute-start(bf16[768,1024]{1,0:T(8,128)(2,1)S(1)} %pad_maximum_fusion.4), channel_id=1, source_target_pairs={{0,16},{4,20},{8,24},{12,28},{16,0},{20,4},{24,8},{28,12},{1,17},{... | collective-permute-start | bytes 4718600 | tf_op jit(solution)/shard_map/ppermute | solution.py:739
  584.8 26.8 %collective-permute-start.23 = (bf16[1536,1024]{1,0:T(8,128)(2,1)S(1)}, bf16[1536,1024]{1,0:T(8,128)(2,1)}, u32[]{:S(2)}, u32[]{:S(2)}) collective-permute-start(bf16[1536,1024]{1,0:T(8,128)(2,1)S(1)} %pad_maximum_fusion.1.refs_1_), channel_id=1, source_target_pairs={{0,4},{4,0},{8,12},{12,8},{16,20},{20,16},{24,28},{28,24},{1,5},{5... | collective-permute-start | bytes 9437192 | tf_op jit(solution)/shard_map/ppermute | solution.py:739
  588.9 22.7 %collective-permute-start.26 = (bf16[1536,1024]{1,0:T(8,128)(2,1)}, bf16[1536,1024]{1,0:T(8,128)(2,1)}, u32[]{:S(2)}, u32[]{:S(2)}) collective-permute-start(bf16[1536,1024]{1,0:T(8,128)(2,1)} %pad_maximum_fusion.2.refs_2_), channel_id=1, source_target_pairs={{0,4},{4,0},{8,12},{12,8},{16,20},{20,16},{24,28},{28,24},{1,5},{5... | collective-permute-start | bytes 9437192 | tf_op jit(solution)/shard_map/ppermute | solution.py:739
  (33 other events, 941.8 us)

commit v3 on v2

--- a/solution.py
+++ b/solution.py
@@ -103,10 +103,47 @@
         flying[half].wait()
 
 
-def gather_kernel(reps, shard_count, piece, out, z_send, z_recv, sends, recvs):
+def spread_others(out, orders, columns, rep_at, shard_at, shard_count, sends, recvs):
+    bits = len(orders[0])
+    flying = [[] for _ in range(HALVES)]
+    for at in reversed(range(bits)):
+        window = 2 ** (bits - 1 - at)
+        for half in range(HALVES):
+            order = orders[half]
+            place = rep_place(rep_at, order)
+            begin = place // window * window
+            for copy in flying[half]:
+                copy.wait()
+            flying[half] = []
+            for step in range(1, shard_count):
+                block = out.at[
+                    (shard_at + step) % shard_count, pl.ds(begin, window), :, columns[half]
+                ]
+                copy = pltpu.make_async_remote_copy(
+                    src_ref=block,
+                    dst_ref=block,
+                    send_sem=sends.at[half, at, step],
+                    recv_sem=recvs.at[half, at, step],
+                    device_id=(partner(rep_at, order[at]), shard_at),
+                    device_id_type=MESH,
+                )
+                copy.start()
+                flying[half].append(copy)
+    for half in range(HALVES):
+        for copy in flying[half]:
+            copy.wait()
+
+
+def gather_kernel(reps, shard_count, *refs):
+    weights, (dy, routes, out, side, right, left) = refs[:5], refs[5:11]
+    piece, z_send, z_recv, sends, recvs, d_send, d_recv = refs[11:]
     rep_at, shard_at = (lax.axis_index("rep"), lax.axis_index("shard"))
     orders = bit_orders(reps)
     columns = halves_of(piece.shape[-1])
+    begin = 0
+    for ref in weights:
+        piece[:, :, begin : begin + ref.shape[-1]] = ref[...]
+        begin += ref.shape[-1]
     meet(rep_at, shard_at, reps, shard_count)
     flying = []
     for half in range(HALVES):
@@ -122,26 +159,61 @@
             )
             copy.start()
             flying.append(copy)
-        out[shard_at, place, :, columns[half]] = piece[place, :, columns[half]]
+
+    @pl.loop(0, reps)
+    def _(index):
+        out[shard_at, index] = piece[index]
+
+    rows, width = dy.shape
+    for at in range(0, rows, LANES):
+        here = slice(at, at + LANES)
+        side[here, :width] = dy[here, :]
+        named = routes[here, :]
+        lane = lane_of((LANES, PAD))
+        mask = lane == named[:, 0:1]
+        for k in range(1, named.shape[1]):
+            mask = mask | (lane == named[:, k : k + 1])
+        side[here, width:] = jnp.where(mask, 1.0, 0.0).astype(side.dtype)
     for copy in flying:
         copy.wait()
-    spread(out, orders, columns, rep_at, shard_at, sends, recvs)
-
-
-def gather_all(piece, reps, shard_count, number):
-    own, width = piece.shape
+    flying = []
+    if shard_count > 1:
+        for number, (step, target) in enumerate(((1, right), (shard_count - 1, left))):
+            copy = pltpu.make_async_remote_copy(
+                src_ref=side,
+                dst_ref=target,
+                send_sem=d_send.at[number],
+                recv_sem=d_recv.at[number],
+                device_id=(rep_at, (shard_at + step) % shard_count),
+                device_id_type=MESH,
+            )
+            copy.start()
+            flying.append(copy)
+    spread_others(out, orders, columns, rep_at, shard_at, shard_count, sends, recvs)
+    for copy in flying:
+        copy.wait()
+
+
+def gather_all(weights, dy, routes, reps, shard_count, number):
+    own = weights[0].shape[0]
+    width = sum(w.shape[1] for w in weights)
     rows = own // reps
     bits = reps.bit_length() - 1
-    out = pl.pallas_call(
+    kind = weights[0].dtype
+    wide = jax.ShapeDtypeStruct((dy.shape[0], dy.shape[1] + PAD), kind)
+    out, side, right, left = pl.pallas_call(
         lambda *refs: gather_kernel(reps, shard_count, *refs),
-        out_shape=jax.ShapeDtypeStruct((shard_count, reps, rows, width), piece.dtype),
-        in_specs=[pl.BlockSpec(memory_space=pltpu.VMEM)],
-        out_specs=pl.BlockSpec(memory_space=pltpu.VMEM),
+        out_shape=[jax.ShapeDtypeStruct((shard_count, reps, rows, width), kind), wide, wide, wide],
+        in_specs=[pl.BlockSpec(memory_space=pltpu.VMEM)] * (len(weights) + 2),
+        out_specs=[pl.BlockSpec(memory_space=pltpu.VMEM)] * 4,
         scratch_shapes=[
+            pltpu.VMEM((reps, rows, width), kind),
             pltpu.SemaphoreType.DMA((HALVES, shard_count)),
             pltpu.SemaphoreType.DMA((HALVES, shard_count)),
-            pltpu.SemaphoreType.DMA((HALVES, bits)),
-            pltpu.SemaphoreType.DMA((HALVES, bits)),
+            pltpu.SemaphoreType.DMA((HALVES, bits, shard_count)),
+            pltpu.SemaphoreType.DMA((HALVES, bits, shard_count)),
+            pltpu.SemaphoreType.DMA((2,)),
+            pltpu.SemaphoreType.DMA((2,)),
         ],
         compiler_params=pltpu.CompilerParams(
             collective_id=number, has_side_effects=True, vmem_limit_bytes=VMEM_BYTES
@@ -149,8 +221,8 @@
         cost_estimate=pl.CostEstimate(
             flops=0, bytes_accessed=shard_count * own * width, transcendentals=0
         ),
-    )(piece.reshape(reps, rows, width))
-    return out.reshape(shard_count * own, width)
+    )(*[w.reshape(reps, rows, w.shape[1]) for w in weights], dy, routes)
+    return out.reshape(shard_count * own, width), side, right, left
 
 
 def reduce_kernel(reps, shard_count, parts, out, *scratch):
@@ -452,9 +524,9 @@
 
 def backward_kernel(
     tokens, side, middle, second, back_own, back_left, back_right, w, ct, st, doc_col, doc_row,
-    first_t, q8, keys, values, att_t, lse,
-    joint, grad_tokens,
-    bias, grad_middle, grad_branch, grad_att, grad_pre, grad_first, dq_t, dk, dv, rows_t,
+    q8, keys, values, att_t, lse,
+    grad_out, rows_t, grad_middle, grad_pre,
+    bias, grad_branch, grad_att, dq_t, dk, dv,
 ):
     rows, width = tokens.shape
     q_cols, kv_cols = q8.shape[1], keys.shape[1]
@@ -462,7 +534,7 @@
     small_at = w.shape[1] - PAD
     small = w[:, small_at:]
     gains = small.astype(F32).T
-    gain_in, gain_mid = gains[EXPERTS : EXPERTS + 1], gains[EXPERTS + 1 : EXPERTS + 2]
+    gain_mid = gains[EXPERTS + 1 : EXPERTS + 2]
     tall = back_own.shape[1]
     gain_sum = jnp.zeros((1, width), F32)
     router_t = jnp.zeros((PAD, width), F32)
@@ -501,9 +573,7 @@
 
     @pl.loop(0, width // TILE)
     def _(j):
-        joint[:, pl.ds(pl.multiple_of(qkv_cols + j * TILE, TILE), TILE)] = dot(
-            att_t[...], grad_branch[:, tile_at(j)]
-        ).astype(BF16)
+        grad_out[:, tile_at(j)] = dot(att_t[...], grad_branch[:, tile_at(j)]).astype(BF16)
         out_rows = w[tile_at(j), pl.ds(qkv_cols, width)]
         grad_att[:, tile_at(j)] = dot_nt(grad_branch[...], out_rows).astype(BF16)
 
@@ -551,6 +621,19 @@
         grad_pre[:, pl.ds(k_at, LANES)] = grad_k.astype(BF16)
         grad_pre[:, pl.ds(v_at, LANES)] = grad_v.astype(BF16)
 
+
+def finish_kernel(
+    tokens, w, grad_middle, grad_pre, grad_out, rows_in, first_t,
+    joint, grad_tokens,
+    grad_first, rows_t,
+):
+    rows, width = tokens.shape
+    qkv_cols = grad_pre.shape[1]
+    small_at = w.shape[1] - PAD
+    gain_in = w[:, small_at:].astype(F32).T[EXPERTS : EXPERTS + 1]
+    joint[:, qkv_cols:small_at] = grad_out[...]
+    rows_t[...] = rows_in[...]
+
     @pl.loop(0, qkv_cols // TILE)
     def _(j):
         joint[:, tile_at(j)] = dot(first_t[...], grad_pre[:, tile_at(j)]).astype(BF16)
@@ -577,29 +660,40 @@
 def backward_block(tokens, side, middle, second, backs, w, ct, st, doc_ids, kept):
     rows, width = tokens.shape
     q_cols, kv_cols = kept[1].shape[1], kept[2].shape[1]
-    outs = [shape_of((width, w.shape[1]), BF16), shape_of((rows, width), F32)]
+    outs = [
+        shape_of((width, width), BF16),
+        shape_of((PAD, width), F32),
+        shape_of((rows, width), F32),
+        shape_of((rows, q_cols + 2 * kv_cols), BF16),
+    ]
     scratch = [
         pltpu.VMEM((rows, rows), F32),
-        pltpu.VMEM((rows, width), F32),
         pltpu.VMEM((rows, width), BF16),
         pltpu.VMEM((rows, q_cols), BF16),
-        pltpu.VMEM((rows, q_cols + 2 * kv_cols), BF16),
-        pltpu.VMEM((rows, width), F32),
         pltpu.VMEM((LANES, rows), F32),
         pltpu.VMEM((GROUP, rows, LANES), F32),
         pltpu.VMEM((GROUP, rows, LANES), F32),
-        pltpu.VMEM((PAD, width), F32),
     ]
     return local_call(
         backward_kernel, outs, scratch,
-        tokens, side, middle, second, *backs, w, ct, st, doc_ids[:, None], doc_ids[None, :], *kept,
+        tokens, side, middle, second, *backs, w, ct, st, doc_ids[:, None], doc_ids[None, :], *kept[1:],
+    )
+
+
+def finish_block(tokens, w, grad_middle, grad_pre, grad_out, rows_t, first_t):
+    rows, width = tokens.shape
+    outs = [shape_of((width, w.shape[1]), BF16), shape_of((rows, width), F32)]
+    scratch = [pltpu.VMEM((rows, width), F32), pltpu.VMEM((PAD, width), F32)]
+    return local_call(
+        finish_kernel, outs, scratch, tokens, w, grad_middle, grad_pre, grad_out, rows_t, first_t
     )
 
 
 def expert_kernel(
     aliased, first_expert, second, side, small, in_w, down_w, *refs
 ):
-    gated, grad_both, comb, back, gates, grad_gates, comb_sum, back_sum = refs[2 * aliased :]
+    gated_t, grad_both, second_t, dy, comb, back = refs[4 * aliased : 4 * aliased + 6]
+    gates, grad_gates, comb_sum, back_sum, gated = refs[4 * aliased + 6 :]
     rows, width = second.shape
     ff = down_w.shape[1]
     at = pl.program_id(0)
@@ -611,6 +705,8 @@
         grad_gates[...] = jnp.zeros_like(grad_gates)
         comb_sum[...] = jnp.zeros_like(comb_sum)
         back_sum[...] = jnp.zeros_like(back_sum)
+        dy[...] = side[:, :width]
+        second_t[...] = second[...].T
 
     mine = lane == first_expert[0] + at
     gate = jnp.sum(jnp.where(mine, gates[...], 0.0), axis=1, keepdims=True)
@@ -625,16 +721,17 @@
         silu_gate = gate_part * sigmoid_gate
         hidden = (silu_gate * up_part).astype(BF16).astype(F32)
         grad_col += jnp.sum(hidden * came, axis=1, keepdims=True)
-        gated[0, 0, :, tile] = (hidden * gate).astype(BF16)
+        gated[:, tile] = (hidden * gate).astype(BF16)
+        gated_t[0, tile, :] = gated[:, tile].T
         grad_hidden = came * gate
         slope = sigmoid_gate + silu_gate * (1.0 - sigmoid_gate)
-        grad_both[0, 0, :, tile] = (grad_hidden * up_part * slope).astype(BF16)
-        grad_both[0, 0, :, up_tile] = (grad_hidden * silu_gate).astype(BF16)
+        grad_both[0, :, tile] = (grad_hidden * up_part * slope).astype(BF16)
+        grad_both[0, :, up_tile] = (grad_hidden * silu_gate).astype(BF16)
     grad_gates[...] += jnp.where(mine, grad_col, 0.0)
     for start in range(0, width, TILE):
         tile = slice(start, start + TILE)
-        comb_sum[:, tile] += dot(gated[0, 0], down_w[0, :, tile])
-        back_sum[:, tile] += dot_nt(grad_both[0, 0], in_w[0, tile, :])
+        comb_sum[:, tile] += dot(gated[...], down_w[0, :, tile])
+        back_sum[:, tile] += dot_nt(grad_both[0], in_w[0, tile, :])
 
     @pl.when(at == pl.num_programs(0) - 1)
     def _():
@@ -657,14 +754,18 @@
         pl.BlockSpec((1, ff, width), lambda e: (e, 0, 0)),
     ] + [pl.BlockSpec(memory_space=pl.ANY)] * len(before)
     out_specs = [
-        pl.BlockSpec((1, 1, rows, ff), lambda e: (e, place, 0, 0)),
-        pl.BlockSpec((1, 1, rows, 2 * ff), lambda e: (e, place, 0, 0)),
+        pl.BlockSpec((1, ff, rows), lambda e: (e, 0, place)),
+        pl.BlockSpec((1, rows, 2 * ff), lambda e: (e, place, 0)),
+        pl.BlockSpec((width, rows), lambda e: (0, place)),
+        pl.BlockSpec((rows, width), lambda e: (place, 0)),
         whole(rows, width),
         whole(*side.shape),
     ]
     outs = [
-        shape_of((experts, count, rows, ff), BF16),
-        shape_of((experts, count, rows, 2 * ff), BF16),
+        shape_of((experts, ff, count * rows), BF16),
+        shape_of((experts, count * rows, 2 * ff), BF16),
+        shape_of((width, count * rows), BF16),
+        shape_of((count * rows, width), BF16),
         shape_of((rows, width), BF16),
         shape_of(side.shape, BF16),
     ]
@@ -679,13 +780,52 @@
             pltpu.VMEM((rows, PAD), F32),
             pltpu.VMEM((rows, width), F32),
             pltpu.VMEM((rows, width), F32),
+            pltpu.VMEM((rows, ff), BF16),
         ],
-        input_output_aliases={6: 0, 7: 1} if before else {},
+        input_output_aliases={6: 0, 7: 1, 8: 2, 9: 3} if before else {},
         compiler_params=pltpu.CompilerParams(
             vmem_limit_bytes=VMEM_BYTES, dimension_semantics=("arbitrary",)
         ),
         cost_estimate=LIGHT,
     )(first_expert, second, side, small, in_w, down_w, *before)
+
+
+def weight_kernel(base, second_t, dy, gated_t, grad_both, grad_in, grad_down):
+    @pl.loop(0, grad_in.shape[1] // TILE)
+    def _(j):
+        grad_in[:, tile_at(j)] = dot(second_t[...], grad_both[0, :, tile_at(j)]).astype(BF16)
+
+    @pl.loop(0, grad_down.shape[1] // TILE)
+    def _(j):
+        grad_down[:, tile_at(j)] = dot(gated_t[0], dy[:, tile_at(j)]).astype(BF16)
+
+
+def weight_block(base, second_t, dy, gated_t, grad_both, experts):
+    width, rows = second_t.shape
+    ff = gated_t.shape[1]
+    grid_spec = pltpu.PrefetchScalarGridSpec(
+        num_scalar_prefetch=1,
+        grid=(experts,),
+        in_specs=[
+            pl.BlockSpec((width, rows), lambda e, at: (0, 0)),
+            pl.BlockSpec((rows, width), lambda e, at: (0, 0)),
+            pl.BlockSpec((1, ff, rows), lambda e, at: (at[0] + e, 0, 0)),
+            pl.BlockSpec((1, rows, 2 * ff), lambda e, at: (at[0] + e, 0, 0)),
+        ],
+        out_specs=[
+            pl.BlockSpec((width, 2 * ff), lambda e, at: (e, 0)),
+            pl.BlockSpec((ff, width), lambda e, at: (e, 0)),
+        ],
+    )
+    return pl.pallas_call(
+        weight_kernel,
+        grid_spec=grid_spec,
+        out_shape=[shape_of((experts * width, 2 * ff), BF16), shape_of((experts * ff, width), BF16)],
+        compiler_params=pltpu.CompilerParams(
+            vmem_limit_bytes=VMEM_BYTES, dimension_semantics=("arbitrary",)
+        ),
+        cost_estimate=LIGHT,
+    )(base[None].astype(jnp.int32), second_t, dy, gated_t, grad_both)
 
 
 def shift(block, count, step):
@@ -716,10 +856,10 @@
     return shift(far[:half], count, -1), shift(far[half:], count, 1)
 
 
-def near_rest(parts, left, right, count):
+def near_rest(parts, left, right, count, after=()):
     half = parts[0].shape[0] // 2
     if count == 2:
-        return jnp.concatenate([left, right], axis=0), jnp.zeros_like(parts[0])
+        return jnp.concatenate([left, right], axis=0), jnp.zeros_like(parts[0]), after
     for step in reversed(range(1, count // 2)):
         near, far = parts[step], parts[count - step]
         if step == count // 2 - 1:
@@ -727,8 +867,10 @@
             right = jnp.concatenate([far[:half], add_low(far[half:], right)], axis=0)
         else:
             left, right = add_low(near, left), add_low(far, right)
+        if step == 1:
+            left, right, after = tie(left, right, after)
         left, right = shift(left, count, -1), shift(right, count, 1)
-    return left, right
+    return left, right, after
 
 
 def add_low(a, b):
@@ -823,12 +965,6 @@
     shard_at = lax.axis_index("shard")
     reps, shard_count = (lax.axis_size("rep"), lax.axis_size("shard"))
 
-    mask_own = jnp.any(
-        routes[:, :, None] == jnp.arange(PAD, dtype=jnp.int32)[None, None, :], axis=1
-    )
-    side = jnp.concatenate([cotangent, mask_own.astype(bf16)], axis=1)
-    side_parts, side_right, side_left = gather_near(side, shard_count)
-
     small = jnp.concatenate(
         [
             w_router,
@@ -838,8 +974,9 @@
         ],
         axis=1,
     )
-    all_w = gather_all(
-        jnp.concatenate([w_query, w_key, w_value, w_out, small], axis=1), reps, shard_count, 1
+    weights = [w_query, w_key, w_value, w_out, small]
+    all_w, side, side_right, side_left = gather_all(
+        weights, cotangent, routes, reps, shard_count, 1
     )
     small_at = query_cols + 2 * kv_cols + w_out.shape[1]
 
@@ -847,8 +984,15 @@
     cosine, sine_table = cosine[:, 0, :], sine_table[:, 0, :]
     ct = jnp.concatenate([cosine] * 4, axis=1)
     st = jnp.concatenate([-sine_table, sine_table] * 2, axis=1)
-    all_w, side_parts, side_right, side_left = tie(all_w, side_parts, side_right, side_left)
-    side_far = gather_far(side_right, side_left, shard_count)
+    side_parts = {0: side}
+    for step in range(1, (shard_count - 1) // 2 + 1):
+        if step > 1:
+            side_right, side_left = shift(side_right, shard_count, 1), shift(side_left, shard_count, -1)
+        side_parts[step], side_parts[shard_count - step] = side_right, side_left
+    if shard_count > 2:
+        side_far = gather_far(side_right, side_left, shard_count)
+    else:
+        side_far = (side_right,)
     second_low, middle, *kept = forward_block(
         tokens, all_w, ct, st, doc_ids, query_cols, kv_cols
     )
@@ -863,7 +1007,7 @@
     combs, backs, kept_parts = {}, {}, ()
     back_far = None
     for place, k in enumerate(order):
-        gated, grad_both, combs[k], backs[k] = expert_block(
+        *kept_parts, combs[k], backs[k] = expert_block(
             first_expert,
             second_parts[k],
             side_parts[k],
@@ -875,69 +1019,70 @@
             kept_parts,
         )
         if k == 0:
-            gated, grad_both, second_parts, ends = tie(gated, grad_both, second_parts, ends)
+            kept_parts, second_parts, ends = tie(kept_parts, second_parts, ends)
             second_parts[far_at] = jnp.concatenate(gather_far(*ends, shard_count))
-        kept_parts = (gated, grad_both)
         if k == far_at:
             back_far = far_first(backs, shard_count)
         elif back_far is not None:
-            gated, grad_both, back_far, backs = tie(gated, grad_both, back_far, backs)
-            kept_parts = (gated, grad_both)
-    back_near = near_rest(backs, *back_far, shard_count)
-    group_rows = shard_count * row_count
-    second_all = jnp.concatenate([second_parts[k] for k in order])
-    dy_all = jnp.concatenate([side_parts[k][:, :model_width] for k in order])
-    grad_in_here = jnp.einsum(
-        "td,etf->edf",
-        second_all,
-        grad_both.reshape(own_experts, group_rows, 2 * ff),
-        preferred_element_type=f32,
-    ).astype(bf16)
-    grad_down_here = jnp.einsum(
-        "etf,td->efd",
-        gated.reshape(own_experts, group_rows, ff),
-        dy_all,
-        preferred_element_type=f32,
-    ).astype(bf16)
+            kept_parts, back_far, backs = tie(kept_parts, back_far, backs)
+    *back_near, kept_parts = near_rest(backs, *back_far, shard_count, kept_parts)
+    gated_t, grad_both, second_t, dy_all = kept_parts
 
     rep_at = lax.axis_index("rep")
     bits = reps.bit_length() - 1
     bit_of = [rep_at // 2**bit % 2 for bit in range(bits)]
-    grads = [g.reshape(-1, model_width) for g in (grad_in_here, grad_down_here)]
-    away = jnp.concatenate([part_of(g, 1 - bit_of[0]) for g in grads])
-    mine = jnp.concatenate([part_of(g, bit_of[0]) for g in grads])
-    held = add_low(mine, across(away, reps, 0))
-    back_near, held, combs = tie(back_near, held, combs)
+    half = own_experts // 2
+    grads = (second_t, dy_all, gated_t, grad_both)
+    away = weight_block((1 - bit_of[0]) * half, *grads, half)
+    core = [across(part, reps, 0) for part in away]
+    away, grads = tie(away, grads)
+    mine = weight_block(bit_of[0] * half, *grads, half)
+    in_rows, down_rows = [part.shape[0] for part in mine]
+    cut = (in_rows + down_rows) // 2
+    held_in, held_down = [add_low(a, b) for a, b in zip(mine, core)]
+    blocks = [held_in[:cut], jnp.concatenate([held_in[cut:], held_down])]
+    block_orders = orders_of(bits)
+    steps = bits - 1
+    turns = [("sum", at) for at in range(steps)] + [("copy", at) for at in reversed(range(steps))]
+
+    def begin(turn, blocks):
+        kind, at = turn
+        send = sent if kind == "sum" else lambda b, n, bit, _: across(b, n, bit)
+        return [send(b, reps, o[at], bit_of) for b, o in zip(blocks, block_orders)]
+
+    def finish(turn, blocks, came):
+        kind, at = turn
+        if kind == "sum":
+            return [kept_sum(b, c, o[at], bit_of) for b, c, o in zip(blocks, came, block_orders)]
+        return [both_halves(b, c, bit_of[o[at]]) for b, c, o in zip(blocks, came, block_orders)]
+
+    came = begin(turns[0], blocks)
+    back_near, blocks, combs = tie(back_near, blocks, combs)
     comb_far = far_first(combs, shard_count)
-    cut = held.shape[0] // 2
-    blocks, block_orders = [held[:cut], held[cut:]], orders_of(bits)
-    steps = bits - 1
-    came = [sent(b, reps, o[0], bit_of) for b, o in zip(blocks, block_orders)]
-    joint, grad_tokens = backward_block(
+    middle_back = backward_block(
         tokens, side, middle, second_low, (backs[0], *back_near), all_w, ct, st, doc_ids, kept
     )
-    joint, came, comb_far, blocks, combs = tie(joint, came, comb_far, blocks, combs)
-    comb_near = near_rest(combs, *comb_far, shard_count)
-    blocks = [kept_sum(b, c, o[0], bit_of) for b, c, o in zip(blocks, came, block_orders)]
+    middle_back, came, comb_far, blocks, combs = tie(middle_back, came, comb_far, blocks, combs)
+    *comb_near, _ = near_rest(combs, *comb_far, shard_count)
+    blocks = finish(turns[0], blocks, came)
+    middle_back, blocks = tie(middle_back, blocks)
+    came = begin(turns[1], blocks)
+    grad_out, rows_t, grad_middle, grad_pre = middle_back
+    joint, grad_tokens = finish_block(
+        tokens, all_w, grad_middle, grad_pre, grad_out, rows_t, kept[0]
+    )
+    joint, came, blocks = tie(joint, came, blocks)
+    blocks = finish(turns[1], blocks, came)
     joint, blocks = tie(joint, blocks)
-    came = [sent(b, reps, o[1], bit_of) for b, o in zip(blocks, block_orders)]
+    came = begin(turns[2], blocks)
     joint_own = reduce_all(joint, reps, shard_count, 3)
     joint_own, blocks, comb_near, came = tie(joint_own, blocks, comb_near, came)
     mixed = middle + combs[0].astype(f32) + sum(part.astype(f32) for part in comb_near)
     mixed = mixed.astype(bf16)
-    blocks = [kept_sum(b, c, o[1], bit_of) for b, c, o in zip(blocks, came, block_orders)]
-    for at in range(2, steps):
-        blocks = [
-            kept_sum(b, sent(b, reps, o[at], bit_of), o[at], bit_of)
-            for b, o in zip(blocks, block_orders)
-        ]
-    for at in reversed(range(steps)):
-        blocks = [
-            both_halves(b, across(b, reps, o[at]), bit_of[o[at]])
-            for b, o in zip(blocks, block_orders)
-        ]
+    blocks = finish(turns[2], blocks, came)
+    for turn in turns[3:]:
+        blocks = finish(turn, blocks, begin(turn, blocks))
     others = [across(b, reps, 0) for b in blocks]
-    in_rows, down_rows = [g.shape[0] // 2 for g in grads]
     grad_in_own = place_half(*blocks, 0, in_rows, None, bit_of[0])
     grad_down_own = place_half(*blocks, in_rows, down_rows, None, bit_of[0])
     grad_in_own = place_half(*others, 0, in_rows, grad_in_own, 1 - bit_of[0])

time: 633 us -> 554 us (0.88)
  waiting for transfers between devices: 113 us -> 68.6 us
  Pallas kernels: 345 us -> 380 us
  matrix products: 31.8 us -> 0 us
  local copies, waits for them, and re-layouts: 43.5 us -> 18.8 us
  other arithmetic: 50.8 us -> 40.4 us
    pallas_call x0 -> x2, Pallas kernels: none -> 46.1 us  [weight_block(): pl.pallas_call(weight_kernel, grid_spec=grid_spec, out_shape=[shape_of((e...]
    dot_general x2 -> x0, matrix products: 31.8 us -> none  [the longest x1 22.5 us: shards(): jnp.einsum('td,etf->edf', second_all, grad_both.reshape(own_experts, grou...]
    ppermute x16 -> x14, waiting for transfers between devices: 59.3 us -> 33.7 us  [shift(): lax.ppermute(block, 'shard', [(at, (at + step) % count) for at in range(c...]
    ppermute x11 -> x12, waiting for transfers between devices: 53.7 us -> 34.9 us  [across(): lax.ppermute(block, 'rep', [(at, at ^ 2 ** bit) for at in range(reps)])]
    pallas_call x1, Pallas kernels: 99.7 us -> 81.1 us  [gather_all(): pl.pallas_call(lambda *refs: gather_kernel(reps, shard_count, *refs), out...]
    dynamic_slice x6 -> x3, local copies, waits for them, and re-layouts: 11.4 us -> 1.38 us  [part_of(): return lax.dynamic_slice_in_dim(block, index * half, half, axis=0)]
    ppermute x16 -> x14, starting transfers between devices: 30.8 us -> 22.6 us  [shift(): lax.ppermute(block, 'shard', [(at, (at + step) % count) for at in range(c...]
    convert_element_type x9 -> x10, other arithmetic: 22.4 us -> 14.7 us  [add_low(): return (a.astype(F32) + b.astype(F32)).astype(BF16)]
  transfers between devices with their start and end apart: 27 -> 26, of which waited for: 7 -> 5; matrix products, arithmetic and copies ran while one was open for 9% -> 7% of each run, Pallas kernels for 50% -> 45%
where the time goes in v3:
time: 554 us; the launch traced here: 546 us
  Pallas kernels  380 us (69%)
  waiting for transfers between devices  68.6 us (12%)
  other arithmetic  40.4 us (7%)
  starting transfers between devices  36.1 us (7%)
  local copies, waits for them, and re-layouts  18.8 us (3%)
    pallas_call x4, Pallas kernels, expert_block(): pl.pallas_call(lambda *refs: expert_kernel(bool(before), *refs), grid=(ex...  83.3 us
    pallas_call x1, Pallas kernels, gather_all(): pl.pallas_call(lambda *refs: gather_kernel(reps, shard_count, *refs), out...  81.1 us
    pallas_call x4, Pallas kernels, local_call(): pl.pallas_call(kernel, out_shape=outs, in_specs=[pl.BlockSpec(memory_spac...  76.3 us
    pallas_call x1, Pallas kernels, reduce_all(): pl.pallas_call(lambda *refs: reduce_kernel(reps, shard_count, *refs), out...  69.6 us
    pallas_call x2, Pallas kernels, weight_block(): pl.pallas_call(weight_kernel, grid_spec=grid_spec, out_shape=[shape_of((e...  46.1 us
    ppermute x12, waiting for transfers between devices, across(): lax.ppermute(block, 'rep', [(at, at ^ 2 ** bit) for at in range(reps)])  34.9 us
    ppermute x14, waiting for transfers between devices, shift(): lax.ppermute(block, 'shard', [(at, (at + step) % count) for at in range(c...  33.7 us
    pallas_call x4, Pallas kernels, place_half(): pl.pallas_call(lambda *refs: place_kernel(first, cut, *refs), grid_spec=g...  23.9 us
  transfers between devices with their start and end apart: 26, of which 5 were waited for; matrix products, arithmetic and copies ran while one was open for 7% of the time, Pallas kernels for 45%

profile of v3, /device:TPU:0, one launch (start us, length us, event | category | flops | bytes accessed | tf_op | source)
XLA Modules:
  0.0 545.7 jit_solution(11391361279112848692)
XLA Ops:
  5.6 81.1 %shard_map.212 = (bf16[4,8,32,3200]{3,2,1,0:T(8,128)(2,1)}, bf16[512,1152]{1,0:T(8,128)(2,1)}, bf16[512,1152]{1,0:T(8,128)(2,1)}, bf16[512,1152]{1,0:T(8,128)(2,1)}) custom-call(bf16[8,32,1024]{2,1,0:T(8,128)(2,1)} %bitcast.27, bf16[8,32,512]{2,1,0:T(8,128)(2,1)} %bitcast.29, bf16[8,32,512]{2,1,0:T(8,128)(2,1)} %bitcast.30, bf16[8,32,1024]{2,1,0:T(8,128)(2,1)} %bitcast.28, ...), custom_call_target="tpu_custom_call" | custom-call | bytes 3276800 | tf_op jit(solution)/shard_map/pallas_call | solution.py:204
  89.0 3.8 collective-permute-start.1
  96.2 25.2 %shard_map.213 = (bf16[512,1024]{1,0:T(8,128)(2,1)}, f32[512,1024]{1,0:T(8,128)}, bf16[1024,512]{1,0:T(8,128)(2,1)}, bf16[512,1024]{1,0:T(8,128)(2,1)}, bf16[512...) custom-call(bf16[512,1024]{1,0:T(8,128)(2,1)} %tokens.5, ...), custom_call_target="tpu_custom_call" | custom-call | flops 1000000 | bytes 100000 | tf_op jit(solution)/shard_map/pallas_call | solution.py:492
  121.5 4.0 collective-permute-start.3
  127.2 20.9 %shard_map.214 = (bf16[4,512,2048]{2,1,0:T(8,128)(2,1)}, bf16[4,2048,1024]{2,1,0:T(8,128)(2,1)}, bf16[1024,2048]{1,0:T(8,128)(2,1)}, bf16[2048,1024]{1,0:T(8,128...) custom-call(s32[1]{0:T(128)} %bitcast.8.refs_0_, bf16[512,1024]{1,0:T(8,128)(2,1)} %get-tuple-element.142.refs_1_.second, ...), custom_call_target="tpu_custom_call" | custom-call | flops 1000000 | bytes 100000 | tf_op jit(solution)/shard_map/pallas_call | solution.py:772
  149.6 17.9 %collective-permute-done.3.refs_1_ = bf16[512,1024]{1,0:T(8,128)(2,1)S(1)} collective-permute-done((bf16[512,1024]{1,0:T(8,128)(2,1)}, bf16[512,1024]{1,0:T(8,128)(2,1)S(1)}, u32[]{:S(2)}, u32[]{:S(2)}) %collective-permute-start.3) | collective-permute-done | bytes 1048608 | tf_op jit(solution)/shard_map/ppermute | solution.py:832
  170.8 20.8 %shard_map.215 = (bf16[4,512,2048]{2,1,0:T(8,128)(2,1)}, bf16[4,2048,1024]{2,1,0:T(8,128)(2,1)}, bf16[1024,2048]{1,0:T(8,128)(2,1)}, bf16[2048,1024]{1,0:T(8,128...) custom-call(s32[1]{0:T(128)} %bitcast.8.refs_0_, ...), custom_call_target="tpu_custom_call", output_to_operand_aliasing={{0}: (6, {}), {1}: (7, {}), {2}: (8, {}), {3}: (9, {})} | custom-call | flops 1000000 | bytes 100000 | tf_op jit(solution)/shard_map/pallas_call | solution.py:772
  192.7 20.8 %shard_map.216 = (bf16[4,512,2048]{2,1,0:T(8,128)(2,1)}, bf16[4,2048,1024]{2,1,0:T(8,128)(2,1)}, bf16[1024,2048]{1,0:T(8,128)(2,1)}, bf16[2048,1024]{1,0:T(8,128...) custom-call(s32[1]{0:T(128)} %bitcast.8.refs_0_, ...), custom_call_target="tpu_custom_call", output_to_operand_aliasing={{0}: (6, {}), {1}: (7, {}), {2}: (8, {}), {3}: (9, {})} | custom-call | flops 1000000 | bytes 100000 | tf_op jit(solution)/shard_map/pallas_call | solution.py:772
  214.8 3.7 collective-permute-start.6
  218.8 20.9 %shard_map.217 = (bf16[4,512,2048]{2,1,0:T(8,128)(2,1)}, bf16[4,2048,1024]{2,1,0:T(8,128)(2,1)}, bf16[1024,2048]{1,0:T(8,128)(2,1)}, bf16[2048,1024]{1,0:T(8,128...) custom-call(s32[1]{0:T(128)} %bitcast.8.refs_0_, ...), custom_call_target="tpu_custom_call", output_to_operand_aliasing={{0}: (6, {}), {1}: (7, {}), {2}: (8, {}), {3}: (9, {})} | custom-call | flops 1000000 | bytes 100000 | tf_op jit(solution)/shard_map/pallas_call | solution.py:772
  245.6 23.1 %shard_map.218 = (bf16[2048,1024]{1,0:T(8,128)(2,1)}, bf16[1024,1024]{1,0:T(8,128)(2,1)}) custom-call(s32[1]{0:T(128)} %bitcast.10.base, bf16[1024,2048]{1,0:T(8,128)(2,1)} %get-tuple-element.190.second_t, bf16[2048,1024]{1,0:T(8,128)(2,1)} %get-tuple-element.191.dy, bf16[4,512,2048]{2,1,0:T(8,128)(2,1)} %get-tuple-element.192.gated_t, ...), custom_call_target="tpu_custom_call" | custom-call | flops 1000000 | bytes 100000 | tf_op jit(solution)/shard_map/pallas_call | solution.py:820
  271.6 23.1 %shard_map.219 = (bf16[2048,1024]{1,0:T(8,128)(2,1)}, bf16[1024,1024]{1,0:T(8,128)(2,1)}) custom-call(s32[1]{0:T(128)} %bitcast.9.base, bf16[1024,2048]{1,0:T(8,128)(2,1)} %get-tuple-element.190.second_t, bf16[2048,1024]{1,0:T(8,128)(2,1)} %get-tuple-element.191.dy, bf16[4,512,2048]{2,1,0:T(8,128)(2,1)} %get-tuple-element.192.gated_t, ...), custom_call_target="tpu_custom_call" | custom-call | flops 1000000 | bytes 100000 | tf_op jit(solution)/shard_map/pallas_call | solution.py:820
  297.4 4.3 add_convert_fusion
  312.1 11.0 %collective-permute-done.9.back_right = bf16[512,1152]{1,0:T(8,128)(2,1)} collective-permute-done((bf16[512,1152]{1,0:T(8,128)(2,1)}, bf16[512,1152]{1,0:T(8,128)(2,1)}, u32[]{:S(2)}, u32[]{:S(2)}) %collective-permute-start.9) | collective-permute-done | bytes 1179680 | tf_op jit(solution)/shard_map/ppermute | solution.py:832
  326.3 31.2 %shard_map.220 = (bf16[1024,1024]{1,0:T(8,128)(2,1)}, f32[128,1024]{1,0:T(8,128)}, f32[512,1024]{1,0:T(8,128)}, bf16[512,2048]{1,0:T(8,128)(2,1)}) custom-call(bf16[512,1024]{1,0:T(8,128)(2,1)} %tokens.5, bf16[512,1152]{1,0:T(8,128)(2,1)} %get-tuple-element.138.refs_2_.side, f32[512,1024]{1,0:T(8,128)} %get-tuple-element.137.middle, ...), custom_call_target="tpu_custom_call" | custom-call | flops 1000000 | bytes 100000 | tf_op jit(solution)/shard_map/pallas_call | solution.py:492
  370.7 3.8 collective-permute-start.18
  374.7 16.8 %shard_map.221 = (bf16[1024,3200]{1,0:T(8,128)(2,1)}, f32[512,1024]{1,0:T(8,128)}) custom-call(bf16[512,1024]{1,0:T(8,128)(2,1)} %tokens.5, bf16[1024,3200]{1,0:T(8,128)(2,1)} %bitcast.22, f32[512,1024]{1,0:T(8,128)} %get-tuple-element.226.grad_middle, bf16[512,2048]{1,0:T(8,128)(2,1)} %get-tuple-element.227.grad_pre, ...), custom_call_target="tpu_custom_call" | custom-call | flops 1000000 | bytes 100000 | tf_op jit(solution)/shard_map/pallas_call | solution.py:492
  393.4 69.6 %shard_map.222 = bf16[1,8,32,3200]{3,2,1,0:T(8,128)(2,1)} custom-call(bf16[4,8,32,3200]{3,2,1,0:T(8,128)(2,1)} %bitcast.24), custom_call_target="tpu_custom_call" | custom-call | bytes 3276800 | tf_op jit(solution)/shard_map/pallas_call | solution.py:322
  469.3 34.9 %collective-permute-done.22 = bf16[768,1024]{1,0:T(8,128)(2,1)} collective-permute-done((bf16[768,1024]{1,0:T(8,128)(2,1)}, bf16[768,1024]{1,0:T(8,128)(2,1)}, u32[]{:S(2)}, u32[]{:S(2)}) %collective-permute-start.22) | collective-permute-done | bytes 1572896 | tf_op jit(solution)/shard_map/ppermute | solution.py:881
  517.4 4.2 add_convert_fusion.4
  521.6 7.6 %shard_map.224.refs_3_ = f32[4096,1024]{1,0:T(8,128)} custom-call(s32[1]{0:T(128)} %bitcast.14.refs_0_, bf16[1536,1024]{1,0:T(8,128)(2,1)} %copy-done, bf16[1536,1024]{1,0:T(8,128)(2,1)} %pad_maximum_fusion.2.refs_2_), custom_call_target="tpu_custom_call" | custom-call | flops 1000000 | bytes 100000 | tf_op jit(solution)/shard_map/pallas_call | solution.py:932
  529.2 4.4 shard_map.226.refs_3_
  533.5 7.6 %shard_map.225 = f32[4096,1024]{1,0:T(8,128)} custom-call(s32[1]{0:T(128)} %bitcast.13.refs_0_, bf16[1536,1024]{1,0:T(8,128)(2,1)} %collective-permute-done.23.refs_1_, bf16[1536,1024]{1,0:T(8,128)(2,1)} %collective-permute-done.25.refs_2_, f32[4096,1024]{1,0:T(8,128)} %shard_map.224.refs_3_), custom_call_target="tpu_custom_call", output_to_operand_aliasing={{}: (3, {})} | custom-call | flops 1000000 | bytes 100000 | tf_op jit(solution)/shard_map/pallas_call | solution.py:932
  541.2 4.4 shard_map.227
  (128 shorter events, 79.6 us)
Async XLA Ops:
  87.8 33.6 %collective-permute-start = (bf16[256,1152]{1,0:T(8,128)(2,1)S(1)}, bf16[256,1152]{1,0:T(8,128)(2,1)S(1)}, u32[]{:S(2)}, u32[]{:S(2)}) collective-permute-start(bf16[256,1152]{1,0:T(8,128)(2,1)S(1)} %slice.66), channel_id=1, source_target_pairs={{0,1},{1,2},{2,3},{3,0},{4,5},{5,6},{6,7},{7,4},{8,9},{9,10},{10,1... | collective-permute-start | bytes 1769480 | tf_op jit(solution)/shard_map/ppermute | solution.py:832
  89.0 32.4 %collective-permute-start.1 = (bf16[256,1152]{1,0:T(8,128)(2,1)S(1)}, bf16[256,1152]{1,0:T(8,128)(2,1)S(1)}, u32[]{:S(2)}, u32[]{:S(2)}) collective-permute-start(bf16[256,1152]{1,0:T(8,128)(2,1)S(1)} %slice.67), channel_id=1, source_target_pairs={{0,3},{1,0},{2,1},{3,2},{4,7},{5,4},{6,5},{7,6},{8,11},{9,8},{10,9... | collective-permute-start | bytes 1769480 | tf_op jit(solution)/shard_map/ppermute | solution.py:832
  121.5 28.2 %collective-permute-start.2 = (bf16[512,1024]{1,0:T(8,128)(2,1)}, bf16[512,1024]{1,0:T(8,128)(2,1)S(1)}, u32[]{:S(2)}, u32[]{:S(2)}) collective-permute-start(bf16[512,1024]{1,0:T(8,128)(2,1)} %get-tuple-element.142.refs_1_.second), channel_id=1, source_target_pairs={{0,1},{1,2},{2,3},{3,0},{4,5},{5,6},{6,7},{7,4},{8,9},{9,10},{10,1... | collective-permute-start | bytes 3145736 | tf_op jit(solution)/shard_map/ppermute | solution.py:832
  121.5 46.0 %collective-permute-start.3 = (bf16[512,1024]{1,0:T(8,128)(2,1)}, bf16[512,1024]{1,0:T(8,128)(2,1)S(1)}, u32[]{:S(2)}, u32[]{:S(2)}) collective-permute-start(bf16[512,1024]{1,0:T(8,128)(2,1)} %get-tuple-element.142.refs_1_.second), channel_id=1, source_target_pairs={{0,3},{1,0},{2,1},{3,2},{4,7},{5,4},{6,5},{7,6},{8,11},{9,8},{10,9... | collective-permute-start | bytes 3145736 | tf_op jit(solution)/shard_map/ppermute | solution.py:832
  167.5 24.1 %collective-permute-start.5 = (bf16[256,1024]{1,0:T(8,128)(2,1)S(1)}, bf16[256,1024]{1,0:T(8,128)(2,1)S(1)}, u32[]{:S(2)}, u32[]{:S(2)}) collective-permute-start(bf16[256,1024]{1,0:T(8,128)(2,1)S(1)} %slice.70), channel_id=1, source_target_pairs={{0,3},{1,0},{2,1},{3,2},{4,7},{5,4},{6,5},{7,6},{8,11},{9,8},{10,9... | collective-permute-start | bytes 1572872 | tf_op jit(solution)/shard_map/ppermute | solution.py:832
  214.8 24.9 %collective-permute-start.6 = (bf16[256,1152]{1,0:T(8,128)(2,1)S(1)}, bf16[256,1152]{1,0:T(8,128)(2,1)S(1)}, u32[]{:S(2)}, u32[]{:S(2)}) collective-permute-start(bf16[256,1152]{1,0:T(8,128)(2,1)S(1)} %get-tuple-element.316), channel_id=1, source_target_pairs={{0,3},{1,0},{2,1},{3,2},{4,7},{5,4},{6,5},{7,6},{8,11},{9,8},{10,9... | collective-permute-start | bytes 1769480 | tf_op jit(solution)/shard_map/ppermute | solution.py:832
  218.6 24.4 %collective-permute-start.7 = (bf16[256,1152]{1,0:T(8,128)(2,1)S(1)}, bf16[256,1152]{1,0:T(8,128)(2,1)S(1)}, u32[]{:S(2)}, u32[]{:S(2)}) collective-permute-start(bf16[256,1152]{1,0:T(8,128)(2,1)S(1)} %get-tuple-element.315), channel_id=1, source_target_pairs={{0,1},{1,2},{2,3},{3,0},{4,5},{5,6},{6,7},{7,4},{8,9},{9,10},{10,1... | collective-permute-start | bytes 1769480 | tf_op jit(solution)/shard_map/ppermute | solution.py:832
  268.7 28.7 %collective-permute-start.10 = (bf16[2048,1024]{1,0:T(8,128)(2,1)}, bf16[2048,1024]{1,0:T(8,128)(2,1)}, u32[]{:S(2)}, u32[]{:S(2)}) collective-permute-start(bf16[2048,1024]{1,0:T(8,128)(2,1)} %get-tuple-element.188), channel_id=1, source_target_pairs={{0,4},{4,0},{8,12},{12,8},{16,20},{20,16},{24,28},{28,24},{1,5},{5... | collective-permute-start | bytes 12582920 | tf_op jit(solution)/shard_map/ppermute | solution.py:881
  268.7 26.0 %collective-permute-start.11 = (bf16[1024,1024]{1,0:T(8,128)(2,1)}, bf16[1024,1024]{1,0:T(8,128)(2,1)S(1)}, u32[]{:S(2)}, u32[]{:S(2)}) collective-permute-start(bf16[1024,1024]{1,0:T(8,128)(2,1)} %get-tuple-element.189), channel_id=1, source_target_pairs={{0,4},{4,0},{8,12},{12,8},{16,20},{20,16},{24,28},{28,24},{1,5},{5... | collective-permute-start | bytes 6291464 | tf_op jit(solution)/shard_map/ppermute | solution.py:881
  269.2 42.9 %collective-permute-start.8 = (bf16[512,1152]{1,0:T(8,128)(2,1)}, bf16[512,1152]{1,0:T(8,128)(2,1)}, u32[]{:S(2)}, u32[]{:S(2)}) collective-permute-start(bf16[512,1152]{1,0:T(8,128)(2,1)} %pad_maximum_fusion.6), channel_id=1, source_target_pairs={{0,3},{1,0},{2,1},{3,2},{4,7},{5,4},{6,5},{7,6},{8,11},{9,8},{10,9... | collective-permute-start | bytes 3538952 | tf_op jit(solution)/shard_map/ppermute | solution.py:832
  271.1 51.9 %collective-permute-start.9 = (bf16[512,1152]{1,0:T(8,128)(2,1)}, bf16[512,1152]{1,0:T(8,128)(2,1)}, u32[]{:S(2)}, u32[]{:S(2)}) collective-permute-start(bf16[512,1152]{1,0:T(8,128)(2,1)} %pad_maximum_fusion.7), channel_id=1, source_target_pairs={{0,1},{1,2},{2,3},{3,0},{4,5},{5,6},{6,7},{7,4},{8,9},{9,10},{10,1... | collective-permute-start | bytes 3538952 | tf_op jit(solution)/shard_map/ppermute | solution.py:832
  303.4 54.1 %collective-permute-start.12 = (bf16[768,1024]{1,0:T(8,128)(2,1)}, bf16[768,1024]{1,0:T(8,128)(2,1)}, u32[]{:S(2)}, u32[]{:S(2)}) collective-permute-start(bf16[768,1024]{1,0:T(8,128)(2,1)} %constant_dynamic-slice_fusion.2), channel_id=1, source_target_pairs={{0,8},{4,12},{8,0},{12,4},{16,24},{20,28},{24,16},{28,20},{1,9},{5... | collective-permute-start | bytes 4718600 | tf_op jit(solution)/shard_map/ppermute | solution.py:881
  307.4 50.1 %collective-permute-start.13 = (bf16[768,1024]{1,0:T(8,128)(2,1)}, bf16[768,1024]{1,0:T(8,128)(2,1)}, u32[]{:S(2)}, u32[]{:S(2)}) collective-permute-start(bf16[768,1024]{1,0:T(8,128)(2,1)} %fusion), channel_id=1, source_target_pairs={{0,16},{4,20},{8,24},{12,28},{16,0},{20,4},{24,8},{28,12},{1,17},{... | collective-permute-start | bytes 4718600 | tf_op jit(solution)/shard_map/ppermute | solution.py:881
  324.1 33.4 %collective-permute-start.14 = (bf16[256,1024]{1,0:T(8,128)(2,1)}, bf16[256,1024]{1,0:T(8,128)(2,1)}, u32[]{:S(2)}, u32[]{:S(2)}) collective-permute-start(bf16[256,1024]{1,0:T(8,128)(2,1)} %get-tuple-element.318), channel_id=1, source_target_pairs={{0,3},{1,0},{2,1},{3,2},{4,7},{5,4},{6,5},{7,6},{8,11},{9,8},{10,9... | collective-permute-start | bytes 1572872 | tf_op jit(solution)/shard_map/ppermute | solution.py:832
  326.1 31.4 %collective-permute-start.15 = (bf16[256,1024]{1,0:T(8,128)(2,1)}, bf16[256,1024]{1,0:T(8,128)(2,1)}, u32[]{:S(2)}, u32[]{:S(2)}) collective-permute-start(bf16[256,1024]{1,0:T(8,128)(2,1)} %get-tuple-element.317), channel_id=1, source_target_pairs={{0,1},{1,2},{2,3},{3,0},{4,5},{5,6},{6,7},{7,4},{8,9},{9,10},{10,1... | collective-permute-start | bytes 1572872 | tf_op jit(solution)/shard_map/ppermute | solution.py:832
  362.1 29.4 %collective-permute-start.16 = (bf16[384,1024]{1,0:T(8,128)(2,1)S(1)}, bf16[384,1024]{1,0:T(8,128)(2,1)S(1)}, u32[]{:S(2)}, u32[]{:S(2)}) collective-permute-start(bf16[384,1024]{1,0:T(8,128)(2,1)S(1)} %constant_dynamic-slice_fusion.1), channel_id=1, source_target_pairs={{0,16},{4,20},{8,24},{12,28},{16,0},{20,4},{24,8},{28,12},{1,17},{... | collective-permute-start | bytes 2359304 | tf_op jit(solution)/shard_map/ppermute | solution.py:881
  363.7 27.8 %collective-permute-start.17 = (bf16[384,1024]{1,0:T(8,128)(2,1)S(1)}, bf16[384,1024]{1,0:T(8,128)(2,1)S(1)}, u32[]{:S(2)}, u32[]{:S(2)}) collective-permute-start(bf16[384,1024]{1,0:T(8,128)(2,1)S(1)} %constant_dynamic-slice_fusion), channel_id=1, source_target_pairs={{0,8},{4,12},{8,0},{12,4},{16,24},{20,28},{24,16},{28,20},{1,9},{5... | collective-permute-start | bytes 2359304 | tf_op jit(solution)/shard_map/ppermute | solution.py:881
  370.7 92.3 %collective-permute-start.18 = (bf16[512,1024]{1,0:T(8,128)(2,1)S(1)}, bf16[512,1024]{1,0:T(8,128)(2,1)}, u32[]{:S(2)}, u32[]{:S(2)}) collective-permute-start(bf16[512,1024]{1,0:T(8,128)(2,1)S(1)} %pad_maximum_fusion.9), channel_id=1, source_target_pairs={{0,3},{1,0},{2,1},{3,2},{4,7},{5,4},{6,5},{7,6},{8,11},{9,8},{10,9... | collective-permute-start | bytes 3145736 | tf_op jit(solution)/shard_map/ppermute | solution.py:832
  374.5 88.6 %collective-permute-start.19 = (bf16[512,1024]{1,0:T(8,128)(2,1)}, bf16[512,1024]{1,0:T(8,128)(2,1)}, u32[]{:S(2)}, u32[]{:S(2)}) collective-permute-start(bf16[512,1024]{1,0:T(8,128)(2,1)} %pad_maximum_fusion.10), channel_id=1, source_target_pairs={{0,1},{1,2},{2,3},{3,0},{4,5},{5,6},{6,7},{7,4},{8,9},{9,10},{10,1... | collective-permute-start | bytes 3145736 | tf_op jit(solution)/shard_map/ppermute | solution.py:832
  392.1 71.0 %collective-permute-start.20 = (bf16[384,1024]{1,0:T(8,128)(2,1)S(1)}, bf16[384,1024]{1,0:T(8,128)(2,1)}, u32[]{:S(2)}, u32[]{:S(2)}) collective-permute-start(bf16[384,1024]{1,0:T(8,128)(2,1)S(1)} %add_convert_fusion.6), channel_id=1, source_target_pairs={{0,16},{4,20},{8,24},{12,28},{16,0},{20,4},{24,8},{28,12},{1,17},{... | collective-permute-start | bytes 2359304 | tf_op jit(solution)/shard_map/ppermute | solution.py:881
  392.2 70.9 %collective-permute-start.21 = (bf16[384,1024]{1,0:T(8,128)(2,1)S(1)}, bf16[384,1024]{1,0:T(8,128)(2,1)S(1)}, u32[]{:S(2)}, u32[]{:S(2)}) collective-permute-start(bf16[384,1024]{1,0:T(8,128)(2,1)S(1)} %add_convert_fusion.5), channel_id=1, source_target_pairs={{0,8},{4,12},{8,0},{12,4},{16,24},{20,28},{24,16},{28,20},{1,9},{5... | collective-permute-start | bytes 2359304 | tf_op jit(solution)/shard_map/ppermute | solution.py:881
  466.5 37.7 %collective-permute-start.22 = (bf16[768,1024]{1,0:T(8,128)(2,1)}, bf16[768,1024]{1,0:T(8,128)(2,1)}, u32[]{:S(2)}, u32[]{:S(2)}) collective-permute-start(bf16[768,1024]{1,0:T(8,128)(2,1)} %pad_maximum_fusion.3), channel_id=1, source_target_pairs={{0,8},{4,12},{8,0},{12,4},{16,24},{20,28},{24,16},{28,20},{1,9},{5... | collective-permute-start | bytes 4718600 | tf_op jit(solution)/shard_map/ppermute | solution.py:881
  469.2 37.7 %collective-permute-start.24 = (bf16[768,1024]{1,0:T(8,128)(2,1)S(1)}, bf16[768,1024]{1,0:T(8,128)(2,1)S(1)}, u32[]{:S(2)}, u32[]{:S(2)}) collective-permute-start(bf16[768,1024]{1,0:T(8,128)(2,1)S(1)} %pad_maximum_fusion.4), channel_id=1, source_target_pairs={{0,16},{4,20},{8,24},{12,28},{16,0},{20,4},{24,8},{28,12},{1,17},{... | collective-permute-start | bytes 4718600 | tf_op jit(solution)/shard_map/ppermute | solution.py:881
  506.8 26.7 %collective-permute-start.23 = (bf16[1536,1024]{1,0:T(8,128)(2,1)S(1)}, bf16[1536,1024]{1,0:T(8,128)(2,1)}, u32[]{:S(2)}, u32[]{:S(2)}) collective-permute-start(bf16[1536,1024]{1,0:T(8,128)(2,1)S(1)} %pad_maximum_fusion.1.refs_1_), channel_id=1, source_target_pairs={{0,4},{4,0},{8,12},{12,8},{16,20},{20,16},{24,28},{28,24},{1,5},{5... | collective-permute-start | bytes 9437192 | tf_op jit(solution)/shard_map/ppermute | solution.py:881
  (15 other events, 221.8 us)

commit v4 on v3

--- a/solution.py
+++ b/solution.py
@@ -1,3 +1,5 @@
+import math
+
 import jax
 import jax.numpy as jnp
 from jax import lax
@@ -225,7 +227,34 @@
     return out.reshape(shard_count * own, width), side, right, left
 
 
-def reduce_kernel(reps, shard_count, parts, out, *scratch):
+def spread_steps(pieces, outs, orders, rep_at, shard_at, sends, recvs):
+    flying = []
+    places = [rep_place(rep_at, order) for order in orders]
+    for piece, out, place in zip(pieces, outs, places):
+        out[place] = piece[...]
+    for at in reversed(range(len(orders[0]))):
+        window = 2 ** (len(orders[0]) - 1 - at)
+        for copy in flying:
+            copy.wait()
+        flying = []
+        for half, (out, place, order) in enumerate(zip(outs, places, orders)):
+            block = out.at[pl.ds(place // window * window, window)]
+            copy = pltpu.make_async_remote_copy(
+                src_ref=block,
+                dst_ref=block,
+                send_sem=sends.at[half, at],
+                recv_sem=recvs.at[half, at],
+                device_id=(partner(rep_at, order[at]), shard_at),
+                device_id_type=MESH,
+            )
+            copy.start()
+            flying.append(copy)
+        yield
+    for copy in flying:
+        copy.wait()
+
+
+def reduce_kernel(reps, shard_count, parts, upper, lower, out, upper_out, lower_out, *scratch):
     bits = reps.bit_length() - 1
     f32 = jnp.float32
     landed = [scratch[half * bits : (half + 1) * bits] for half in range(HALVES)]
@@ -233,7 +262,7 @@
     if shard_count > 1:
         z_land, (z_send, z_recv) = (rest[:HALVES], rest[HALVES : HALVES + 2])
         rest = rest[HALVES + 2 :]
-    r_send, r_recv, sends, recvs = rest
+    r_send, r_recv, sends, recvs, s_send, s_recv = rest
     rep_at, shard_at = (lax.axis_index("rep"), lax.axis_index("shard"))
     orders = bit_orders(reps)
     columns = halves_of(parts.shape[-1])
@@ -259,6 +288,10 @@
 
     for half in range(HALVES):
         begin(half, 0)
+    steps = spread_steps(
+        (upper, lower), (upper_out, lower_out), orders_of(bits), rep_at, shard_at, s_send, s_recv
+    )
+    next(steps, None)
     for at in range(bits):
         many = reps // 2 ** (at + 1)
         for half in range(HALVES):
@@ -275,6 +308,8 @@
 
             if at + 1 < bits:
                 begin(half, at + 1)
+        if at > 0 and at + 1 < bits:
+            next(steps, None)
     copies = []
     if shard_count > 1:
         for half in range(HALVES):
@@ -302,9 +337,11 @@
         else:
             out[0, place, :, columns[half]] = landed[half][-1][0, 0]
     spread(out, orders, columns, rep_at, shard_at, sends, recvs)
-
-
-def reduce_all(parts, reps, shard_count, number):
+    for _ in steps:
+        pass
+
+
+def reduce_all(parts, upper, lower, reps, shard_count, number):
     total, width = parts.shape
     rows = total // (reps * shard_count)
     bits = reps.bit_length() - 1
@@ -318,12 +355,13 @@
     if shard_count > 1:
         scratch += [pltpu.VMEM((shard_count - 1, rows, wide), parts.dtype) for wide in widths]
         scratch += [pltpu.SemaphoreType.DMA((HALVES, shard_count)) for _ in range(2)]
-    scratch += [pltpu.SemaphoreType.DMA((HALVES, bits)) for _ in range(4)]
-    out = pl.pallas_call(
+    scratch += [pltpu.SemaphoreType.DMA((HALVES, bits)) for _ in range(6)]
+    out, *wholes = pl.pallas_call(
         lambda *refs: reduce_kernel(reps, shard_count, *refs),
-        out_shape=jax.ShapeDtypeStruct((1, reps, rows, width), parts.dtype),
-        in_specs=[pl.BlockSpec(memory_space=pltpu.VMEM)],
-        out_specs=pl.BlockSpec(memory_space=pltpu.VMEM),
+        out_shape=[jax.ShapeDtypeStruct((1, reps, rows, width), parts.dtype)]
+        + [jax.ShapeDtypeStruct((reps // 2, *piece.shape), piece.dtype) for piece in (upper, lower)],
+        in_specs=[pl.BlockSpec(memory_space=pltpu.VMEM)] * 3,
+        out_specs=[pl.BlockSpec(memory_space=pltpu.VMEM)] * 3,
         scratch_shapes=scratch,
         compiler_params=pltpu.CompilerParams(
             collective_id=number, has_side_effects=True, vmem_limit_bytes=VMEM_BYTES
@@ -331,8 +369,9 @@
         cost_estimate=pl.CostEstimate(
             flops=0, bytes_accessed=total * width, transcendentals=0
         ),
-    )(parts.reshape(shard_count, reps, rows, width))
-    return out.reshape(reps * rows, width)
+    )(parts.reshape(shard_count, reps, rows, width), upper, lower)
+    wholes = [whole.reshape(-1, whole.shape[-1]) for whole in wholes]
+    return out.reshape(reps * rows, width), wholes
 
 
 F32, BF16 = jnp.float32, jnp.bfloat16
@@ -523,7 +562,7 @@
 
 
 def backward_kernel(
-    tokens, side, middle, second, back_own, back_left, back_right, w, ct, st, doc_col, doc_row,
+    tokens, side, middle, second, back_own, left_up, right_up, left_low, right_low, w, ct, st, doc_col, doc_row,
     q8, keys, values, att_t, lse,
     grad_out, rows_t, grad_middle, grad_pre,
     bias, grad_branch, grad_att, dq_t, dk, dv,
@@ -540,12 +579,15 @@
     router_t = jnp.zeros((PAD, width), F32)
     for at in range(0, rows, LANES):
         here = slice(at, at + LANES)
+        cut = left_up.shape[0]
+        back_left, back_right = (left_up, right_up) if at < cut else (left_low, right_low)
+        there = slice(at - cut * (at >= cut), at - cut * (at >= cut) + LANES)
         mask = side[here, width:] > 0
         gates = gate_softmax(second[here, :], small, mask)
         came = (
             back_own[here, width:].astype(F32)
-            + back_left[here, width:].astype(F32)
-            + back_right[here, width:].astype(F32)
+            + back_left[there, width:].astype(F32)
+            + back_right[there, width:].astype(F32)
         )
         gate_back = jnp.where(
             lane_of(came.shape) < EXPERTS, came + pltpu.roll(came, tall - width - EXPERTS, 1), 0.0
@@ -555,8 +597,8 @@
         router_t += dot(grad_logits.T.astype(BF16), second[here, :])
         grad_second = (
             back_own[here, :width].astype(F32)
-            + back_left[here, :width].astype(F32)
-            + back_right[here, :width].astype(F32)
+            + back_left[there, :width].astype(F32)
+            + back_right[there, :width].astype(F32)
             + dot_nt(low_logits, small)
         )
         x = middle[here, :]
@@ -790,37 +832,45 @@
     )(first_expert, second, side, small, in_w, down_w, *before)
 
 
-def weight_kernel(base, second_t, dy, gated_t, grad_both, grad_in, grad_down):
-    @pl.loop(0, grad_in.shape[1] // TILE)
-    def _(j):
-        grad_in[:, tile_at(j)] = dot(second_t[...], grad_both[0, :, tile_at(j)]).astype(BF16)
-
-    @pl.loop(0, grad_down.shape[1] // TILE)
-    def _(j):
-        grad_down[:, tile_at(j)] = dot(gated_t[0], dy[:, tile_at(j)]).astype(BF16)
-
-
-def weight_block(base, second_t, dy, gated_t, grad_both, experts):
+def weight_kernel(base, second_t, dy, gated_t, grad_both, *outs):
+    def fill(grad_in, grad_down):
+        for start in range(0, grad_in.shape[1], 2 * TILE):
+            tile = slice(start, start + 2 * TILE)
+            grad_in[:, tile] = dot(second_t[...], grad_both[0, :, tile]).astype(BF16)
+            grad_down[:, tile] = dot(gated_t[0], dy[:, tile]).astype(BF16)
+
+    early = pl.program_id(0) < pl.num_programs(0) // 2
+    pl.when(early)(lambda: fill(*outs[:2]))
+    pl.when(jnp.logical_not(early))(lambda: fill(*outs[2:]))
+
+
+def weight_block(base, second_t, dy, gated_t, grad_both):
     width, rows = second_t.shape
-    ff = gated_t.shape[1]
+    experts, ff = gated_t.shape[:2]
+    half = experts // 2
+    first = lambda e, at: (jnp.minimum(e, half - 1), 0)
+    last = lambda e, at: (jnp.maximum(e - half, 0), 0)
     grid_spec = pltpu.PrefetchScalarGridSpec(
         num_scalar_prefetch=1,
         grid=(experts,),
         in_specs=[
             pl.BlockSpec((width, rows), lambda e, at: (0, 0)),
             pl.BlockSpec((rows, width), lambda e, at: (0, 0)),
-            pl.BlockSpec((1, ff, rows), lambda e, at: (at[0] + e, 0, 0)),
-            pl.BlockSpec((1, rows, 2 * ff), lambda e, at: (at[0] + e, 0, 0)),
+            pl.BlockSpec((1, ff, rows), lambda e, at: ((at[0] + e) % experts, 0, 0)),
+            pl.BlockSpec((1, rows, 2 * ff), lambda e, at: ((at[0] + e) % experts, 0, 0)),
         ],
         out_specs=[
-            pl.BlockSpec((width, 2 * ff), lambda e, at: (e, 0)),
-            pl.BlockSpec((ff, width), lambda e, at: (e, 0)),
+            pl.BlockSpec((width, 2 * ff), first),
+            pl.BlockSpec((ff, width), first),
+            pl.BlockSpec((width, 2 * ff), last),
+            pl.BlockSpec((ff, width), last),
         ],
     )
+    pair = [shape_of((half * width, 2 * ff), BF16), shape_of((half * ff, width), BF16)]
     return pl.pallas_call(
         weight_kernel,
         grid_spec=grid_spec,
-        out_shape=[shape_of((experts * width, 2 * ff), BF16), shape_of((experts * ff, width), BF16)],
+        out_shape=pair * 2,
         compiler_params=pltpu.CompilerParams(
             vmem_limit_bytes=VMEM_BYTES, dimension_semantics=("arbitrary",)
         ),
@@ -859,7 +909,7 @@
 def near_rest(parts, left, right, count, after=()):
     half = parts[0].shape[0] // 2
     if count == 2:
-        return jnp.concatenate([left, right], axis=0), jnp.zeros_like(parts[0]), after
+        return left, jnp.zeros_like(left), right, jnp.zeros_like(right), after
     for step in reversed(range(1, count // 2)):
         near, far = parts[step], parts[count - step]
         if step == count // 2 - 1:
@@ -869,8 +919,13 @@
             left, right = add_low(near, left), add_low(far, right)
         if step == 1:
             left, right, after = tie(left, right, after)
+            rows = left.shape[0]
+            split = rows // LANES * 3 // 4 * LANES
+            ends = ((0, split), (split, rows))
+            cuts = [part[start:stop] for start, stop in ends for part in (left, right)]
+            shifted = [shift(part, count, (-1, 1)[at % 2]) for at, part in enumerate(cuts)]
+            return *shifted, after
         left, right = shift(left, count, -1), shift(right, count, 1)
-    return left, right, after
 
 
 def add_low(a, b):
@@ -886,12 +941,6 @@
     return lax.dynamic_slice_in_dim(block, index * half, half, axis=0)
 
 
-def both_halves(mine, other, index):
-    first = jnp.where(index == 0, mine, other)
-    last = jnp.where(index == 0, other, mine)
-    return jnp.concatenate([first, last])
-
-
 def orders_of(bits):
     return list(range(1, bits)), list(range(1, bits))[::-1]
 
@@ -917,17 +966,18 @@
 
 
 def place_half(upper, lower, begin, rows, target, index):
-    cut, width = upper.shape[0] // TILE, upper.shape[1]
-    first, blocks = begin // TILE, rows // TILE
+    step = math.gcd(2 * TILE, upper.shape[0], begin, rows)
+    cut, width = upper.shape[0] // step, upper.shape[1]
+    first, blocks = begin // step, rows // step
     grid_spec = pltpu.PrefetchScalarGridSpec(
         num_scalar_prefetch=1,
         grid=(blocks,),
         in_specs=[
-            pl.BlockSpec((TILE, width), lambda at, half: (jnp.minimum(first + at, cut - 1), 0)),
-            pl.BlockSpec((TILE, width), lambda at, half: (jnp.maximum(first + at - cut, 0), 0)),
+            pl.BlockSpec((step, width), lambda at, half: (jnp.minimum(first + at, cut - 1), 0)),
+            pl.BlockSpec((step, width), lambda at, half: (jnp.maximum(first + at - cut, 0), 0)),
         ]
         + [pl.BlockSpec(memory_space=pl.ANY)] * (target is not None),
-        out_specs=pl.BlockSpec((TILE, width), lambda at, half: (half[0] * blocks + at, 0)),
+        out_specs=pl.BlockSpec((step, width), lambda at, half: (half[0] * blocks + at, 0)),
     )
     return pl.pallas_call(
         lambda *refs: place_kernel(first, cut, *refs),
@@ -1033,55 +1083,50 @@
     bit_of = [rep_at // 2**bit % 2 for bit in range(bits)]
     half = own_experts // 2
     grads = (second_t, dy_all, gated_t, grad_both)
-    away = weight_block((1 - bit_of[0]) * half, *grads, half)
+    *away, mine_in, mine_down = weight_block((1 - bit_of[0]) * half, *grads)
+    mine = (mine_in, mine_down)
+    away, back_early = tie(away, back_near[:2])
     core = [across(part, reps, 0) for part in away]
-    away, grads = tie(away, grads)
-    mine = weight_block(bit_of[0] * half, *grads, half)
     in_rows, down_rows = [part.shape[0] for part in mine]
     cut = (in_rows + down_rows) // 2
     held_in, held_down = [add_low(a, b) for a, b in zip(mine, core)]
+    held_in, held_down, back_late = tie(held_in, held_down, back_near[2:])
     blocks = [held_in[:cut], jnp.concatenate([held_in[cut:], held_down])]
     block_orders = orders_of(bits)
     steps = bits - 1
-    turns = [("sum", at) for at in range(steps)] + [("copy", at) for at in reversed(range(steps))]
-
-    def begin(turn, blocks):
-        kind, at = turn
-        send = sent if kind == "sum" else lambda b, n, bit, _: across(b, n, bit)
-        return [send(b, reps, o[at], bit_of) for b, o in zip(blocks, block_orders)]
-
-    def finish(turn, blocks, came):
-        kind, at = turn
-        if kind == "sum":
-            return [kept_sum(b, c, o[at], bit_of) for b, c, o in zip(blocks, came, block_orders)]
-        return [both_halves(b, c, bit_of[o[at]]) for b, c, o in zip(blocks, came, block_orders)]
-
-    came = begin(turns[0], blocks)
-    back_near, blocks, combs = tie(back_near, blocks, combs)
+
+    def begin(at, blocks):
+        return [sent(b, reps, o[at], bit_of) for b, o in zip(blocks, block_orders)]
+
+    def finish(at, blocks, came):
+        return [kept_sum(b, c, o[at], bit_of) for b, c, o in zip(blocks, came, block_orders)]
+
+    came = begin(0, blocks)
+    back_near, blocks, combs = tie([*back_early, *back_late], blocks, combs)
     comb_far = far_first(combs, shard_count)
     middle_back = backward_block(
         tokens, side, middle, second_low, (backs[0], *back_near), all_w, ct, st, doc_ids, kept
     )
     middle_back, came, comb_far, blocks, combs = tie(middle_back, came, comb_far, blocks, combs)
     *comb_near, _ = near_rest(combs, *comb_far, shard_count)
-    blocks = finish(turns[0], blocks, came)
+    blocks = finish(0, blocks, came)
     middle_back, blocks = tie(middle_back, blocks)
-    came = begin(turns[1], blocks)
+    came = begin(1, blocks)
     grad_out, rows_t, grad_middle, grad_pre = middle_back
     joint, grad_tokens = finish_block(
         tokens, all_w, grad_middle, grad_pre, grad_out, rows_t, kept[0]
     )
     joint, came, blocks = tie(joint, came, blocks)
-    blocks = finish(turns[1], blocks, came)
-    joint, blocks = tie(joint, blocks)
-    came = begin(turns[2], blocks)
-    joint_own = reduce_all(joint, reps, shard_count, 3)
-    joint_own, blocks, comb_near, came = tie(joint_own, blocks, comb_near, came)
-    mixed = middle + combs[0].astype(f32) + sum(part.astype(f32) for part in comb_near)
+    blocks = finish(1, blocks, came)
+    for at in range(2, steps):
+        blocks = finish(at, blocks, begin(at, blocks))
+    joint_own, blocks = reduce_all(joint, *blocks, reps, shard_count, 3)
+    joint_own, blocks, comb_near = tie(joint_own, blocks, comb_near)
+    upper, lower = [
+        comb_near[at].astype(f32) + comb_near[at + 1].astype(f32) for at in (0, 2)
+    ]
+    mixed = middle + combs[0].astype(f32) + jnp.concatenate([upper, lower])
     mixed = mixed.astype(bf16)
-    blocks = finish(turns[2], blocks, came)
-    for turn in turns[3:]:
-        blocks = finish(turn, blocks, begin(turn, blocks))
     others = [across(b, reps, 0) for b in blocks]
     grad_in_own = place_half(*blocks, 0, in_rows, None, bit_of[0])
     grad_down_own = place_half(*blocks, in_rows, down_rows, None, bit_of[0])

time: 554 us -> 528 us (0.953)
  waiting for transfers between devices: 68.6 us -> 31.6 us
  Pallas kernels: 380 us -> 393 us
  other arithmetic: 40.4 us -> 32.5 us
  local copies, waits for them, and re-layouts: 18.8 us -> 25.3 us
    pallas_call x1, Pallas kernels: 69.6 us -> 98.4 us  [reduce_all(): pl.pallas_call(lambda *refs: reduce_kernel(reps, shard_count, *refs), out...]
    ppermute x12 -> x8, waiting for transfers between devices: 34.9 us -> 6.61 us  [across(): lax.ppermute(block, 'rep', [(at, at ^ 2 ** bit) for at in range(reps)])]
    pallas_call x2 -> x1, Pallas kernels: 46.1 us -> 34.8 us  [weight_block(): pl.pallas_call(weight_kernel, grid_spec=grid_spec, out_shape=pair * 2, co...]
    ppermute x14 -> x18, waiting for transfers between devices: 33.7 us -> 25 us  [shift(): lax.ppermute(block, 'shard', [(at, (at + step) % count) for at in range(c...]
    ppermute x14 -> x18, starting transfers between devices: 22.6 us -> 31.1 us  [shift(): lax.ppermute(block, 'shard', [(at, (at + step) % count) for at in range(c...]
    ppermute x12 -> x8, starting transfers between devices: 13.5 us -> 5.06 us  [across(): lax.ppermute(block, 'rep', [(at, at ^ 2 ** bit) for at in range(reps)])]
  transfers between devices with their start and end apart: 26 -> 26, of which waited for: 5 -> 5; matrix products, arithmetic and copies ran while one was open for 7% -> 7% of each run, Pallas kernels for 45% -> 54%
where the time goes in v4:
time: 528 us; the launch traced here: 521 us
  Pallas kernels  393 us (74%)
  starting transfers between devices  36.2 us (7%)
  other arithmetic  32.5 us (6%)
  waiting for transfers between devices  31.6 us (6%)
  local copies, waits for them, and re-layouts  25.3 us (5%)
    pallas_call x1, Pallas kernels, reduce_all(): pl.pallas_call(lambda *refs: reduce_kernel(reps, shard_count, *refs), out...  98.4 us
    pallas_call x4, Pallas kernels, expert_block(): pl.pallas_call(lambda *refs: expert_kernel(bool(before), *refs), grid=(ex...  83.5 us
    pallas_call x1, Pallas kernels, gather_all(): pl.pallas_call(lambda *refs: gather_kernel(reps, shard_count, *refs), out...  81 us
    pallas_call x4, Pallas kernels, local_call(): pl.pallas_call(kernel, out_shape=outs, in_specs=[pl.BlockSpec(memory_spac...  76.4 us
    pallas_call x1, Pallas kernels, weight_block(): pl.pallas_call(weight_kernel, grid_spec=grid_spec, out_shape=pair * 2, co...  34.8 us
    ppermute x18, starting transfers between devices, shift(): lax.ppermute(block, 'shard', [(at, (at + step) % count) for at in range(c...  31.1 us
    ppermute x18, waiting for transfers between devices, shift(): lax.ppermute(block, 'shard', [(at, (at + step) % count) for at in range(c...  25 us
    pallas_call x4, Pallas kernels, place_half(): pl.pallas_call(lambda *refs: place_kernel(first, cut, *refs), grid_spec=g...  19.3 us
  transfers between devices with their start and end apart: 26, of which 5 were waited for; matrix products, arithmetic and copies ran while one was open for 7% of the time, Pallas kernels for 54%

profile of v4, /device:TPU:0, one launch (start us, length us, event | category | flops | bytes accessed | tf_op | source)
XLA Modules:
  0.0 520.7 jit_solution(7132152844591413770)
XLA Ops:
  5.6 81.0 %shard_map.212 = (bf16[4,8,32,3200]{3,2,1,0:T(8,128)(2,1)}, bf16[512,1152]{1,0:T(8,128)(2,1)}, bf16[512,1152]{1,0:T(8,128)(2,1)}, bf16[512,1152]{1,0:T(8,128)(2,1)}) custom-call(bf16[8,32,1024]{2,1,0:T(8,128)(2,1)} %bitcast.34, bf16[8,32,512]{2,1,0:T(8,128)(2,1)} %bitcast.36, bf16[8,32,512]{2,1,0:T(8,128)(2,1)} %bitcast.37, bf16[8,32,1024]{2,1,0:T(8,128)(2,1)} %bitcast.35, ...), custom_call_target="tpu_custom_call" | custom-call | bytes 3276800 | tf_op jit(solution)/shard_map/pallas_call | solution.py:206
  89.0 3.8 collective-permute-start.1
  96.2 25.2 %shard_map.213 = (bf16[512,1024]{1,0:T(8,128)(2,1)}, f32[512,1024]{1,0:T(8,128)}, bf16[1024,512]{1,0:T(8,128)(2,1)}, bf16[512,1024]{1,0:T(8,128)(2,1)}, bf16[512...) custom-call(bf16[512,1024]{1,0:T(8,128)(2,1)} %tokens.5, ...), custom_call_target="tpu_custom_call" | custom-call | flops 1000000 | bytes 100000 | tf_op jit(solution)/shard_map/pallas_call | solution.py:531
  121.5 4.0 collective-permute-start.3
  127.2 20.9 %shard_map.214 = (bf16[4,512,2048]{2,1,0:T(8,128)(2,1)}, bf16[4,2048,1024]{2,1,0:T(8,128)(2,1)}, bf16[1024,2048]{1,0:T(8,128)(2,1)}, bf16[2048,1024]{1,0:T(8,128...) custom-call(s32[1]{0:T(128)} %bitcast.8.refs_0_, bf16[512,1024]{1,0:T(8,128)(2,1)} %get-tuple-element.148.refs_1_.second, ...), custom_call_target="tpu_custom_call" | custom-call | flops 1000000 | bytes 100000 | tf_op jit(solution)/shard_map/pallas_call | solution.py:814
  149.6 17.9 %collective-permute-done.3.refs_1_ = bf16[512,1024]{1,0:T(8,128)(2,1)S(1)} collective-permute-done((bf16[512,1024]{1,0:T(8,128)(2,1)}, bf16[512,1024]{1,0:T(8,128)(2,1)S(1)}, u32[]{:S(2)}, u32[]{:S(2)}) %collective-permute-start.3) | collective-permute-done | bytes 1048608 | tf_op jit(solution)/shard_map/ppermute | solution.py:882
  170.8 20.8 %shard_map.215 = (bf16[4,512,2048]{2,1,0:T(8,128)(2,1)}, bf16[4,2048,1024]{2,1,0:T(8,128)(2,1)}, bf16[1024,2048]{1,0:T(8,128)(2,1)}, bf16[2048,1024]{1,0:T(8,128...) custom-call(s32[1]{0:T(128)} %bitcast.8.refs_0_, ...), custom_call_target="tpu_custom_call", output_to_operand_aliasing={{0}: (6, {}), {1}: (7, {}), {2}: (8, {}), {3}: (9, {})} | custom-call | flops 1000000 | bytes 100000 | tf_op jit(solution)/shard_map/pallas_call | solution.py:814
  192.8 20.8 %shard_map.216 = (bf16[4,512,2048]{2,1,0:T(8,128)(2,1)}, bf16[4,2048,1024]{2,1,0:T(8,128)(2,1)}, bf16[1024,2048]{1,0:T(8,128)(2,1)}, bf16[2048,1024]{1,0:T(8,128...) custom-call(s32[1]{0:T(128)} %bitcast.8.refs_0_, ...), custom_call_target="tpu_custom_call", output_to_operand_aliasing={{0}: (6, {}), {1}: (7, {}), {2}: (8, {}), {3}: (9, {})} | custom-call | flops 1000000 | bytes 100000 | tf_op jit(solution)/shard_map/pallas_call | solution.py:814
  214.9 3.7 collective-permute-start.6
  219.0 20.9 %shard_map.217 = (bf16[4,512,2048]{2,1,0:T(8,128)(2,1)}, bf16[4,2048,1024]{2,1,0:T(8,128)(2,1)}, bf16[1024,2048]{1,0:T(8,128)(2,1)}, bf16[2048,1024]{1,0:T(8,128...) custom-call(s32[1]{0:T(128)} %bitcast.8.refs_0_, ...), custom_call_target="tpu_custom_call", output_to_operand_aliasing={{0}: (6, {}), {1}: (7, {}), {2}: (8, {}), {3}: (9, {})} | custom-call | flops 1000000 | bytes 100000 | tf_op jit(solution)/shard_map/pallas_call | solution.py:814
  239.9 3.2 collective-permute-done.7
  247.1 34.8 %shard_map.218 = (bf16[2048,1024]{1,0:T(8,128)(2,1)}, bf16[1024,1024]{1,0:T(8,128)(2,1)}, bf16[2048,1024]{1,0:T(8,128)(2,1)}, bf16[1024,1024]{1,0:T(8,128)(2,1)}) custom-call(s32[1]{0:T(128)} %bitcast.9.base, bf16[1024,2048]{1,0:T(8,128)(2,1)} %get-tuple-element.188.second_t, bf16[2048,1024]{1,0:T(8,128)(2,1)} %get-tuple-element.189.dy, ...), custom_call_target="tpu_custom_call" | custom-call | flops 1000000 | bytes 100000 | tf_op jit(solution)/shard_map/pallas_call | solution.py:870
  288.3 6.6 %collective-permute-done.11 = bf16[1024,1024]{1,0:T(8,128)(2,1)} collective-permute-done((bf16[1024,1024]{1,0:T(8,128)(2,1)}, bf16[1024,1024]{1,0:T(8,128)(2,1)}, u32[]{:S(2)}, u32[]{:S(2)}) %collective-permute-start.11) | collective-permute-done | bytes 2097184 | tf_op jit(solution)/shard_map/ppermute | solution.py:936
  294.9 3.3 add_convert_fusion.1
  298.3 4.3 add_convert_fusion
  316.8 31.1 %shard_map.219 = (bf16[1024,1024]{1,0:T(8,128)(2,1)}, f32[128,1024]{1,0:T(8,128)}, f32[512,1024]{1,0:T(8,128)}, bf16[512,2048]{1,0:T(8,128)(2,1)}) custom-call(bf16[512,1024]{1,0:T(8,128)(2,1)} %tokens.5, bf16[512,1152]{1,0:T(8,128)(2,1)} %get-tuple-element.144.refs_2_.side, f32[512,1024]{1,0:T(8,128)} %get-tuple-element.143.middle, ...), custom_call_target="tpu_custom_call" | custom-call | flops 1000000 | bytes 100000 | tf_op jit(solution)/shard_map/pallas_call | solution.py:531
  359.6 3.8 collective-permute-start.20
  365.3 4.2 collective-permute-start.22
  369.5 17.0 %shard_map.220 = (bf16[1024,3200]{1,0:T(8,128)(2,1)}, f32[512,1024]{1,0:T(8,128)}) custom-call(bf16[512,1024]{1,0:T(8,128)(2,1)} %tokens.5, bf16[1024,3200]{1,0:T(8,128)(2,1)} %bitcast.23, f32[512,1024]{1,0:T(8,128)} %get-tuple-element.238.grad_middle, bf16[512,2048]{1,0:T(8,128)(2,1)} %get-tuple-element.239.grad_pre, ...), custom_call_target="tpu_custom_call" | custom-call | flops 1000000 | bytes 100000 | tf_op jit(solution)/shard_map/pallas_call | solution.py:531
  390.0 98.4 %shard_map.221 = (bf16[1,8,32,3200]{3,2,1,0:T(8,128)(2,1)}, bf16[4,384,1024]{2,1,0:T(8,128)(2,1)}, bf16[4,384,1024]{2,1,0:T(8,128)(2,1)}) custom-call(bf16[4,8,32,3200]{3,2,1,0:T(8,128)(2,1)} %bitcast.31, bf16[384,1024]{1,0:T(8,128)(2,1)} %add_convert_fusion.5.refs_1_, bf16[384,1024]{1,0:T(8,128)(2,1)} %add_convert_fusion.4.refs_2_), custom_call_target="tpu_custom_call" | custom-call | bytes 3276800 | tf_op jit(solution)/shard_map/pallas_call | solution.py:359
  494.5 5.9 %shard_map.223.refs_3_ = f32[4096,1024]{1,0:T(8,128)} custom-call(s32[1]{0:T(128)} %bitcast.15.refs_0_, bf16[1536,1024]{1,0:T(8,128)(2,1)} %bitcast.29, bf16[1536,1024]{1,0:T(8,128)(2,1)} %bitcast.26), custom_call_target="tpu_custom_call" | custom-call | flops 1000000 | bytes 100000 | tf_op jit(solution)/shard_map/pallas_call | solution.py:982
  500.4 3.8 shard_map.225.refs_3_
  510.6 5.9 %shard_map.224 = f32[4096,1024]{1,0:T(8,128)} custom-call(s32[1]{0:T(128)} %bitcast.14.refs_0_, bf16[1536,1024]{1,0:T(8,128)(2,1)} %copy-done, bf16[1536,1024]{1,0:T(8,128)(2,1)} %collective-permute-done.25.refs_2_, f32[4096,1024]{1,0:T(8,128)} %shard_map.223.refs_3_), custom_call_target="tpu_custom_call", output_to_operand_aliasing={{}: (3, {})} | custom-call | flops 1000000 | bytes 100000 | tf_op jit(solution)/shard_map/pallas_call | solution.py:982
  516.5 3.7 shard_map.226
  (149 shorter events, 74.0 us)
Async XLA Ops:
  87.8 33.7 %collective-permute-start = (bf16[256,1152]{1,0:T(8,128)(2,1)S(1)}, bf16[256,1152]{1,0:T(8,128)(2,1)S(1)}, u32[]{:S(2)}, u32[]{:S(2)}) collective-permute-start(bf16[256,1152]{1,0:T(8,128)(2,1)S(1)} %slice.90), channel_id=1, source_target_pairs={{0,1},{1,2},{2,3},{3,0},{4,5},{5,6},{6,7},{7,4},{8,9},{9,10},{10,1... | collective-permute-start | bytes 1769480 | tf_op jit(solution)/shard_map/ppermute | solution.py:882
  89.0 32.4 %collective-permute-start.1 = (bf16[256,1152]{1,0:T(8,128)(2,1)S(1)}, bf16[256,1152]{1,0:T(8,128)(2,1)S(1)}, u32[]{:S(2)}, u32[]{:S(2)}) collective-permute-start(bf16[256,1152]{1,0:T(8,128)(2,1)S(1)} %slice.91), channel_id=1, source_target_pairs={{0,3},{1,0},{2,1},{3,2},{4,7},{5,4},{6,5},{7,6},{8,11},{9,8},{10,9... | collective-permute-start | bytes 1769480 | tf_op jit(solution)/shard_map/ppermute | solution.py:882
  121.4 28.2 %collective-permute-start.2 = (bf16[512,1024]{1,0:T(8,128)(2,1)}, bf16[512,1024]{1,0:T(8,128)(2,1)S(1)}, u32[]{:S(2)}, u32[]{:S(2)}) collective-permute-start(bf16[512,1024]{1,0:T(8,128)(2,1)} %get-tuple-element.148.refs_1_.second), channel_id=1, source_target_pairs={{0,1},{1,2},{2,3},{3,0},{4,5},{5,6},{6,7},{7,4},{8,9},{9,10},{10,1... | collective-permute-start | bytes 3145736 | tf_op jit(solution)/shard_map/ppermute | solution.py:882
  121.5 46.0 %collective-permute-start.3 = (bf16[512,1024]{1,0:T(8,128)(2,1)}, bf16[512,1024]{1,0:T(8,128)(2,1)S(1)}, u32[]{:S(2)}, u32[]{:S(2)}) collective-permute-start(bf16[512,1024]{1,0:T(8,128)(2,1)} %get-tuple-element.148.refs_1_.second), channel_id=1, source_target_pairs={{0,3},{1,0},{2,1},{3,2},{4,7},{5,4},{6,5},{7,6},{8,11},{9,8},{10,9... | collective-permute-start | bytes 3145736 | tf_op jit(solution)/shard_map/ppermute | solution.py:882
  167.6 24.1 %collective-permute-start.5 = (bf16[256,1024]{1,0:T(8,128)(2,1)S(1)}, bf16[256,1024]{1,0:T(8,128)(2,1)S(1)}, u32[]{:S(2)}, u32[]{:S(2)}) collective-permute-start(bf16[256,1024]{1,0:T(8,128)(2,1)S(1)} %slice.94), channel_id=1, source_target_pairs={{0,3},{1,0},{2,1},{3,2},{4,7},{5,4},{6,5},{7,6},{8,11},{9,8},{10,9... | collective-permute-start | bytes 1572872 | tf_op jit(solution)/shard_map/ppermute | solution.py:882
  169.5 22.2 %collective-permute-start.4 = (bf16[256,1024]{1,0:T(8,128)(2,1)S(1)}, bf16[256,1024]{1,0:T(8,128)(2,1)S(1)}, u32[]{:S(2)}, u32[]{:S(2)}) collective-permute-start(bf16[256,1024]{1,0:T(8,128)(2,1)S(1)} %slice.93), channel_id=1, source_target_pairs={{0,1},{1,2},{2,3},{3,0},{4,5},{5,6},{6,7},{7,4},{8,9},{9,10},{10,1... | collective-permute-start | bytes 1572872 | tf_op jit(solution)/shard_map/ppermute | solution.py:882
  214.9 25.0 %collective-permute-start.6 = (bf16[256,1152]{1,0:T(8,128)(2,1)S(1)}, bf16[256,1152]{1,0:T(8,128)(2,1)S(1)}, u32[]{:S(2)}, u32[]{:S(2)}) collective-permute-start(bf16[256,1152]{1,0:T(8,128)(2,1)S(1)} %get-tuple-element.320), channel_id=1, source_target_pairs={{0,3},{1,0},{2,1},{3,2},{4,7},{5,4},{6,5},{7,6},{8,11},{9,8},{10,9... | collective-permute-start | bytes 1769480 | tf_op jit(solution)/shard_map/ppermute | solution.py:882
  218.6 24.5 %collective-permute-start.7 = (bf16[256,1152]{1,0:T(8,128)(2,1)S(1)}, bf16[256,1152]{1,0:T(8,128)(2,1)S(1)}, u32[]{:S(2)}, u32[]{:S(2)}) collective-permute-start(bf16[256,1152]{1,0:T(8,128)(2,1)S(1)} %get-tuple-element.319), channel_id=1, source_target_pairs={{0,1},{1,2},{2,3},{3,0},{4,5},{5,6},{6,7},{7,4},{8,9},{9,10},{10,1... | collective-permute-start | bytes 1769480 | tf_op jit(solution)/shard_map/ppermute | solution.py:882
  243.8 38.2 %collective-permute-start.8 = (bf16[384,1152]{1,0:T(8,128)(2,1)S(1)}, bf16[384,1152]{1,0:T(8,128)(2,1)}, u32[]{:S(2)}, u32[]{:S(2)}) collective-permute-start(bf16[384,1152]{1,0:T(8,128)(2,1)S(1)} %slice.101), channel_id=1, source_target_pairs={{0,3},{1,0},{2,1},{3,2},{4,7},{5,4},{6,5},{7,6},{8,11},{9,8},{10,9... | collective-permute-start | bytes 2654216 | tf_op jit(solution)/shard_map/ppermute | solution.py:882
  246.9 37.4 %collective-permute-start.9 = (bf16[384,1152]{1,0:T(8,128)(2,1)}, bf16[384,1152]{1,0:T(8,128)(2,1)}, u32[]{:S(2)}, u32[]{:S(2)}) collective-permute-start(bf16[384,1152]{1,0:T(8,128)(2,1)} %slice.102), channel_id=1, source_target_pairs={{0,1},{1,2},{2,3},{3,0},{4,5},{5,6},{6,7},{7,4},{8,9},{9,10},{10,1... | collective-permute-start | bytes 2654216 | tf_op jit(solution)/shard_map/ppermute | solution.py:882
  284.9 17.7 %collective-permute-start.12 = (bf16[128,1152]{1,0:T(8,128)(2,1)S(1)}, bf16[128,1152]{1,0:T(8,128)(2,1)S(1)}, u32[]{:S(2)}, u32[]{:S(2)}) collective-permute-start(bf16[128,1152]{1,0:T(8,128)(2,1)S(1)} %slice.103), channel_id=1, source_target_pairs={{0,3},{1,0},{2,1},{3,2},{4,7},{5,4},{6,5},{7,6},{8,11},{9,8},{10,9... | collective-permute-start | bytes 884744 | tf_op jit(solution)/shard_map/ppermute | solution.py:882
  288.1 14.6 %collective-permute-start.13 = (bf16[128,1152]{1,0:T(8,128)(2,1)S(1)}, bf16[128,1152]{1,0:T(8,128)(2,1)S(1)}, u32[]{:S(2)}, u32[]{:S(2)}) collective-permute-start(bf16[128,1152]{1,0:T(8,128)(2,1)S(1)} %slice.104), channel_id=1, source_target_pairs={{0,1},{1,2},{2,3},{3,0},{4,5},{5,6},{6,7},{7,4},{8,9},{9,10},{10,1... | collective-permute-start | bytes 884744 | tf_op jit(solution)/shard_map/ppermute | solution.py:882
  304.8 43.1 %collective-permute-start.14 = (bf16[768,1024]{1,0:T(8,128)(2,1)}, bf16[768,1024]{1,0:T(8,128)(2,1)}, u32[]{:S(2)}, u32[]{:S(2)}) collective-permute-start(bf16[768,1024]{1,0:T(8,128)(2,1)} %constant_dynamic-slice_fusion.2), channel_id=1, source_target_pairs={{0,8},{4,12},{8,0},{12,4},{16,24},{20,28},{24,16},{28,20},{1,9},{5... | collective-permute-start | bytes 4718600 | tf_op jit(solution)/shard_map/ppermute | solution.py:936
  308.8 39.1 %collective-permute-start.15 = (bf16[768,1024]{1,0:T(8,128)(2,1)}, bf16[768,1024]{1,0:T(8,128)(2,1)}, u32[]{:S(2)}, u32[]{:S(2)}) collective-permute-start(bf16[768,1024]{1,0:T(8,128)(2,1)} %fusion.1), channel_id=1, source_target_pairs={{0,16},{4,20},{8,24},{12,28},{16,0},{20,4},{24,8},{28,12},{1,17},{... | collective-permute-start | bytes 4718600 | tf_op jit(solution)/shard_map/ppermute | solution.py:936
  313.4 34.4 %collective-permute-start.16 = (bf16[256,1024]{1,0:T(8,128)(2,1)}, bf16[256,1024]{1,0:T(8,128)(2,1)}, u32[]{:S(2)}, u32[]{:S(2)}) collective-permute-start(bf16[256,1024]{1,0:T(8,128)(2,1)} %get-tuple-element.322), channel_id=1, source_target_pairs={{0,3},{1,0},{2,1},{3,2},{4,7},{5,4},{6,5},{7,6},{8,11},{9,8},{10,9... | collective-permute-start | bytes 1572872 | tf_op jit(solution)/shard_map/ppermute | solution.py:882
  316.5 31.4 %collective-permute-start.17 = (bf16[256,1024]{1,0:T(8,128)(2,1)}, bf16[256,1024]{1,0:T(8,128)(2,1)}, u32[]{:S(2)}, u32[]{:S(2)}) collective-permute-start(bf16[256,1024]{1,0:T(8,128)(2,1)} %get-tuple-element.321), channel_id=1, source_target_pairs={{0,1},{1,2},{2,3},{3,0},{4,5},{5,6},{6,7},{7,4},{8,9},{9,10},{10,1... | collective-permute-start | bytes 1572872 | tf_op jit(solution)/shard_map/ppermute | solution.py:882
  353.9 32.5 %collective-permute-start.18 = (bf16[384,1024]{1,0:T(8,128)(2,1)}, bf16[384,1024]{1,0:T(8,128)(2,1)S(1)}, u32[]{:S(2)}, u32[]{:S(2)}) collective-permute-start(bf16[384,1024]{1,0:T(8,128)(2,1)} %constant_dynamic-slice_fusion.1), channel_id=1, source_target_pairs={{0,16},{4,20},{8,24},{12,28},{16,0},{20,4},{24,8},{28,12},{1,17},{... | collective-permute-start | bytes 2359304 | tf_op jit(solution)/shard_map/ppermute | solution.py:936
  355.3 31.2 %collective-permute-start.19 = (bf16[384,1024]{1,0:T(8,128)(2,1)}, bf16[384,1024]{1,0:T(8,128)(2,1)}, u32[]{:S(2)}, u32[]{:S(2)}) collective-permute-start(bf16[384,1024]{1,0:T(8,128)(2,1)} %constant_dynamic-slice_fusion), channel_id=1, source_target_pairs={{0,8},{4,12},{8,0},{12,4},{16,24},{20,28},{24,16},{28,20},{1,9},{5... | collective-permute-start | bytes 2359304 | tf_op jit(solution)/shard_map/ppermute | solution.py:936
  359.6 128.8 %collective-permute-start.20 = (bf16[384,1024]{1,0:T(8,128)(2,1)}, bf16[384,1024]{1,0:T(8,128)(2,1)}, u32[]{:S(2)}, u32[]{:S(2)}) collective-permute-start(bf16[384,1024]{1,0:T(8,128)(2,1)} %slice.113), channel_id=1, source_target_pairs={{0,3},{1,0},{2,1},{3,2},{4,7},{5,4},{6,5},{7,6},{8,11},{9,8},{10,9... | collective-permute-start | bytes 2359304 | tf_op jit(solution)/shard_map/ppermute | solution.py:882
  364.3 124.1 %collective-permute-start.21 = (bf16[384,1024]{1,0:T(8,128)(2,1)}, bf16[384,1024]{1,0:T(8,128)(2,1)}, u32[]{:S(2)}, u32[]{:S(2)}) collective-permute-start(bf16[384,1024]{1,0:T(8,128)(2,1)} %slice.114), channel_id=1, source_target_pairs={{0,1},{1,2},{2,3},{3,0},{4,5},{5,6},{6,7},{7,4},{8,9},{9,10},{10,1... | collective-permute-start | bytes 2359304 | tf_op jit(solution)/shard_map/ppermute | solution.py:882
  365.3 123.1 %collective-permute-start.22 = (bf16[128,1024]{1,0:T(8,128)(2,1)S(1)}, bf16[128,1024]{1,0:T(8,128)(2,1)S(1)}, u32[]{:S(2)}, u32[]{:S(2)}) collective-permute-start(bf16[128,1024]{1,0:T(8,128)(2,1)S(1)} %slice.115), channel_id=1, source_target_pairs={{0,3},{1,0},{2,1},{3,2},{4,7},{5,4},{6,5},{7,6},{8,11},{9,8},{10,9... | collective-permute-start | bytes 786440 | tf_op jit(solution)/shard_map/ppermute | solution.py:882
  386.5 102.0 %collective-permute-start.23 = (bf16[128,1024]{1,0:T(8,128)(2,1)S(1)}, bf16[128,1024]{1,0:T(8,128)(2,1)S(1)}, u32[]{:S(2)}, u32[]{:S(2)}) collective-permute-start(bf16[128,1024]{1,0:T(8,128)(2,1)S(1)} %slice.116), channel_id=1, source_target_pairs={{0,1},{1,2},{2,3},{3,0},{4,5},{5,6},{6,7},{7,4},{8,9},{9,10},{10,1... | collective-permute-start | bytes 786440 | tf_op jit(solution)/shard_map/ppermute | solution.py:882
  489.2 19.7 %collective-permute-start.24 = (bf16[1536,1024]{1,0:T(8,128)(2,1)}, bf16[1536,1024]{1,0:T(8,128)(2,1)S(1)}, u32[]{:S(2)}, u32[]{:S(2)}) collective-permute-start(bf16[1536,1024]{1,0:T(8,128)(2,1)} %bitcast.28), channel_id=1, source_target_pairs={{0,4},{4,0},{8,12},{12,8},{16,20},{20,16},{24,28},{28,24},{1,5},{5... | collective-permute-start | bytes 9437192 | tf_op jit(solution)/shard_map/ppermute | solution.py:936
  489.6 19.3 %collective-permute-start.25 = (bf16[1536,1024]{1,0:T(8,128)(2,1)}, bf16[1536,1024]{1,0:T(8,128)(2,1)}, u32[]{:S(2)}, u32[]{:S(2)}) collective-permute-start(bf16[1536,1024]{1,0:T(8,128)(2,1)} %bitcast.25), channel_id=1, source_target_pairs={{0,4},{4,0},{8,12},{12,8},{16,20},{20,16},{24,28},{28,24},{1,5},{5... | collective-permute-start | bytes 9437192 | tf_op jit(solution)/shard_map/ppermute | solution.py:936
  (25 other events, 225.7 us)

commit v5 on v4

--- a/solution.py
+++ b/solution.py
@@ -178,22 +178,47 @@
         side[here, width:] = jnp.where(mask, 1.0, 0.0).astype(side.dtype)
     for copy in flying:
         copy.wait()
-    flying = []
-    if shard_count > 1:
-        for number, (step, target) in enumerate(((1, right), (shard_count - 1, left))):
-            copy = pltpu.make_async_remote_copy(
-                src_ref=side,
-                dst_ref=target,
-                send_sem=d_send.at[number],
-                recv_sem=d_recv.at[number],
-                device_id=(rep_at, (shard_at + step) % shard_count),
-                device_id_type=MESH,
-            )
-            copy.start()
-            flying.append(copy)
+    top = shard_count - 1
+    neighbours = []
+    for number, (step, target) in enumerate(((1, right), (top, left))):
+        copy = pltpu.make_async_remote_copy(
+            src_ref=side,
+            dst_ref=target,
+            send_sem=d_send.at[number],
+            recv_sem=d_recv.at[number],
+            device_id=(rep_at, (shard_at + step) % shard_count),
+            device_id_type=MESH,
+        )
+        neighbours.append(copy)
+    sends_right, sends_left = shard_at < top, shard_at > 0
+
+    @pl.when(sends_right)
+    def _():
+        neighbours[0].start()
+
+    @pl.when(sends_left)
+    def _():
+        neighbours[1].start()
+
+    @pl.when(shard_at == 0)
+    def _():
+        right[...] = jnp.zeros_like(right)
+
+    @pl.when(shard_at == top)
+    def _():
+        left[...] = jnp.zeros_like(left)
+
     spread_others(out, orders, columns, rep_at, shard_at, shard_count, sends, recvs)
-    for copy in flying:
-        copy.wait()
+
+    @pl.when(sends_right)
+    def _():
+        neighbours[0].wait_send()
+        neighbours[1].wait_recv()
+
+    @pl.when(sends_left)
+    def _():
+        neighbours[1].wait_send()
+        neighbours[0].wait_recv()
 
 
 def gather_all(weights, dy, routes, reps, shard_count, number):
@@ -289,7 +314,7 @@
     for half in range(HALVES):
         begin(half, 0)
     steps = spread_steps(
-        (upper, lower), (upper_out, lower_out), orders_of(bits), rep_at, shard_at, s_send, s_recv
+        (upper, lower), (upper_out, lower_out), last_orders(bits), rep_at, shard_at, s_send, s_recv
     )
     next(steps, None)
     for at in range(bits):
@@ -359,7 +384,7 @@
     out, *wholes = pl.pallas_call(
         lambda *refs: reduce_kernel(reps, shard_count, *refs),
         out_shape=[jax.ShapeDtypeStruct((1, reps, rows, width), parts.dtype)]
-        + [jax.ShapeDtypeStruct((reps // 2, *piece.shape), piece.dtype) for piece in (upper, lower)],
+        + [jax.ShapeDtypeStruct((reps // 4, *piece.shape), piece.dtype) for piece in (upper, lower)],
         in_specs=[pl.BlockSpec(memory_space=pltpu.VMEM)] * 3,
         out_specs=[pl.BlockSpec(memory_space=pltpu.VMEM)] * 3,
         scratch_shapes=scratch,
@@ -562,7 +587,7 @@
 
 
 def backward_kernel(
-    tokens, side, middle, second, back_own, left_up, right_up, left_low, right_low, w, ct, st, doc_col, doc_row,
+    tokens, side, middle, second, back_own, back_left, back_right, w, ct, st, doc_col, doc_row,
     q8, keys, values, att_t, lse,
     grad_out, rows_t, grad_middle, grad_pre,
     bias, grad_branch, grad_att, dq_t, dk, dv,
@@ -579,15 +604,12 @@
     router_t = jnp.zeros((PAD, width), F32)
     for at in range(0, rows, LANES):
         here = slice(at, at + LANES)
-        cut = left_up.shape[0]
-        back_left, back_right = (left_up, right_up) if at < cut else (left_low, right_low)
-        there = slice(at - cut * (at >= cut), at - cut * (at >= cut) + LANES)
         mask = side[here, width:] > 0
         gates = gate_softmax(second[here, :], small, mask)
         came = (
             back_own[here, width:].astype(F32)
-            + back_left[there, width:].astype(F32)
-            + back_right[there, width:].astype(F32)
+            + back_left[here, width:].astype(F32)
+            + back_right[here, width:].astype(F32)
         )
         gate_back = jnp.where(
             lane_of(came.shape) < EXPERTS, came + pltpu.roll(came, tall - width - EXPERTS, 1), 0.0
@@ -597,8 +619,8 @@
         router_t += dot(grad_logits.T.astype(BF16), second[here, :])
         grad_second = (
             back_own[here, :width].astype(F32)
-            + back_left[there, :width].astype(F32)
-            + back_right[there, :width].astype(F32)
+            + back_left[here, :width].astype(F32)
+            + back_right[here, :width].astype(F32)
             + dot_nt(low_logits, small)
         )
         x = middle[here, :]
@@ -906,10 +928,10 @@
     return shift(far[:half], count, -1), shift(far[half:], count, 1)
 
 
-def near_rest(parts, left, right, count, after=()):
+def near_rest(parts, left, right, count):
     half = parts[0].shape[0] // 2
     if count == 2:
-        return left, jnp.zeros_like(left), right, jnp.zeros_like(right), after
+        return jnp.concatenate([left, right], axis=0), jnp.zeros_like(parts[0])
     for step in reversed(range(1, count // 2)):
         near, far = parts[step], parts[count - step]
         if step == count // 2 - 1:
@@ -917,15 +939,8 @@
             right = jnp.concatenate([far[:half], add_low(far[half:], right)], axis=0)
         else:
             left, right = add_low(near, left), add_low(far, right)
-        if step == 1:
-            left, right, after = tie(left, right, after)
-            rows = left.shape[0]
-            split = rows // LANES * 3 // 4 * LANES
-            ends = ((0, split), (split, rows))
-            cuts = [part[start:stop] for start, stop in ends for part in (left, right)]
-            shifted = [shift(part, count, (-1, 1)[at % 2]) for at, part in enumerate(cuts)]
-            return *shifted, after
         left, right = shift(left, count, -1), shift(right, count, 1)
+    return left, right
 
 
 def add_low(a, b):
@@ -939,6 +954,16 @@
 def part_of(block, index):
     half = block.shape[0] // 2
     return lax.dynamic_slice_in_dim(block, index * half, half, axis=0)
+
+
+def last_orders(bits):
+    return [order[:-1] for order in orders_of(bits)]
+
+
+def both_halves(mine, other, index):
+    first = jnp.where(index == 0, mine, other)
+    last = jnp.where(index == 0, other, mine)
+    return jnp.concatenate([first, last])
 
 
 def orders_of(bits):
@@ -1034,28 +1059,19 @@
     cosine, sine_table = cosine[:, 0, :], sine_table[:, 0, :]
     ct = jnp.concatenate([cosine] * 4, axis=1)
     st = jnp.concatenate([-sine_table, sine_table] * 2, axis=1)
-    side_parts = {0: side}
-    for step in range(1, (shard_count - 1) // 2 + 1):
-        if step > 1:
-            side_right, side_left = shift(side_right, shard_count, 1), shift(side_left, shard_count, -1)
-        side_parts[step], side_parts[shard_count - step] = side_right, side_left
-    if shard_count > 2:
-        side_far = gather_far(side_right, side_left, shard_count)
-    else:
-        side_far = (side_right,)
+    top = shard_count - 1
+    wraps = [lax.ppermute(side, "shard", [pair]) for pair in ((top, 0), (0, top))]
     second_low, middle, *kept = forward_block(
         tokens, all_w, ct, st, doc_ids, query_cols, kv_cols
     )
-    second_low, side_far = tie(second_low, side_far)
+    second_low, wraps = tie(second_low, wraps)
     far_at = shard_count // 2
-    side_parts[far_at] = jnp.concatenate(side_far)
+    side_parts = {0: side}
     second_parts, *ends = gather_near(second_low, shard_count)
     first_expert = (shard_at * own_experts)[None].astype(jnp.int32)
     order = sorted(range(shard_count), key=lambda k: min(k, shard_count - k))
-    order = order[:-2] + order[:-3:-1]
     small_full = all_w[:, small_at:]
     combs, backs, kept_parts = {}, {}, ()
-    back_far = None
     for place, k in enumerate(order):
         *kept_parts, combs[k], backs[k] = expert_block(
             first_expert,
@@ -1069,13 +1085,20 @@
             kept_parts,
         )
         if k == 0:
-            kept_parts, second_parts, ends = tie(kept_parts, second_parts, ends)
+            kept_parts, wraps, side_right, side_left = tie(kept_parts, wraps, side_right, side_left)
+            side_right = jnp.where(shard_at == 0, wraps[0], side_right)
+            side_left = jnp.where(shard_at == top, wraps[1], side_left)
+            for step in range(1, (shard_count - 1) // 2 + 1):
+                if step > 1:
+                    side_right = shift(side_right, shard_count, 1)
+                    side_left = shift(side_left, shard_count, -1)
+                side_parts[step], side_parts[shard_count - step] = side_right, side_left
+            kept_parts, second_parts, ends, side_right, side_left = tie(
+                kept_parts, second_parts, ends, side_right, side_left
+            )
             second_parts[far_at] = jnp.concatenate(gather_far(*ends, shard_count))
-        if k == far_at:
-            back_far = far_first(backs, shard_count)
-        elif back_far is not None:
-            kept_parts, back_far, backs = tie(kept_parts, back_far, backs)
-    *back_near, kept_parts = near_rest(backs, *back_far, shard_count, kept_parts)
+            side_parts[far_at] = jnp.concatenate(gather_far(side_right, side_left, shard_count))
+    back_far = far_first(backs, shard_count)
     gated_t, grad_both, second_t, dy_all = kept_parts
 
     rep_at = lax.axis_index("rep")
@@ -1085,12 +1108,12 @@
     grads = (second_t, dy_all, gated_t, grad_both)
     *away, mine_in, mine_down = weight_block((1 - bit_of[0]) * half, *grads)
     mine = (mine_in, mine_down)
-    away, back_early = tie(away, back_near[:2])
+    away, back_far, backs = tie(away, back_far, backs)
+    back_near = near_rest(backs, *back_far, shard_count)
     core = [across(part, reps, 0) for part in away]
     in_rows, down_rows = [part.shape[0] for part in mine]
     cut = (in_rows + down_rows) // 2
     held_in, held_down = [add_low(a, b) for a, b in zip(mine, core)]
-    held_in, held_down, back_late = tie(held_in, held_down, back_near[2:])
     blocks = [held_in[:cut], jnp.concatenate([held_in[cut:], held_down])]
     block_orders = orders_of(bits)
     steps = bits - 1
@@ -1102,30 +1125,31 @@
         return [kept_sum(b, c, o[at], bit_of) for b, c, o in zip(blocks, came, block_orders)]
 
     came = begin(0, blocks)
-    back_near, blocks, combs = tie([*back_early, *back_late], blocks, combs)
+    back_near, came, blocks, combs = tie(back_near, came, blocks, combs)
+    blocks = finish(0, blocks, came)
+    back_near, blocks, combs = tie(back_near, blocks, combs)
+    came = begin(1, blocks)
     comb_far = far_first(combs, shard_count)
     middle_back = backward_block(
         tokens, side, middle, second_low, (backs[0], *back_near), all_w, ct, st, doc_ids, kept
     )
     middle_back, came, comb_far, blocks, combs = tie(middle_back, came, comb_far, blocks, combs)
-    *comb_near, _ = near_rest(combs, *comb_far, shard_count)
-    blocks = finish(0, blocks, came)
+    comb_near = near_rest(combs, *comb_far, shard_count)
+    blocks = finish(1, blocks, came)
+    for at in range(2, steps):
+        blocks = finish(at, blocks, begin(at, blocks))
     middle_back, blocks = tie(middle_back, blocks)
-    came = begin(1, blocks)
+    last_bits = [order[-1] for order in block_orders]
+    came = [across(b, reps, bit) for b, bit in zip(blocks, last_bits)]
     grad_out, rows_t, grad_middle, grad_pre = middle_back
     joint, grad_tokens = finish_block(
         tokens, all_w, grad_middle, grad_pre, grad_out, rows_t, kept[0]
     )
     joint, came, blocks = tie(joint, came, blocks)
-    blocks = finish(1, blocks, came)
-    for at in range(2, steps):
-        blocks = finish(at, blocks, begin(at, blocks))
+    blocks = [both_halves(b, c, bit_of[bit]) for b, c, bit in zip(blocks, came, last_bits)]
     joint_own, blocks = reduce_all(joint, *blocks, reps, shard_count, 3)
     joint_own, blocks, comb_near = tie(joint_own, blocks, comb_near)
-    upper, lower = [
-        comb_near[at].astype(f32) + comb_near[at + 1].astype(f32) for at in (0, 2)
-    ]
-    mixed = middle + combs[0].astype(f32) + jnp.concatenate([upper, lower])
+    mixed = middle + combs[0].astype(f32) + sum(part.astype(f32) for part in comb_near)
     mixed = mixed.astype(bf16)
     others = [across(b, reps, 0) for b in blocks]
     grad_in_own = place_half(*blocks, 0, in_rows, None, bit_of[0])

time: 528 us -> 533 us (level)
  waiting for transfers between devices: 31.6 us -> 59.2 us
  Pallas kernels: 393 us -> 367 us
  other arithmetic: 32.5 us -> 38.5 us
    ppermute x18 -> x14, waiting for transfers between devices: 25 us -> 51.6 us  [shift(): lax.ppermute(block, 'shard', [(at, (at + step) % count) for at in range(c...]
    pallas_call x1, Pallas kernels: 81 us -> 55.8 us  [gather_all(): pl.pallas_call(lambda *refs: gather_kernel(reps, shard_count, *refs), out...]
    ppermute x0 -> x2, starting transfers between devices: none -> 7.79 us  [shards(): lax.ppermute(side, 'shard', [pair])]
    ppermute x18 -> x14, starting transfers between devices: 31.1 us -> 23.5 us  [shift(): lax.ppermute(block, 'shard', [(at, (at + step) % count) for at in range(c...]
  transfers between devices with their start and end apart: 26 -> 26, of which waited for: 5 -> 6; matrix products, arithmetic and copies ran while one was open for 7% -> 7% of each run, Pallas kernels for 54% -> 53%
where the time goes in v5:
time: 533 us; the launch traced here: 526 us
  Pallas kernels  367 us (69%)
  waiting for transfers between devices  59.2 us (11%)
  starting transfers between devices  38.8 us (7%)
  other arithmetic  38.5 us (7%)
  local copies, waits for them, and re-layouts  20.6 us (4%)
    pallas_call x1, Pallas kernels, reduce_all(): pl.pallas_call(lambda *refs: reduce_kernel(reps, shard_count, *refs), out...  97.1 us
    pallas_call x4, Pallas kernels, expert_block(): pl.pallas_call(lambda *refs: expert_kernel(bool(before), *refs), grid=(ex...  83.6 us
    pallas_call x4, Pallas kernels, local_call(): pl.pallas_call(kernel, out_shape=outs, in_specs=[pl.BlockSpec(memory_spac...  76.2 us
    pallas_call x1, Pallas kernels, gather_all(): pl.pallas_call(lambda *refs: gather_kernel(reps, shard_count, *refs), out...  55.8 us
    ppermute x14, waiting for transfers between devices, shift(): lax.ppermute(block, 'shard', [(at, (at + step) % count) for at in range(c...  51.6 us
    pallas_call x1, Pallas kernels, weight_block(): pl.pallas_call(weight_kernel, grid_spec=grid_spec, out_shape=pair * 2, co...  34.9 us
    ppermute x14, starting transfers between devices, shift(): lax.ppermute(block, 'shard', [(at, (at + step) % count) for at in range(c...  23.5 us
    pallas_call x4, Pallas kernels, place_half(): pl.pallas_call(lambda *refs: place_kernel(first, cut, *refs), grid_spec=g...  19.6 us
  transfers between devices with their start and end apart: 26, of which 6 were waited for; matrix products, arithmetic and copies ran while one was open for 7% of the time, Pallas kernels for 53%

profile of v5, /device:TPU:0, one launch (start us, length us, event | category | flops | bytes accessed | tf_op | source)
XLA Modules:
  0.0 525.7 jit_solution(17863478822181627728)
XLA Ops:
  5.6 55.8 %shard_map.212 = (bf16[4,8,32,3200]{3,2,1,0:T(8,128)(2,1)}, bf16[512,1152]{1,0:T(8,128)(2,1)}, bf16[512,1152]{1,0:T(8,128)(2,1)}, bf16[512,1152]{1,0:T(8,128)(2,1)}) custom-call(bf16[8,32,1024]{2,1,0:T(8,128)(2,1)} %bitcast.34, bf16[8,32,512]{2,1,0:T(8,128)(2,1)} %bitcast.36, bf16[8,32,512]{2,1,0:T(8,128)(2,1)} %bitcast.37, bf16[8,32,1024]{2,1,0:T(8,128)(2,1)} %bitcast.35, ...), custom_call_target="tpu_custom_call" | custom-call | bytes 3276800 | tf_op jit(solution)/shard_map/pallas_call | solution.py:231
  62.7 6.5 %collective-permute-start.1 = (bf16[512,1152]{1,0:T(8,128)(2,1)}, bf16[512,1152]{1,0:T(8,128)(2,1)S(1)}, u32[]{:S(2)}, u32[]{:S(2)}) collective-permute-start(bf16[512,1152]{1,0:T(8,128)(2,1)} %get-tuple-element.142.refs_2_.side), channel_id=1, source_target_pairs={{0,3},{4,7},{8,11},{12,15},{16,19},{20,23},{24,27},{28,31}} | collective-permute-start | bytes 3538952 | tf_op jit(solution)/shard_map/ppermute | solution.py:1063
  74.3 25.2 %shard_map.213 = (bf16[512,1024]{1,0:T(8,128)(2,1)}, f32[512,1024]{1,0:T(8,128)}, bf16[1024,512]{1,0:T(8,128)(2,1)}, bf16[512,1024]{1,0:T(8,128)(2,1)}, bf16[512...) custom-call(bf16[512,1024]{1,0:T(8,128)(2,1)} %tokens.5, ...), custom_call_target="tpu_custom_call" | custom-call | flops 1000000 | bytes 100000 | tf_op jit(solution)/shard_map/pallas_call | solution.py:556
  99.6 4.1 collective-permute-start.3
  103.7 21.0 %shard_map.214 = (bf16[4,512,2048]{2,1,0:T(8,128)(2,1)}, bf16[4,2048,1024]{2,1,0:T(8,128)(2,1)}, bf16[1024,2048]{1,0:T(8,128)(2,1)}, bf16[2048,1024]{1,0:T(8,128...) custom-call(s32[1]{0:T(128)} %bitcast.9.refs_0_, bf16[512,1024]{1,0:T(8,128)(2,1)} %get-tuple-element.144.refs_1_.second, ...), custom_call_target="tpu_custom_call" | custom-call | flops 1000000 | bytes 100000 | tf_op jit(solution)/shard_map/pallas_call | solution.py:836
  127.7 19.8 %collective-permute-done.3.refs_1_ = bf16[512,1024]{1,0:T(8,128)(2,1)S(1)} collective-permute-done((bf16[512,1024]{1,0:T(8,128)(2,1)}, bf16[512,1024]{1,0:T(8,128)(2,1)S(1)}, u32[]{:S(2)}, u32[]{:S(2)}) %collective-permute-start.3) | collective-permute-done | bytes 1048608 | tf_op jit(solution)/shard_map/ppermute | solution.py:904
  147.7 3.9 collective-permute-start.5
  151.7 4.4 collective-permute-start.7
  156.1 20.8 %shard_map.215 = (bf16[4,512,2048]{2,1,0:T(8,128)(2,1)}, bf16[4,2048,1024]{2,1,0:T(8,128)(2,1)}, bf16[1024,2048]{1,0:T(8,128)(2,1)}, bf16[2048,1024]{1,0:T(8,128...) custom-call(s32[1]{0:T(128)} %bitcast.9.refs_0_, ...), custom_call_target="tpu_custom_call", output_to_operand_aliasing={{0}: (6, {}), {1}: (7, {}), {2}: (8, {}), {3}: (9, {})} | custom-call | flops 1000000 | bytes 100000 | tf_op jit(solution)/shard_map/pallas_call | solution.py:836
  176.9 20.8 %shard_map.216 = (bf16[4,512,2048]{2,1,0:T(8,128)(2,1)}, bf16[4,2048,1024]{2,1,0:T(8,128)(2,1)}, bf16[1024,2048]{1,0:T(8,128)(2,1)}, bf16[2048,1024]{1,0:T(8,128...) custom-call(s32[1]{0:T(128)} %bitcast.9.refs_0_, ...), custom_call_target="tpu_custom_call", output_to_operand_aliasing={{0}: (6, {}), {1}: (7, {}), {2}: (8, {}), {3}: (9, {})} | custom-call | flops 1000000 | bytes 100000 | tf_op jit(solution)/shard_map/pallas_call | solution.py:836
  199.9 21.0 %shard_map.217 = (bf16[4,512,2048]{2,1,0:T(8,128)(2,1)}, bf16[4,2048,1024]{2,1,0:T(8,128)(2,1)}, bf16[1024,2048]{1,0:T(8,128)(2,1)}, bf16[2048,1024]{1,0:T(8,128...) custom-call(s32[1]{0:T(128)} %bitcast.9.refs_0_, ...), custom_call_target="tpu_custom_call", output_to_operand_aliasing={{0}: (6, {}), {1}: (7, {}), {2}: (8, {}), {3}: (9, {})} | custom-call | flops 1000000 | bytes 100000 | tf_op jit(solution)/shard_map/pallas_call | solution.py:836
  224.3 34.9 %shard_map.218 = (bf16[2048,1024]{1,0:T(8,128)(2,1)}, bf16[1024,1024]{1,0:T(8,128)(2,1)}, bf16[2048,1024]{1,0:T(8,128)(2,1)}, bf16[1024,1024]{1,0:T(8,128)(2,1)}) custom-call(s32[1]{0:T(128)} %bitcast.8.base, bf16[1024,2048]{1,0:T(8,128)(2,1)} %get-tuple-element.179.second_t, bf16[2048,1024]{1,0:T(8,128)(2,1)} %get-tuple-element.180.dy, ...), custom_call_target="tpu_custom_call" | custom-call | flops 1000000 | bytes 100000 | tf_op jit(solution)/shard_map/pallas_call | solution.py:892
  263.7 6.3 %collective-permute-done.14 = bf16[1024,1024]{1,0:T(8,128)(2,1)S(1)} collective-permute-done((bf16[1024,1024]{1,0:T(8,128)(2,1)}, bf16[1024,1024]{1,0:T(8,128)(2,1)S(1)}, u32[]{:S(2)}, u32[]{:S(2)}) %collective-permute-start.14) | collective-permute-done | bytes 2097184 | tf_op jit(solution)/shard_map/ppermute | solution.py:951
  274.2 4.3 add_convert_fusion
  288.4 5.9 %collective-permute-done.11.back_right = bf16[512,1152]{1,0:T(8,128)(2,1)} collective-permute-done((bf16[512,1152]{1,0:T(8,128)(2,1)}, bf16[512,1152]{1,0:T(8,128)(2,1)}, u32[]{:S(2)}, u32[]{:S(2)}) %collective-permute-start.11) | collective-permute-done | bytes 1179680 | tf_op jit(solution)/shard_map/ppermute | solution.py:904
  294.3 24.3 %collective-permute-done.10.back_left = bf16[512,1152]{1,0:T(8,128)(2,1)} collective-permute-done((bf16[512,1152]{1,0:T(8,128)(2,1)}, bf16[512,1152]{1,0:T(8,128)(2,1)}, u32[]{:S(2)}, u32[]{:S(2)}) %collective-permute-start.10) | collective-permute-done | bytes 1179680 | tf_op jit(solution)/shard_map/ppermute | solution.py:904
  331.7 31.0 %shard_map.219 = (bf16[1024,1024]{1,0:T(8,128)(2,1)}, f32[128,1024]{1,0:T(8,128)}, f32[512,1024]{1,0:T(8,128)}, bf16[512,2048]{1,0:T(8,128)(2,1)}) custom-call(bf16[512,1024]{1,0:T(8,128)(2,1)} %tokens.5, bf16[512,1152]{1,0:T(8,128)(2,1)} %get-tuple-element.142.refs_2_.side, f32[512,1024]{1,0:T(8,128)} %get-tuple-element.141.middle, ...), custom_call_target="tpu_custom_call" | custom-call | flops 1000000 | bytes 100000 | tf_op jit(solution)/shard_map/pallas_call | solution.py:556
  371.7 3.9 collective-permute-start.22
  375.6 16.8 %shard_map.220 = (bf16[1024,3200]{1,0:T(8,128)(2,1)}, f32[512,1024]{1,0:T(8,128)}) custom-call(bf16[512,1024]{1,0:T(8,128)(2,1)} %tokens.5, bf16[1024,3200]{1,0:T(8,128)(2,1)} %bitcast.23, f32[512,1024]{1,0:T(8,128)} %get-tuple-element.238.grad_middle, bf16[512,2048]{1,0:T(8,128)(2,1)} %get-tuple-element.239.grad_pre, ...), custom_call_target="tpu_custom_call" | custom-call | flops 1000000 | bytes 100000 | tf_op jit(solution)/shard_map/pallas_call | solution.py:556
  397.7 97.1 %shard_map.221 = (bf16[1,8,32,3200]{3,2,1,0:T(8,128)(2,1)}, bf16[2,768,1024]{2,1,0:T(8,128)(2,1)}, bf16[2,768,1024]{2,1,0:T(8,128)(2,1)}) custom-call(bf16[4,8,32,3200]{3,2,1,0:T(8,128)(2,1)} %bitcast.31, bf16[768,1024]{1,0:T(8,128)(2,1)} %pad_maximum_fusion.1.refs_1_, bf16[768,1024]{1,0:T(8,128)(2,1)} %pad_maximum_fusion.2.refs_2_), custom_call_target="tpu_custom_call" | custom-call | bytes 3276800 | tf_op jit(solution)/shard_map/pallas_call | solution.py:384
  500.1 3.7 shard_map.225.refs_3_
  503.8 6.3 %shard_map.223.refs_3_ = f32[4096,1024]{1,0:T(8,128)} custom-call(s32[1]{0:T(128)} %bitcast.15.refs_0_, bf16[1536,1024]{1,0:T(8,128)(2,1)} %bitcast.30, bf16[1536,1024]{1,0:T(8,128)(2,1)} %bitcast.27), custom_call_target="tpu_custom_call" | custom-call | flops 1000000 | bytes 100000 | tf_op jit(solution)/shard_map/pallas_call | solution.py:1007
  515.9 3.7 shard_map.226
  519.6 5.9 %shard_map.224 = f32[4096,1024]{1,0:T(8,128)} custom-call(s32[1]{0:T(128)} %bitcast.14.refs_0_, bf16[1536,1024]{1,0:T(8,128)(2,1)} %copy-done.2, bf16[1536,1024]{1,0:T(8,128)(2,1)} %collective-permute-done.25.refs_2_, f32[4096,1024]{1,0:T(8,128)} %shard_map.223.refs_3_), custom_call_target="tpu_custom_call", output_to_operand_aliasing={{}: (3, {})} | custom-call | flops 1000000 | bytes 100000 | tf_op jit(solution)/shard_map/pallas_call | solution.py:1007
  (145 shorter events, 77.0 us)
Async XLA Ops:
  61.4 38.1 %collective-permute-start = (bf16[512,1152]{1,0:T(8,128)(2,1)}, bf16[512,1152]{1,0:T(8,128)(2,1)S(1)}, u32[]{:S(2)}, u32[]{:S(2)}) collective-permute-start(bf16[512,1152]{1,0:T(8,128)(2,1)} %get-tuple-element.142.refs_2_.side), channel_id=1, source_target_pairs={{3,0},{7,4},{11,8},{15,12},{19,16},{23,20},{27,24},{31,28}} | collective-permute-start | bytes 3538952 | tf_op jit(solution)/shard_map/ppermute | solution.py:1063
  62.7 36.8 %collective-permute-start.1 = (bf16[512,1152]{1,0:T(8,128)(2,1)}, bf16[512,1152]{1,0:T(8,128)(2,1)S(1)}, u32[]{:S(2)}, u32[]{:S(2)}) collective-permute-start(bf16[512,1152]{1,0:T(8,128)(2,1)} %get-tuple-element.142.refs_2_.side), channel_id=1, source_target_pairs={{0,3},{4,7},{8,11},{12,15},{16,19},{20,23},{24,27},{28,31}} | collective-permute-start | bytes 3538952 | tf_op jit(solution)/shard_map/ppermute | solution.py:1063
  99.5 28.1 %collective-permute-start.2 = (bf16[512,1024]{1,0:T(8,128)(2,1)}, bf16[512,1024]{1,0:T(8,128)(2,1)S(1)}, u32[]{:S(2)}, u32[]{:S(2)}) collective-permute-start(bf16[512,1024]{1,0:T(8,128)(2,1)} %get-tuple-element.144.refs_1_.second), channel_id=1, source_target_pairs={{0,1},{1,2},{2,3},{3,0},{4,5},{5,6},{6,7},{7,4},{8,9},{9,10},{10,1... | collective-permute-start | bytes 3145736 | tf_op jit(solution)/shard_map/ppermute | solution.py:904
  99.6 47.9 %collective-permute-start.3 = (bf16[512,1024]{1,0:T(8,128)(2,1)}, bf16[512,1024]{1,0:T(8,128)(2,1)S(1)}, u32[]{:S(2)}, u32[]{:S(2)}) collective-permute-start(bf16[512,1024]{1,0:T(8,128)(2,1)} %get-tuple-element.144.refs_1_.second), channel_id=1, source_target_pairs={{0,3},{1,0},{2,1},{3,2},{4,7},{5,4},{6,5},{7,6},{8,11},{9,8},{10,9... | collective-permute-start | bytes 3145736 | tf_op jit(solution)/shard_map/ppermute | solution.py:904
  147.5 50.2 %collective-permute-start.4 = (bf16[256,1024]{1,0:T(8,128)(2,1)S(1)}, bf16[256,1024]{1,0:T(8,128)(2,1)S(1)}, u32[]{:S(2)}, u32[]{:S(2)}) collective-permute-start(bf16[256,1024]{1,0:T(8,128)(2,1)S(1)} %slice.67), channel_id=1, source_target_pairs={{0,1},{1,2},{2,3},{3,0},{4,5},{5,6},{6,7},{7,4},{8,9},{9,10},{10,1... | collective-permute-start | bytes 1572872 | tf_op jit(solution)/shard_map/ppermute | solution.py:904
  147.7 50.1 %collective-permute-start.5 = (bf16[256,1024]{1,0:T(8,128)(2,1)S(1)}, bf16[256,1024]{1,0:T(8,128)(2,1)S(1)}, u32[]{:S(2)}, u32[]{:S(2)}) collective-permute-start(bf16[256,1024]{1,0:T(8,128)(2,1)S(1)} %slice.68), channel_id=1, source_target_pairs={{0,3},{1,0},{2,1},{3,2},{4,7},{5,4},{6,5},{7,6},{8,11},{9,8},{10,9... | collective-permute-start | bytes 1572872 | tf_op jit(solution)/shard_map/ppermute | solution.py:904
  151.6 47.2 %collective-permute-start.6 = (bf16[256,1152]{1,0:T(8,128)(2,1)S(1)}, bf16[256,1152]{1,0:T(8,128)(2,1)S(1)}, u32[]{:S(2)}, u32[]{:S(2)}) collective-permute-start(bf16[256,1152]{1,0:T(8,128)(2,1)S(1)} %slice.69), channel_id=1, source_target_pairs={{0,1},{1,2},{2,3},{3,0},{4,5},{5,6},{6,7},{7,4},{8,9},{9,10},{10,1... | collective-permute-start | bytes 1769480 | tf_op jit(solution)/shard_map/ppermute | solution.py:904
  151.7 47.1 %collective-permute-start.7 = (bf16[256,1152]{1,0:T(8,128)(2,1)S(1)}, bf16[256,1152]{1,0:T(8,128)(2,1)S(1)}, u32[]{:S(2)}, u32[]{:S(2)}) collective-permute-start(bf16[256,1152]{1,0:T(8,128)(2,1)S(1)} %slice.70), channel_id=1, source_target_pairs={{0,3},{1,0},{2,1},{3,2},{4,7},{5,4},{6,5},{7,6},{8,11},{9,8},{10,9... | collective-permute-start | bytes 1769480 | tf_op jit(solution)/shard_map/ppermute | solution.py:904
  222.2 37.0 %collective-permute-start.8 = (bf16[256,1152]{1,0:T(8,128)(2,1)S(1)}, bf16[256,1152]{1,0:T(8,128)(2,1)S(1)}, u32[]{:S(2)}, u32[]{:S(2)}) collective-permute-start(bf16[256,1152]{1,0:T(8,128)(2,1)S(1)} %get-tuple-element.320), channel_id=1, source_target_pairs={{0,3},{1,0},{2,1},{3,2},{4,7},{5,4},{6,5},{7,6},{8,11},{9,8},{10,9... | collective-permute-start | bytes 1769480 | tf_op jit(solution)/shard_map/ppermute | solution.py:904
  222.6 36.6 %collective-permute-start.9 = (bf16[256,1152]{1,0:T(8,128)(2,1)S(1)}, bf16[256,1152]{1,0:T(8,128)(2,1)}, u32[]{:S(2)}, u32[]{:S(2)}) collective-permute-start(bf16[256,1152]{1,0:T(8,128)(2,1)S(1)} %get-tuple-element.319), channel_id=1, source_target_pairs={{0,1},{1,2},{2,3},{3,0},{4,5},{5,6},{6,7},{7,4},{8,9},{9,10},{10,1... | collective-permute-start | bytes 1769480 | tf_op jit(solution)/shard_map/ppermute | solution.py:904
  263.1 31.2 %collective-permute-start.11 = (bf16[512,1152]{1,0:T(8,128)(2,1)}, bf16[512,1152]{1,0:T(8,128)(2,1)}, u32[]{:S(2)}, u32[]{:S(2)}) collective-permute-start(bf16[512,1152]{1,0:T(8,128)(2,1)} %pad_maximum_fusion.5), channel_id=1, source_target_pairs={{0,1},{1,2},{2,3},{3,0},{4,5},{5,6},{6,7},{7,4},{8,9},{9,10},{10,1... | collective-permute-start | bytes 3538952 | tf_op jit(solution)/shard_map/ppermute | solution.py:904
  281.3 37.3 %collective-permute-start.15 = (bf16[768,1024]{1,0:T(8,128)(2,1)}, bf16[768,1024]{1,0:T(8,128)(2,1)}, u32[]{:S(2)}, u32[]{:S(2)}) collective-permute-start(bf16[768,1024]{1,0:T(8,128)(2,1)} %fusion), channel_id=1, source_target_pairs={{0,16},{4,20},{8,24},{12,28},{16,0},{20,4},{24,8},{28,12},{1,17},{... | collective-permute-start | bytes 4718600 | tf_op jit(solution)/shard_map/ppermute | solution.py:951
  282.7 37.2 %collective-permute-start.13 = (bf16[768,1024]{1,0:T(8,128)(2,1)}, bf16[768,1024]{1,0:T(8,128)(2,1)}, u32[]{:S(2)}, u32[]{:S(2)}) collective-permute-start(bf16[768,1024]{1,0:T(8,128)(2,1)} %constant_dynamic-slice_fusion.2), channel_id=1, source_target_pairs={{0,8},{4,12},{8,0},{12,4},{16,24},{20,28},{24,16},{28,20},{1,9},{5... | collective-permute-start | bytes 4718600 | tf_op jit(solution)/shard_map/ppermute | solution.py:951
  286.2 32.4 %collective-permute-start.10 = (bf16[512,1152]{1,0:T(8,128)(2,1)}, bf16[512,1152]{1,0:T(8,128)(2,1)}, u32[]{:S(2)}, u32[]{:S(2)}) collective-permute-start(bf16[512,1152]{1,0:T(8,128)(2,1)} %pad_maximum_fusion.4), channel_id=1, source_target_pairs={{0,3},{1,0},{2,1},{3,2},{4,7},{5,4},{6,5},{7,6},{8,11},{9,8},{10,9... | collective-permute-start | bytes 3538952 | tf_op jit(solution)/shard_map/ppermute | solution.py:904
  325.2 37.5 %collective-permute-start.16 = (bf16[384,1024]{1,0:T(8,128)(2,1)}, bf16[384,1024]{1,0:T(8,128)(2,1)}, u32[]{:S(2)}, u32[]{:S(2)}) collective-permute-start(bf16[384,1024]{1,0:T(8,128)(2,1)} %constant_dynamic-slice_fusion.1), channel_id=1, source_target_pairs={{0,16},{4,20},{8,24},{12,28},{16,0},{20,4},{24,8},{28,12},{1,17},{... | collective-permute-start | bytes 2359304 | tf_op jit(solution)/shard_map/ppermute | solution.py:951
  327.7 35.1 %collective-permute-start.17 = (bf16[384,1024]{1,0:T(8,128)(2,1)}, bf16[384,1024]{1,0:T(8,128)(2,1)}, u32[]{:S(2)}, u32[]{:S(2)}) collective-permute-start(bf16[384,1024]{1,0:T(8,128)(2,1)} %constant_dynamic-slice_fusion), channel_id=1, source_target_pairs={{0,8},{4,12},{8,0},{12,4},{16,24},{20,28},{24,16},{28,20},{1,9},{5... | collective-permute-start | bytes 2359304 | tf_op jit(solution)/shard_map/ppermute | solution.py:951
  329.3 33.4 %collective-permute-start.18 = (bf16[256,1024]{1,0:T(8,128)(2,1)}, bf16[256,1024]{1,0:T(8,128)(2,1)}, u32[]{:S(2)}, u32[]{:S(2)}) collective-permute-start(bf16[256,1024]{1,0:T(8,128)(2,1)} %get-tuple-element.322), channel_id=1, source_target_pairs={{0,3},{1,0},{2,1},{3,2},{4,7},{5,4},{6,5},{7,6},{8,11},{9,8},{10,9... | collective-permute-start | bytes 1572872 | tf_op jit(solution)/shard_map/ppermute | solution.py:904
  331.2 31.6 %collective-permute-start.19 = (bf16[256,1024]{1,0:T(8,128)(2,1)}, bf16[256,1024]{1,0:T(8,128)(2,1)}, u32[]{:S(2)}, u32[]{:S(2)}) collective-permute-start(bf16[256,1024]{1,0:T(8,128)(2,1)} %get-tuple-element.321), channel_id=1, source_target_pairs={{0,1},{1,2},{2,3},{3,0},{4,5},{5,6},{6,7},{7,4},{8,9},{9,10},{10,1... | collective-permute-start | bytes 1572872 | tf_op jit(solution)/shard_map/ppermute | solution.py:904
  366.7 25.8 %collective-permute-start.20 = (bf16[384,1024]{1,0:T(8,128)(2,1)S(1)}, bf16[384,1024]{1,0:T(8,128)(2,1)}, u32[]{:S(2)}, u32[]{:S(2)}) collective-permute-start(bf16[384,1024]{1,0:T(8,128)(2,1)S(1)} %add_convert_fusion.6), channel_id=1, source_target_pairs={{0,16},{4,20},{8,24},{12,28},{16,0},{20,4},{24,8},{28,12},{1,17},{... | collective-permute-start | bytes 2359304 | tf_op jit(solution)/shard_map/ppermute | solution.py:951
  368.5 24.0 %collective-permute-start.21 = (bf16[384,1024]{1,0:T(8,128)(2,1)}, bf16[384,1024]{1,0:T(8,128)(2,1)}, u32[]{:S(2)}, u32[]{:S(2)}) collective-permute-start(bf16[384,1024]{1,0:T(8,128)(2,1)} %add_convert_fusion.5), channel_id=1, source_target_pairs={{0,8},{4,12},{8,0},{12,4},{16,24},{20,28},{24,16},{28,20},{1,9},{5... | collective-permute-start | bytes 2359304 | tf_op jit(solution)/shard_map/ppermute | solution.py:951
  370.1 124.7 %collective-permute-start.23 = (bf16[512,1024]{1,0:T(8,128)(2,1)S(1)}, bf16[512,1024]{1,0:T(8,128)(2,1)}, u32[]{:S(2)}, u32[]{:S(2)}) collective-permute-start(bf16[512,1024]{1,0:T(8,128)(2,1)S(1)} %pad_maximum_fusion.8), channel_id=1, source_target_pairs={{0,1},{1,2},{2,3},{3,0},{4,5},{5,6},{6,7},{7,4},{8,9},{9,10},{10,1... | collective-permute-start | bytes 3145736 | tf_op jit(solution)/shard_map/ppermute | solution.py:904
  371.7 123.1 %collective-permute-start.22 = (bf16[512,1024]{1,0:T(8,128)(2,1)S(1)}, bf16[512,1024]{1,0:T(8,128)(2,1)}, u32[]{:S(2)}, u32[]{:S(2)}) collective-permute-start(bf16[512,1024]{1,0:T(8,128)(2,1)S(1)} %pad_maximum_fusion.7), channel_id=1, source_target_pairs={{0,3},{1,0},{2,1},{3,2},{4,7},{5,4},{6,5},{7,6},{8,11},{9,8},{10,9... | collective-permute-start | bytes 3145736 | tf_op jit(solution)/shard_map/ppermute | solution.py:904
  494.8 19.4 %collective-permute-start.24 = (bf16[1536,1024]{1,0:T(8,128)(2,1)}, bf16[1536,1024]{1,0:T(8,128)(2,1)S(1)}, u32[]{:S(2)}, u32[]{:S(2)}) collective-permute-start(bf16[1536,1024]{1,0:T(8,128)(2,1)} %bitcast.28), channel_id=1, source_target_pairs={{0,4},{4,0},{8,12},{12,8},{16,20},{20,16},{24,28},{28,24},{1,5},{5... | collective-permute-start | bytes 9437192 | tf_op jit(solution)/shard_map/ppermute | solution.py:951
  495.2 19.0 %collective-permute-start.25 = (bf16[1536,1024]{1,0:T(8,128)(2,1)}, bf16[1536,1024]{1,0:T(8,128)(2,1)}, u32[]{:S(2)}, u32[]{:S(2)}) collective-permute-start(bf16[1536,1024]{1,0:T(8,128)(2,1)} %bitcast.25), channel_id=1, source_target_pairs={{0,4},{4,0},{8,12},{12,8},{16,20},{20,16},{24,28},{28,24},{1,5},{5... | collective-permute-start | bytes 9437192 | tf_op jit(solution)/shard_map/ppermute | solution.py:951
  (25 other events, 294.3 us)

commit v6 on v5

--- a/solution.py
+++ b/solution.py
@@ -316,7 +316,6 @@
     steps = spread_steps(
         (upper, lower), (upper_out, lower_out), last_orders(bits), rep_at, shard_at, s_send, s_recv
     )
-    next(steps, None)
     for at in range(bits):
         many = reps // 2 ** (at + 1)
         for half in range(HALVES):

time: 533 us -> 525 us (0.985)
  Pallas kernels: 367 us -> 359 us
    pallas_call x1, Pallas kernels: 97.1 us -> 88.9 us  [reduce_all(): pl.pallas_call(lambda *refs: reduce_kernel(reps, shard_count, *refs), out...]
where the time goes in v6:
time: 525 us; the launch traced here: 518 us
  Pallas kernels  359 us (68%)
  waiting for transfers between devices  59.2 us (11%)
  starting transfers between devices  38.8 us (7%)
  other arithmetic  38.5 us (7%)
  local copies, waits for them, and re-layouts  20.6 us (4%)
    pallas_call x1, Pallas kernels, reduce_all(): pl.pallas_call(lambda *refs: reduce_kernel(reps, shard_count, *refs), out...  88.9 us
    pallas_call x4, Pallas kernels, expert_block(): pl.pallas_call(lambda *refs: expert_kernel(bool(before), *refs), grid=(ex...  83.6 us
    pallas_call x4, Pallas kernels, local_call(): pl.pallas_call(kernel, out_shape=outs, in_specs=[pl.BlockSpec(memory_spac...  76.2 us
    pallas_call x1, Pallas kernels, gather_all(): pl.pallas_call(lambda *refs: gather_kernel(reps, shard_count, *refs), out...  55.8 us
    ppermute x14, waiting for transfers between devices, shift(): lax.ppermute(block, 'shard', [(at, (at + step) % count) for at in range(c...  51.6 us
    pallas_call x1, Pallas kernels, weight_block(): pl.pallas_call(weight_kernel, grid_spec=grid_spec, out_shape=pair * 2, co...  34.9 us
    ppermute x14, starting transfers between devices, shift(): lax.ppermute(block, 'shard', [(at, (at + step) % count) for at in range(c...  23.5 us
    pallas_call x4, Pallas kernels, place_half(): pl.pallas_call(lambda *refs: place_kernel(first, cut, *refs), grid_spec=g...  19.6 us
  transfers between devices with their start and end apart: 26, of which 6 were waited for; matrix products, arithmetic and copies ran while one was open for 7% of the time, Pallas kernels for 53%

profile of v6, /device:TPU:0, one launch (start us, length us, event | category | flops | bytes accessed | tf_op | source)
XLA Modules:
  0.0 517.6 jit_solution(13576918071650415287)
XLA Ops:
  5.6 55.8 %shard_map.212 = (bf16[4,8,32,3200]{3,2,1,0:T(8,128)(2,1)}, bf16[512,1152]{1,0:T(8,128)(2,1)}, bf16[512,1152]{1,0:T(8,128)(2,1)}, bf16[512,1152]{1,0:T(8,128)(2,1)}) custom-call(bf16[8,32,1024]{2,1,0:T(8,128)(2,1)} %bitcast.34, bf16[8,32,512]{2,1,0:T(8,128)(2,1)} %bitcast.36, bf16[8,32,512]{2,1,0:T(8,128)(2,1)} %bitcast.37, bf16[8,32,1024]{2,1,0:T(8,128)(2,1)} %bitcast.35, ...), custom_call_target="tpu_custom_call" | custom-call | bytes 3276800 | tf_op jit(solution)/shard_map/pallas_call | solution.py:231
  62.7 6.5 %collective-permute-start.1 = (bf16[512,1152]{1,0:T(8,128)(2,1)}, bf16[512,1152]{1,0:T(8,128)(2,1)S(1)}, u32[]{:S(2)}, u32[]{:S(2)}) collective-permute-start(bf16[512,1152]{1,0:T(8,128)(2,1)} %get-tuple-element.142.refs_2_.side), channel_id=1, source_target_pairs={{0,3},{4,7},{8,11},{12,15},{16,19},{20,23},{24,27},{28,31}} | collective-permute-start | bytes 3538952 | tf_op jit(solution)/shard_map/ppermute | solution.py:1062
  74.3 25.2 %shard_map.213 = (bf16[512,1024]{1,0:T(8,128)(2,1)}, f32[512,1024]{1,0:T(8,128)}, bf16[1024,512]{1,0:T(8,128)(2,1)}, bf16[512,1024]{1,0:T(8,128)(2,1)}, bf16[512...) custom-call(bf16[512,1024]{1,0:T(8,128)(2,1)} %tokens.5, ...), custom_call_target="tpu_custom_call" | custom-call | flops 1000000 | bytes 100000 | tf_op jit(solution)/shard_map/pallas_call | solution.py:555
  99.6 4.1 collective-permute-start.3
  103.7 21.0 %shard_map.214 = (bf16[4,512,2048]{2,1,0:T(8,128)(2,1)}, bf16[4,2048,1024]{2,1,0:T(8,128)(2,1)}, bf16[1024,2048]{1,0:T(8,128)(2,1)}, bf16[2048,1024]{1,0:T(8,128...) custom-call(s32[1]{0:T(128)} %bitcast.9.refs_0_, bf16[512,1024]{1,0:T(8,128)(2,1)} %get-tuple-element.144.refs_1_.second, ...), custom_call_target="tpu_custom_call" | custom-call | flops 1000000 | bytes 100000 | tf_op jit(solution)/shard_map/pallas_call | solution.py:835
  127.7 19.8 %collective-permute-done.3.refs_1_ = bf16[512,1024]{1,0:T(8,128)(2,1)S(1)} collective-permute-done((bf16[512,1024]{1,0:T(8,128)(2,1)}, bf16[512,1024]{1,0:T(8,128)(2,1)S(1)}, u32[]{:S(2)}, u32[]{:S(2)}) %collective-permute-start.3) | collective-permute-done | bytes 1048608 | tf_op jit(solution)/shard_map/ppermute | solution.py:903
  147.7 3.9 collective-permute-start.5
  151.7 4.4 collective-permute-start.7
  156.1 20.8 %shard_map.215 = (bf16[4,512,2048]{2,1,0:T(8,128)(2,1)}, bf16[4,2048,1024]{2,1,0:T(8,128)(2,1)}, bf16[1024,2048]{1,0:T(8,128)(2,1)}, bf16[2048,1024]{1,0:T(8,128...) custom-call(s32[1]{0:T(128)} %bitcast.9.refs_0_, ...), custom_call_target="tpu_custom_call", output_to_operand_aliasing={{0}: (6, {}), {1}: (7, {}), {2}: (8, {}), {3}: (9, {})} | custom-call | flops 1000000 | bytes 100000 | tf_op jit(solution)/shard_map/pallas_call | solution.py:835
  176.9 20.8 %shard_map.216 = (bf16[4,512,2048]{2,1,0:T(8,128)(2,1)}, bf16[4,2048,1024]{2,1,0:T(8,128)(2,1)}, bf16[1024,2048]{1,0:T(8,128)(2,1)}, bf16[2048,1024]{1,0:T(8,128...) custom-call(s32[1]{0:T(128)} %bitcast.9.refs_0_, ...), custom_call_target="tpu_custom_call", output_to_operand_aliasing={{0}: (6, {}), {1}: (7, {}), {2}: (8, {}), {3}: (9, {})} | custom-call | flops 1000000 | bytes 100000 | tf_op jit(solution)/shard_map/pallas_call | solution.py:835
  199.9 21.0 %shard_map.217 = (bf16[4,512,2048]{2,1,0:T(8,128)(2,1)}, bf16[4,2048,1024]{2,1,0:T(8,128)(2,1)}, bf16[1024,2048]{1,0:T(8,128)(2,1)}, bf16[2048,1024]{1,0:T(8,128...) custom-call(s32[1]{0:T(128)} %bitcast.9.refs_0_, ...), custom_call_target="tpu_custom_call", output_to_operand_aliasing={{0}: (6, {}), {1}: (7, {}), {2}: (8, {}), {3}: (9, {})} | custom-call | flops 1000000 | bytes 100000 | tf_op jit(solution)/shard_map/pallas_call | solution.py:835
  224.3 34.9 %shard_map.218 = (bf16[2048,1024]{1,0:T(8,128)(2,1)}, bf16[1024,1024]{1,0:T(8,128)(2,1)}, bf16[2048,1024]{1,0:T(8,128)(2,1)}, bf16[1024,1024]{1,0:T(8,128)(2,1)}) custom-call(s32[1]{0:T(128)} %bitcast.8.base, bf16[1024,2048]{1,0:T(8,128)(2,1)} %get-tuple-element.179.second_t, bf16[2048,1024]{1,0:T(8,128)(2,1)} %get-tuple-element.180.dy, ...), custom_call_target="tpu_custom_call" | custom-call | flops 1000000 | bytes 100000 | tf_op jit(solution)/shard_map/pallas_call | solution.py:891
  263.7 6.3 %collective-permute-done.14 = bf16[1024,1024]{1,0:T(8,128)(2,1)S(1)} collective-permute-done((bf16[1024,1024]{1,0:T(8,128)(2,1)}, bf16[1024,1024]{1,0:T(8,128)(2,1)S(1)}, u32[]{:S(2)}, u32[]{:S(2)}) %collective-permute-start.14) | collective-permute-done | bytes 2097184 | tf_op jit(solution)/shard_map/ppermute | solution.py:950
  274.2 4.3 add_convert_fusion
  288.4 5.9 %collective-permute-done.11.back_right = bf16[512,1152]{1,0:T(8,128)(2,1)} collective-permute-done((bf16[512,1152]{1,0:T(8,128)(2,1)}, bf16[512,1152]{1,0:T(8,128)(2,1)}, u32[]{:S(2)}, u32[]{:S(2)}) %collective-permute-start.11) | collective-permute-done | bytes 1179680 | tf_op jit(solution)/shard_map/ppermute | solution.py:903
  294.3 24.3 %collective-permute-done.10.back_left = bf16[512,1152]{1,0:T(8,128)(2,1)} collective-permute-done((bf16[512,1152]{1,0:T(8,128)(2,1)}, bf16[512,1152]{1,0:T(8,128)(2,1)}, u32[]{:S(2)}, u32[]{:S(2)}) %collective-permute-start.10) | collective-permute-done | bytes 1179680 | tf_op jit(solution)/shard_map/ppermute | solution.py:903
  331.7 31.0 %shard_map.219 = (bf16[1024,1024]{1,0:T(8,128)(2,1)}, f32[128,1024]{1,0:T(8,128)}, f32[512,1024]{1,0:T(8,128)}, bf16[512,2048]{1,0:T(8,128)(2,1)}) custom-call(bf16[512,1024]{1,0:T(8,128)(2,1)} %tokens.5, bf16[512,1152]{1,0:T(8,128)(2,1)} %get-tuple-element.142.refs_2_.side, f32[512,1024]{1,0:T(8,128)} %get-tuple-element.141.middle, ...), custom_call_target="tpu_custom_call" | custom-call | flops 1000000 | bytes 100000 | tf_op jit(solution)/shard_map/pallas_call | solution.py:555
  371.7 3.9 collective-permute-start.22
  375.6 16.8 %shard_map.220 = (bf16[1024,3200]{1,0:T(8,128)(2,1)}, f32[512,1024]{1,0:T(8,128)}) custom-call(bf16[512,1024]{1,0:T(8,128)(2,1)} %tokens.5, bf16[1024,3200]{1,0:T(8,128)(2,1)} %bitcast.23, f32[512,1024]{1,0:T(8,128)} %get-tuple-element.238.grad_middle, bf16[512,2048]{1,0:T(8,128)(2,1)} %get-tuple-element.239.grad_pre, ...), custom_call_target="tpu_custom_call" | custom-call | flops 1000000 | bytes 100000 | tf_op jit(solution)/shard_map/pallas_call | solution.py:555
  397.7 88.9 %shard_map.221 = (bf16[1,8,32,3200]{3,2,1,0:T(8,128)(2,1)}, bf16[2,768,1024]{2,1,0:T(8,128)(2,1)}, bf16[2,768,1024]{2,1,0:T(8,128)(2,1)}) custom-call(bf16[4,8,32,3200]{3,2,1,0:T(8,128)(2,1)} %bitcast.31, bf16[768,1024]{1,0:T(8,128)(2,1)} %pad_maximum_fusion.1.refs_1_, bf16[768,1024]{1,0:T(8,128)(2,1)} %pad_maximum_fusion.2.refs_2_), custom_call_target="tpu_custom_call" | custom-call | bytes 3276800 | tf_op jit(solution)/shard_map/pallas_call | solution.py:383
  491.9 3.7 shard_map.225.refs_3_
  495.6 6.3 %shard_map.223.refs_3_ = f32[4096,1024]{1,0:T(8,128)} custom-call(s32[1]{0:T(128)} %bitcast.15.refs_0_, bf16[1536,1024]{1,0:T(8,128)(2,1)} %bitcast.30, bf16[1536,1024]{1,0:T(8,128)(2,1)} %bitcast.27), custom_call_target="tpu_custom_call" | custom-call | flops 1000000 | bytes 100000 | tf_op jit(solution)/shard_map/pallas_call | solution.py:1006
  507.8 3.7 shard_map.226
  511.5 5.9 %shard_map.224 = f32[4096,1024]{1,0:T(8,128)} custom-call(s32[1]{0:T(128)} %bitcast.14.refs_0_, bf16[1536,1024]{1,0:T(8,128)(2,1)} %copy-done.2, bf16[1536,1024]{1,0:T(8,128)(2,1)} %collective-permute-done.25.refs_2_, f32[4096,1024]{1,0:T(8,128)} %shard_map.223.refs_3_), custom_call_target="tpu_custom_call", output_to_operand_aliasing={{}: (3, {})} | custom-call | flops 1000000 | bytes 100000 | tf_op jit(solution)/shard_map/pallas_call | solution.py:1006
  (145 shorter events, 77.0 us)
Async XLA Ops:
  61.4 38.1 %collective-permute-start = (bf16[512,1152]{1,0:T(8,128)(2,1)}, bf16[512,1152]{1,0:T(8,128)(2,1)S(1)}, u32[]{:S(2)}, u32[]{:S(2)}) collective-permute-start(bf16[512,1152]{1,0:T(8,128)(2,1)} %get-tuple-element.142.refs_2_.side), channel_id=1, source_target_pairs={{3,0},{7,4},{11,8},{15,12},{19,16},{23,20},{27,24},{31,28}} | collective-permute-start | bytes 3538952 | tf_op jit(solution)/shard_map/ppermute | solution.py:1062
  62.7 36.8 %collective-permute-start.1 = (bf16[512,1152]{1,0:T(8,128)(2,1)}, bf16[512,1152]{1,0:T(8,128)(2,1)S(1)}, u32[]{:S(2)}, u32[]{:S(2)}) collective-permute-start(bf16[512,1152]{1,0:T(8,128)(2,1)} %get-tuple-element.142.refs_2_.side), channel_id=1, source_target_pairs={{0,3},{4,7},{8,11},{12,15},{16,19},{20,23},{24,27},{28,31}} | collective-permute-start | bytes 3538952 | tf_op jit(solution)/shard_map/ppermute | solution.py:1062
  99.5 28.1 %collective-permute-start.2 = (bf16[512,1024]{1,0:T(8,128)(2,1)}, bf16[512,1024]{1,0:T(8,128)(2,1)S(1)}, u32[]{:S(2)}, u32[]{:S(2)}) collective-permute-start(bf16[512,1024]{1,0:T(8,128)(2,1)} %get-tuple-element.144.refs_1_.second), channel_id=1, source_target_pairs={{0,1},{1,2},{2,3},{3,0},{4,5},{5,6},{6,7},{7,4},{8,9},{9,10},{10,1... | collective-permute-start | bytes 3145736 | tf_op jit(solution)/shard_map/ppermute | solution.py:903
  99.6 47.9 %collective-permute-start.3 = (bf16[512,1024]{1,0:T(8,128)(2,1)}, bf16[512,1024]{1,0:T(8,128)(2,1)S(1)}, u32[]{:S(2)}, u32[]{:S(2)}) collective-permute-start(bf16[512,1024]{1,0:T(8,128)(2,1)} %get-tuple-element.144.refs_1_.second), channel_id=1, source_target_pairs={{0,3},{1,0},{2,1},{3,2},{4,7},{5,4},{6,5},{7,6},{8,11},{9,8},{10,9... | collective-permute-start | bytes 3145736 | tf_op jit(solution)/shard_map/ppermute | solution.py:903
  147.5 50.2 %collective-permute-start.4 = (bf16[256,1024]{1,0:T(8,128)(2,1)S(1)}, bf16[256,1024]{1,0:T(8,128)(2,1)S(1)}, u32[]{:S(2)}, u32[]{:S(2)}) collective-permute-start(bf16[256,1024]{1,0:T(8,128)(2,1)S(1)} %slice.67), channel_id=1, source_target_pairs={{0,1},{1,2},{2,3},{3,0},{4,5},{5,6},{6,7},{7,4},{8,9},{9,10},{10,1... | collective-permute-start | bytes 1572872 | tf_op jit(solution)/shard_map/ppermute | solution.py:903
  147.7 50.1 %collective-permute-start.5 = (bf16[256,1024]{1,0:T(8,128)(2,1)S(1)}, bf16[256,1024]{1,0:T(8,128)(2,1)S(1)}, u32[]{:S(2)}, u32[]{:S(2)}) collective-permute-start(bf16[256,1024]{1,0:T(8,128)(2,1)S(1)} %slice.68), channel_id=1, source_target_pairs={{0,3},{1,0},{2,1},{3,2},{4,7},{5,4},{6,5},{7,6},{8,11},{9,8},{10,9... | collective-permute-start | bytes 1572872 | tf_op jit(solution)/shard_map/ppermute | solution.py:903
  151.6 47.2 %collective-permute-start.6 = (bf16[256,1152]{1,0:T(8,128)(2,1)S(1)}, bf16[256,1152]{1,0:T(8,128)(2,1)S(1)}, u32[]{:S(2)}, u32[]{:S(2)}) collective-permute-start(bf16[256,1152]{1,0:T(8,128)(2,1)S(1)} %slice.69), channel_id=1, source_target_pairs={{0,1},{1,2},{2,3},{3,0},{4,5},{5,6},{6,7},{7,4},{8,9},{9,10},{10,1... | collective-permute-start | bytes 1769480 | tf_op jit(solution)/shard_map/ppermute | solution.py:903
  151.7 47.1 %collective-permute-start.7 = (bf16[256,1152]{1,0:T(8,128)(2,1)S(1)}, bf16[256,1152]{1,0:T(8,128)(2,1)S(1)}, u32[]{:S(2)}, u32[]{:S(2)}) collective-permute-start(bf16[256,1152]{1,0:T(8,128)(2,1)S(1)} %slice.70), channel_id=1, source_target_pairs={{0,3},{1,0},{2,1},{3,2},{4,7},{5,4},{6,5},{7,6},{8,11},{9,8},{10,9... | collective-permute-start | bytes 1769480 | tf_op jit(solution)/shard_map/ppermute | solution.py:903
  222.2 37.0 %collective-permute-start.8 = (bf16[256,1152]{1,0:T(8,128)(2,1)S(1)}, bf16[256,1152]{1,0:T(8,128)(2,1)S(1)}, u32[]{:S(2)}, u32[]{:S(2)}) collective-permute-start(bf16[256,1152]{1,0:T(8,128)(2,1)S(1)} %get-tuple-element.320), channel_id=1, source_target_pairs={{0,3},{1,0},{2,1},{3,2},{4,7},{5,4},{6,5},{7,6},{8,11},{9,8},{10,9... | collective-permute-start | bytes 1769480 | tf_op jit(solution)/shard_map/ppermute | solution.py:903
  222.6 36.6 %collective-permute-start.9 = (bf16[256,1152]{1,0:T(8,128)(2,1)S(1)}, bf16[256,1152]{1,0:T(8,128)(2,1)}, u32[]{:S(2)}, u32[]{:S(2)}) collective-permute-start(bf16[256,1152]{1,0:T(8,128)(2,1)S(1)} %get-tuple-element.319), channel_id=1, source_target_pairs={{0,1},{1,2},{2,3},{3,0},{4,5},{5,6},{6,7},{7,4},{8,9},{9,10},{10,1... | collective-permute-start | bytes 1769480 | tf_op jit(solution)/shard_map/ppermute | solution.py:903
  263.1 31.2 %collective-permute-start.11 = (bf16[512,1152]{1,0:T(8,128)(2,1)}, bf16[512,1152]{1,0:T(8,128)(2,1)}, u32[]{:S(2)}, u32[]{:S(2)}) collective-permute-start(bf16[512,1152]{1,0:T(8,128)(2,1)} %pad_maximum_fusion.5), channel_id=1, source_target_pairs={{0,1},{1,2},{2,3},{3,0},{4,5},{5,6},{6,7},{7,4},{8,9},{9,10},{10,1... | collective-permute-start | bytes 3538952 | tf_op jit(solution)/shard_map/ppermute | solution.py:903
  281.3 37.3 %collective-permute-start.15 = (bf16[768,1024]{1,0:T(8,128)(2,1)}, bf16[768,1024]{1,0:T(8,128)(2,1)}, u32[]{:S(2)}, u32[]{:S(2)}) collective-permute-start(bf16[768,1024]{1,0:T(8,128)(2,1)} %fusion), channel_id=1, source_target_pairs={{0,16},{4,20},{8,24},{12,28},{16,0},{20,4},{24,8},{28,12},{1,17},{... | collective-permute-start | bytes 4718600 | tf_op jit(solution)/shard_map/ppermute | solution.py:950
  282.7 37.2 %collective-permute-start.13 = (bf16[768,1024]{1,0:T(8,128)(2,1)}, bf16[768,1024]{1,0:T(8,128)(2,1)}, u32[]{:S(2)}, u32[]{:S(2)}) collective-permute-start(bf16[768,1024]{1,0:T(8,128)(2,1)} %constant_dynamic-slice_fusion.2), channel_id=1, source_target_pairs={{0,8},{4,12},{8,0},{12,4},{16,24},{20,28},{24,16},{28,20},{1,9},{5... | collective-permute-start | bytes 4718600 | tf_op jit(solution)/shard_map/ppermute | solution.py:950
  286.2 32.4 %collective-permute-start.10 = (bf16[512,1152]{1,0:T(8,128)(2,1)}, bf16[512,1152]{1,0:T(8,128)(2,1)}, u32[]{:S(2)}, u32[]{:S(2)}) collective-permute-start(bf16[512,1152]{1,0:T(8,128)(2,1)} %pad_maximum_fusion.4), channel_id=1, source_target_pairs={{0,3},{1,0},{2,1},{3,2},{4,7},{5,4},{6,5},{7,6},{8,11},{9,8},{10,9... | collective-permute-start | bytes 3538952 | tf_op jit(solution)/shard_map/ppermute | solution.py:903
  325.2 37.5 %collective-permute-start.16 = (bf16[384,1024]{1,0:T(8,128)(2,1)}, bf16[384,1024]{1,0:T(8,128)(2,1)}, u32[]{:S(2)}, u32[]{:S(2)}) collective-permute-start(bf16[384,1024]{1,0:T(8,128)(2,1)} %constant_dynamic-slice_fusion.1), channel_id=1, source_target_pairs={{0,16},{4,20},{8,24},{12,28},{16,0},{20,4},{24,8},{28,12},{1,17},{... | collective-permute-start | bytes 2359304 | tf_op jit(solution)/shard_map/ppermute | solution.py:950
  327.7 35.1 %collective-permute-start.17 = (bf16[384,1024]{1,0:T(8,128)(2,1)}, bf16[384,1024]{1,0:T(8,128)(2,1)}, u32[]{:S(2)}, u32[]{:S(2)}) collective-permute-start(bf16[384,1024]{1,0:T(8,128)(2,1)} %constant_dynamic-slice_fusion), channel_id=1, source_target_pairs={{0,8},{4,12},{8,0},{12,4},{16,24},{20,28},{24,16},{28,20},{1,9},{5... | collective-permute-start | bytes 2359304 | tf_op jit(solution)/shard_map/ppermute | solution.py:950
  329.3 33.4 %collective-permute-start.18 = (bf16[256,1024]{1,0:T(8,128)(2,1)}, bf16[256,1024]{1,0:T(8,128)(2,1)}, u32[]{:S(2)}, u32[]{:S(2)}) collective-permute-start(bf16[256,1024]{1,0:T(8,128)(2,1)} %get-tuple-element.322), channel_id=1, source_target_pairs={{0,3},{1,0},{2,1},{3,2},{4,7},{5,4},{6,5},{7,6},{8,11},{9,8},{10,9... | collective-permute-start | bytes 1572872 | tf_op jit(solution)/shard_map/ppermute | solution.py:903
  331.2 31.6 %collective-permute-start.19 = (bf16[256,1024]{1,0:T(8,128)(2,1)}, bf16[256,1024]{1,0:T(8,128)(2,1)}, u32[]{:S(2)}, u32[]{:S(2)}) collective-permute-start(bf16[256,1024]{1,0:T(8,128)(2,1)} %get-tuple-element.321), channel_id=1, source_target_pairs={{0,1},{1,2},{2,3},{3,0},{4,5},{5,6},{6,7},{7,4},{8,9},{9,10},{10,1... | collective-permute-start | bytes 1572872 | tf_op jit(solution)/shard_map/ppermute | solution.py:903
  366.7 25.8 %collective-permute-start.20 = (bf16[384,1024]{1,0:T(8,128)(2,1)S(1)}, bf16[384,1024]{1,0:T(8,128)(2,1)}, u32[]{:S(2)}, u32[]{:S(2)}) collective-permute-start(bf16[384,1024]{1,0:T(8,128)(2,1)S(1)} %add_convert_fusion.6), channel_id=1, source_target_pairs={{0,16},{4,20},{8,24},{12,28},{16,0},{20,4},{24,8},{28,12},{1,17},{... | collective-permute-start | bytes 2359304 | tf_op jit(solution)/shard_map/ppermute | solution.py:950
  368.5 24.0 %collective-permute-start.21 = (bf16[384,1024]{1,0:T(8,128)(2,1)}, bf16[384,1024]{1,0:T(8,128)(2,1)}, u32[]{:S(2)}, u32[]{:S(2)}) collective-permute-start(bf16[384,1024]{1,0:T(8,128)(2,1)} %add_convert_fusion.5), channel_id=1, source_target_pairs={{0,8},{4,12},{8,0},{12,4},{16,24},{20,28},{24,16},{28,20},{1,9},{5... | collective-permute-start | bytes 2359304 | tf_op jit(solution)/shard_map/ppermute | solution.py:950
  370.1 116.5 %collective-permute-start.23 = (bf16[512,1024]{1,0:T(8,128)(2,1)S(1)}, bf16[512,1024]{1,0:T(8,128)(2,1)}, u32[]{:S(2)}, u32[]{:S(2)}) collective-permute-start(bf16[512,1024]{1,0:T(8,128)(2,1)S(1)} %pad_maximum_fusion.8), channel_id=1, source_target_pairs={{0,1},{1,2},{2,3},{3,0},{4,5},{5,6},{6,7},{7,4},{8,9},{9,10},{10,1... | collective-permute-start | bytes 3145736 | tf_op jit(solution)/shard_map/ppermute | solution.py:903
  371.7 114.9 %collective-permute-start.22 = (bf16[512,1024]{1,0:T(8,128)(2,1)S(1)}, bf16[512,1024]{1,0:T(8,128)(2,1)}, u32[]{:S(2)}, u32[]{:S(2)}) collective-permute-start(bf16[512,1024]{1,0:T(8,128)(2,1)S(1)} %pad_maximum_fusion.7), channel_id=1, source_target_pairs={{0,3},{1,0},{2,1},{3,2},{4,7},{5,4},{6,5},{7,6},{8,11},{9,8},{10,9... | collective-permute-start | bytes 3145736 | tf_op jit(solution)/shard_map/ppermute | solution.py:903
  486.6 19.4 %collective-permute-start.24 = (bf16[1536,1024]{1,0:T(8,128)(2,1)}, bf16[1536,1024]{1,0:T(8,128)(2,1)S(1)}, u32[]{:S(2)}, u32[]{:S(2)}) collective-permute-start(bf16[1536,1024]{1,0:T(8,128)(2,1)} %bitcast.28), channel_id=1, source_target_pairs={{0,4},{4,0},{8,12},{12,8},{16,20},{20,16},{24,28},{28,24},{1,5},{5... | collective-permute-start | bytes 9437192 | tf_op jit(solution)/shard_map/ppermute | solution.py:950
  487.1 19.0 %collective-permute-start.25 = (bf16[1536,1024]{1,0:T(8,128)(2,1)}, bf16[1536,1024]{1,0:T(8,128)(2,1)}, u32[]{:S(2)}, u32[]{:S(2)}) collective-permute-start(bf16[1536,1024]{1,0:T(8,128)(2,1)} %bitcast.25), channel_id=1, source_target_pairs={{0,4},{4,0},{8,12},{12,8},{16,20},{20,16},{24,28},{28,24},{1,5},{5... | collective-permute-start | bytes 9437192 | tf_op jit(solution)/shard_map/ppermute | solution.py:950
  (25 other events, 294.3 us)
